TPU v7x, 256 devices: a whole 4x4x8 slice. The times are simulated.
256 devices in a mesh: sfc: 256 (over z, y, x, core).
Axes of the slice: x: 4, y: 4, z: 8, core: 2. Of those that a mesh axis runs over, the one named last changes fastest.
Arguments:
- b_tiles: bfloat16 [12288, 2, 128, 128], P('sfc'), may hold values from -0.5 to 0.5
- pressure_tile: int32 [12288, 2], P('sfc'), may hold values from 0 to 1535, as said below
- mobility: float32 [12288, 128], P('sfc'), may hold values from 0.1 to 10
- rhs: float32 [1536, 128], P('sfc'), may hold values from -6 to 6
Outputs:
- pressure: float32 [1536, 128], P('sfc')
Inputs may be any that keep to these rules, and one draw needn't show every extreme that they name: `pressure_tile`: a velocity tile on the device with index d couples only with pressure tiles of device d or d + 1 (pressure tile t belongs to device t // 6); the 2 tiles of one velocity tile are distinct; local velocity tile j couples with local pressure tile j mod 6; the last device couples only with its own.
All inputs are finite; a program needn't handle non-finite values.
Results may differ from a plain program's by a relative error of at most 0.0012.
Values may be sent and summed in bfloat16 or wider, within the bound.
No kernel may reach another device: no remote copies, remote signals or barrier semaphores. Data moves between devices by JAX's collectives and lax.ppermute only.
A program may use at most 128 MiB of HBM per device.

v0:
```python
import jax
import jax.numpy as jnp
from jax import lax
from jax.sharding import PartitionSpec as P

relax = 0.5


def from_behind(block, axis, distance):
    devices = range(lax.axis_size(axis))
    route = [(i - distance, i) for i in devices if i - distance in devices]
    return lax.ppermute(block, axis, route)


def gram(left, right):
    return lax.dot_general(
        left, right, (((1,), (1,)), ((), ())), preferred_element_type=jnp.float32
    )


def halves(tiles, relative, weights, width):
    onehot = (relative[:, :, None] == jnp.arange(width, dtype=jnp.int32)[None, None, :]).astype(
        jnp.bfloat16
    )
    placed = jnp.einsum("vkab,vkr->ravb", tiles, onehot, preferred_element_type=jnp.float32)
    placed = placed.reshape(width * tiles.shape[2], tiles.shape[0] * tiles.shape[3])
    root = jnp.sqrt(weights).reshape(-1)
    return (placed * root[None, :]).astype(jnp.bfloat16)


def slot_grid(tiles, relative, weights, width):
    hp = lax.Precision.HIGHEST
    root = jnp.sqrt(weights)
    weighted = (tiles.astype(jnp.float32) * root[:, None, None, :]).astype(jnp.bfloat16)
    prods = jnp.einsum("vkab,vlcb->vklac", weighted, weighted, preferred_element_type=jnp.float32)
    onehot = (relative[:, :, None] == jnp.arange(width, dtype=jnp.int32)[None, None, :]).astype(
        jnp.float32
    )
    pairs = onehot[:, :, None, :, None] * onehot[:, None, :, None, :]
    grid = jnp.einsum("vklrs,vklac->rasc", pairs, prods, precision=hp)
    size = tiles.shape[2]
    return grid.reshape(width * size, width * size)


def shards(b_tiles, pressure_tile, mobility, rhs):
    tiles_here = rhs.shape[0]
    tile_size = rhs.shape[1]
    rows = tiles_here * tile_size
    hp = lax.Precision.HIGHEST
    position = lax.axis_index("sfc")
    relative = pressure_tile - position * tiles_here
    grid = slot_grid(b_tiles, relative, mobility, 2 * tiles_here)
    centre = grid[:rows, :rows]
    upper = grid[:rows, rows:]
    next_rows = halves(b_tiles, relative - tiles_here, mobility, tiles_here)
    received = from_behind(next_rows, "sfc", 1)
    centre = centre + gram(received, received)
    diagonal = jnp.diagonal(centre)
    target = rhs.reshape(rows)
    values = relax * target / diagonal
    for sweep in range(2):
        following = from_behind(values, "sfc", -1)
        carried = from_behind(jnp.dot(values, upper, precision=hp), "sfc", 1)
        result = jnp.dot(centre, values, precision=hp)
        result = result + jnp.dot(upper, following, precision=hp)
        values = values + relax * (target - (result + carried)) / diagonal
    return values.reshape(tiles_here, tile_size)


def solution(mesh):
    placed = (P("sfc", None, None, None), P("sfc", None), P("sfc", None), P("sfc", None))
    return jax.shard_map(
        shards, mesh=mesh, in_specs=placed, out_specs=P("sfc", None), check_vma=False
    )
```

profile of v0, /device:TPU:128, one launch (start us, length us, event | category | flops | bytes accessed | tf_op | source)
XLA Modules:
  0.0 210.9 jit_solution(11250947867360779547)
XLA Ops:
  0.0 0.7 sqrt_bitcast_fusion
  0.8 0.7 broadcast_add_fusion
  1.4 0.1 copy.10
  1.5 7.2 %convolution_bitcast_fusion = f32[6,128,48,128]{3,0,1,2:T(8,128)S(1)} fusion(bf16[48,2,128,128]{3,2,1,0:T(8,128)(2,1)} %param.4, s32[48,2]{1,0:T(8,128)S(1)} %copy.10), kind=kOutput, calls=%fused_computation.6 | convolution fusion | flops 18874944 | bytes 22020480 | tf_op jit(solution)/shard_map/vkab,vkr->ravb/dot_general | solution.py:25
  8.7 18.7 %copy.12 = f32[6,128,48,128]{3,2,1,0:T(8,128)} copy(f32[6,128,48,128]{3,0,1,2:T(8,128)S(1)} %convolution_bitcast_fusion) | data formatting | bytes 37748736 | tf_op jit(solution)/shard_map/vkab,vkr->ravb/transpose | solution.py:25
  27.4 0.0 copy-start.2
  27.4 14.9 %fusion = bf16[768,6144]{1,0:T(8,128)(2,1)} fusion(f32[96,8,48,128]{3,2,1,0:T(8,128)} %bitcast.81, f32[6144]{0:T(1024)S(1)} %get-tuple-element.7), kind=kLoop, calls=%fused_computation.2 | loop fusion | flops 9437184 | bytes 28336128 | tf_op jit(solution)/shard_map/convert_element_type | solution.py:28
  42.3 2.1 collective-permute-start
  44.5 0.0 copy-done.2
  44.5 6.3 %fusion.6 = f32[48,2,128,2,128]{4,2,3,1,0:T(8,128)} fusion(bf16[48,2,128,128]{3,2,1,0:T(8,128)(2,1)S(1)} %copy-done.2, f32[48,128]{1,0:T(8,128)S(1)} %get-tuple-element.8), kind=kOutput, calls=%fused_computation.9 | convolution fusion | flops 814743552 | bytes 15753216 | tf_op jit(solution)/shard_map/vkab,vlcb->vklac/dot_general | solution.py:35
  50.8 12.7 %copy.15 = f32[48,2,128,2,128]{2,0,1,3,4:T(8,128)} copy(f32[48,2,128,2,128]{4,2,3,1,0:T(8,128)} %fusion.6) | data formatting | bytes 25165824 | tf_op jit(solution)/shard_map/vkab,vlcb->vklac/dot_general | solution.py:35
  63.5 15.8 %fusion.3 = f32[12,128,12,128]{3,2,0,1:T(8,128)} fusion(f32[48,2,128,2,128]{2,0,1,3,4:T(8,128)} %copy.15, f32[48,2,12]{0,2,1:T(8,128)S(1)} %fusion.39, f32[48,2,12]{0,1,2:T(2,128)S(1)} %copy.8), kind=kOutput, calls=%fused_computation.8 | convolution fusion | flops 5435845632 | bytes 22029312 | tf_op jit(solution)/shard_map/vklrs,vklac->rasc/dot_general | solution.py:40
  79.3 10.4 %copy.9 = f32[12,128,12,128]{3,2,1,0:T(8,128)} copy(f32[12,128,12,128]{3,2,0,1:T(8,128)} %fusion.3) | data formatting | bytes 18874368 | tf_op jit(solution)/shard_map/vklrs,vklac->rasc/transpose | solution.py:40
  89.7 9.3 %copy.25 = f32[192,8,12,128]{3,1,2,0:T(8,128)S(1)} copy(f32[192,8,12,128]{3,2,1,0:T(8,128)} %bitcast.82) | data formatting | bytes 18874368
  99.0 0.0 copy-start
  99.0 55.0 %collective-permute-done = bf16[768,6144]{1,0:T(8,128)(2,1)} collective-permute-done((bf16[768,6144]{1,0:T(8,128)(2,1)}, bf16[768,6144]{1,0:T(8,128)(2,1)}, u32[]{:S(2)}, u32[]{:S(2)}) %collective-permute-start) | collective-permute-done | bytes 9437216 | tf_op jit(solution)/shard_map/ppermute | solution.py:12
  154.1 0.0 copy-done
  154.1 0.0 copy-start.3
  154.1 14.1 %slice_add_fusion = f32[768,768]{1,0:T(8,128)S(1)} fusion(f32[1536,1536]{1,0:T(8,128)S(1)} %bitcast.83, bf16[768,6144]{1,0:T(8,128)(2,1)} %collective-permute-done), kind=kOutput, calls=%fused_computation.14 | convolution fusion | flops 7248347136 | bytes 23592960 | tf_op jit(solution)/shard_map/dot_general | solution.py:16
  168.2 6.3 %gather_fusion = f32[768]{0:T(1024)S(1)} fusion(f32[768,768]{1,0:T(8,128)S(1)} %slice_add_fusion, s32[768]{0:T(1024)S(1)} %or_reduce_fusion), kind=kCustom, calls=%fused_computation | custom fusion | bytes 12288 | tf_op jit(solution)/shard_map/jit(diagonal)/cond/branch_0_fun/gather | solution.py:58
  174.5 0.0 copy-done.3
  174.5 0.0 copy-start.1
  174.6 2.3 %collective-permute-start.1 = (f32[768]{0:T(1024)S(1)}, f32[768]{0:T(1024)S(1)}, u32[]{:S(2)}, u32[]{:S(2)}) collective-permute-start(f32[768]{0:T(1024)S(1)} %fusion.40), channel_id=1, source_target_pairs={{1,0},{2,1},{3,2},{4,3},{5,4},{6,5},{7,6},{8,7},{9,8},{10,9},{11,1... | collective-permute-start | bytes 9224 | tf_op jit(solution)/shard_map/ppermute | solution.py:12
  176.9 2.1 convolution_reduce_fusion.1
  179.0 2.9 %fusion.22 = f32[768]{0:T(1024)S(1)} fusion(f32[768,1]{0,1:T(1,128)S(1)} %reshape.39, f32[1536,1536]{1,0:T(8,128)} %bitcast.84), kind=kOutput, calls=%fused_computation.24 | convolution fusion | flops 7077888 | bytes 2365440 | tf_op jit(solution)/shard_map/dot_general | solution.py:63
  181.9 2.3 %collective-permute-start.2 = (f32[768]{0:T(1024)S(1)}, f32[768]{0:T(1024)S(1)}, u32[]{:S(2)}, u32[]{:S(2)}) collective-permute-start(f32[768]{0:T(1024)S(1)} %fusion.22), channel_id=1, source_target_pairs={{0,1},{1,2},{2,3},{3,4},{4,5},{5,6},{6,7},{7,8},{8,9},{9,10},{10,1... | collective-permute-start | bytes 9224 | tf_op jit(solution)/shard_map/ppermute | solution.py:12
  184.1 0.0 collective-permute-done.1
  184.2 3.7 %fusion.19 = f32[768]{0:T(1024)S(1)} fusion(f32[768,1]{0,1:T(1,128)S(1)} %reshape.41, f32[1536,1536]{1,0:T(8,128)} %bitcast.85), kind=kOutput, calls=%fused_computation.23 | convolution fusion | flops 7077888 | bytes 2365440 | tf_op jit(solution)/shard_map/dot_general | solution.py:65
  187.9 4.3 %collective-permute-done.2 = f32[768]{0:T(1024)S(1)} collective-permute-done((f32[768]{0:T(1024)S(1)}, f32[768]{0:T(1024)S(1)}, u32[]{:S(2)}, u32[]{:S(2)}) %collective-permute-start.2) | collective-permute-done | bytes 3104 | tf_op jit(solution)/shard_map/ppermute | solution.py:12
  192.2 4.4 %collective-permute-start.3 = (f32[768]{0:T(1024)S(1)}, f32[768]{0:T(1024)S(1)}, u32[]{:S(2)}, u32[]{:S(2)}) collective-permute-start(f32[768]{0:T(1024)S(1)} %fusion.43), channel_id=1, source_target_pairs={{1,0},{2,1},{3,2},{4,3},{5,4},{6,5},{7,6},{8,7},{9,8},{10,9},{11,1... | collective-permute-start | bytes 9224 | tf_op jit(solution)/shard_map/ppermute | solution.py:12
  196.6 2.1 convolution_reduce_fusion
  198.7 0.0 copy-done.1
  198.7 1.2 fusion.28
  200.0 1.9 collective-permute-start.4
  201.9 0.0 collective-permute-done.3
  201.9 2.1 fusion.25
  204.0 6.3 %collective-permute-done.4 = f32[768]{0:T(1024)S(1)} collective-permute-done((f32[768]{0:T(1024)S(1)}, f32[768]{0:T(1024)S(1)}, u32[]{:S(2)}, u32[]{:S(2)}) %collective-permute-start.4) | collective-permute-done | bytes 3104 | tf_op jit(solution)/shard_map/ppermute | solution.py:12
  210.3 0.6 fusion.47
  (9 shorter events, 0.1 us)
Async XLA Ops:
  27.4 17.1 %copy-start.2 = (bf16[48,2,128,128]{3,2,1,0:T(8,128)(2,1)S(1)}, bf16[48,2,128,128]{3,2,1,0:T(8,128)(2,1)}, u32[]{:S(2)}) copy-start(bf16[48,2,128,128]{3,2,1,0:T(8,128)(2,1)} %param.4) | copy-start | bytes 9437188
  42.3 111.7 %collective-permute-start = (bf16[768,6144]{1,0:T(8,128)(2,1)}, bf16[768,6144]{1,0:T(8,128)(2,1)}, u32[]{:S(2)}, u32[]{:S(2)}) collective-permute-start(bf16[768,6144]{1,0:T(8,128)(2,1)} %fusion), channel_id=1, source_target_pairs={{0,1},{1,2},{2,3},{3,4},{4,5},{5,6},{6,7},{7,8},{8,9},{9,10},{10,1... | collective-permute-start | bytes 28311560 | tf_op jit(solution)/shard_map/ppermute | solution.py:12
  99.0 55.1 %copy-start = (f32[192,8,12,128]{3,1,2,0:T(8,128)}, f32[192,8,12,128]{3,1,2,0:T(8,128)S(1)}, u32[]{:S(2)}) copy-start(f32[192,8,12,128]{3,1,2,0:T(8,128)S(1)} %copy.25) | copy-start | bytes 28311556
  154.1 20.5 %copy-start.3 = (f32[6,128]{1,0:T(8,128)S(1)}, f32[6,128]{1,0:T(8,128)}, u32[]{:S(2)}) copy-start(f32[6,128]{1,0:T(8,128)} %param.7) | copy-start | bytes 9220
  174.5 24.2 %copy-start.1 = (f32[192,8,12,128]{3,1,2,0:T(8,128)S(1)}, f32[192,8,12,128]{3,1,2,0:T(8,128)}, u32[]{:S(2)}) copy-start(f32[192,8,12,128]{3,1,2,0:T(8,128)} %copy-done) | copy-start | bytes 28311556
  174.6 9.6 %collective-permute-start.1 = (f32[768]{0:T(1024)S(1)}, f32[768]{0:T(1024)S(1)}, u32[]{:S(2)}, u32[]{:S(2)}) collective-permute-start(f32[768]{0:T(1024)S(1)} %fusion.40), channel_id=1, source_target_pairs={{1,0},{2,1},{3,2},{4,3},{5,4},{6,5},{7,6},{8,7},{9,8},{10,9},{11,1... | collective-permute-start | bytes 9224 | tf_op jit(solution)/shard_map/ppermute | solution.py:12
  181.9 10.4 %collective-permute-start.2 = (f32[768]{0:T(1024)S(1)}, f32[768]{0:T(1024)S(1)}, u32[]{:S(2)}, u32[]{:S(2)}) collective-permute-start(f32[768]{0:T(1024)S(1)} %fusion.22), channel_id=1, source_target_pairs={{0,1},{1,2},{2,3},{3,4},{4,5},{5,6},{6,7},{7,8},{8,9},{9,10},{10,1... | collective-permute-start | bytes 9224 | tf_op jit(solution)/shard_map/ppermute | solution.py:12
  192.2 9.7 %collective-permute-start.3 = (f32[768]{0:T(1024)S(1)}, f32[768]{0:T(1024)S(1)}, u32[]{:S(2)}, u32[]{:S(2)}) collective-permute-start(f32[768]{0:T(1024)S(1)} %fusion.43), channel_id=1, source_target_pairs={{1,0},{2,1},{3,2},{4,3},{5,4},{6,5},{7,6},{8,7},{9,8},{10,9},{11,1... | collective-permute-start | bytes 9224 | tf_op jit(solution)/shard_map/ppermute | solution.py:12
  200.0 10.4 %collective-permute-start.4 = (f32[768]{0:T(1024)S(1)}, f32[768]{0:T(1024)S(1)}, u32[]{:S(2)}, u32[]{:S(2)}) collective-permute-start(f32[768]{0:T(1024)S(1)} %fusion.28), channel_id=1, source_target_pairs={{0,1},{1,2},{2,3},{3,4},{4,5},{5,6},{6,7},{7,8},{8,9},{9,10},{10,1... | collective-permute-start | bytes 9224 | tf_op jit(solution)/shard_map/ppermute | solution.py:12
where the time goes:
time: 212 us; the launch traced here: 211 us
  waiting for transfers between devices  65.7 us (31%)
  local copies, waits for them, and re-layouts  58.3 us (28%)
  matrix products  57.4 us (27%)
  other arithmetic  16.3 us (8%)
  starting transfers between devices  13 us (6%)
    ppermute x5, waiting for transfers between devices, from_behind(): return lax.ppermute(block, axis, route)  65.7 us
    transpose x1, local copies, waits for them, and re-layouts, halves(): jnp.einsum('vkab,vkr->ravb', tiles, onehot, preferred_element_type=jnp.fl...  18.7 us
    dot_general x1, matrix products, slot_grid(): grid = jnp.einsum('vklrs,vklac->rasc', pairs, prods, precision=hp)  15.8 us
    convert_element_type x1, other arithmetic, halves(): return (placed * root[None, :]).astype(jnp.bfloat16)  14.9 us
    dot_general x1, matrix products, gram(): lax.dot_general(left, right, (((1,), (1,)), ((), ())), preferred_element_...  14.1 us
    ppermute x5, starting transfers between devices, from_behind(): return lax.ppermute(block, axis, route)  13 us
    dot_general x1, local copies, waits for them, and re-layouts, slot_grid(): jnp.einsum('vkab,vlcb->vklac', weighted, weighted, preferred_element_type...  12.7 us
    transpose x1, local copies, waits for them, and re-layouts, slot_grid(): grid = jnp.einsum('vklrs,vklac->rasc', pairs, prods, precision=hp)  10.4 us
  transfers between devices with their start and end apart: 5, of which 3 were waited for; matrix products, arithmetic and copies ran while one was open for 33% of the time, Pallas kernels for 0%

commit v1 on v0

v1 whole, which is shorter than its diff:
```python
import jax
import jax.numpy as jnp
from jax import lax
from jax.experimental import pallas as pl
from jax.experimental.pallas import tpu as pltpu
from jax.sharding import PartitionSpec as P

relax = 0.5
f32, bf16 = jnp.float32, jnp.bfloat16
UP = 8
CHUNKS = 6
VMEM = pl.BlockSpec(memory_space=pltpu.VMEM)
SMEM = pl.BlockSpec(memory_space=pltpu.SMEM)
ANY = pl.BlockSpec(memory_space=pl.ANY)
params = pltpu.CompilerParams(vmem_limit_bytes=32 * 1024 * 1024)


def table_row(tile, here):
    slot = tile - lax.axis_index("sfc") * here
    return jnp.where(slot >= here, slot - here + UP, slot)


def assemble(tiles, couples, mobility, rhs, weighted, own, up, sems):
    count, here = tiles.shape[0], rhs.shape[0]
    step = count // CHUNKS
    copies = []
    for c in range(CHUNKS):
        part = pl.ds(c * step, step)
        copies.append(pltpu.make_async_copy(tiles.at[part], weighted.at[part], sems.at[c]))
        copies[-1].start()
    sub = lax.broadcasted_iota(jnp.int32, (8, 128), 0)
    lane = lax.broadcasted_iota(jnp.int32, (8, 128), 1)
    rows = lax.broadcasted_iota(jnp.int32, (16, 128), 0)
    total = jnp.zeros((16, 128), f32)
    for c in range(CHUNKS):
        copies[c].wait()

        def body(j, total):
            v = c * step + j
            root = jnp.sqrt(mobility[pl.ds(v, 1), :])
            half = (weighted[v].astype(f32) * root).astype(bf16)
            weighted[v] = half
            for k in range(2):
                tile = half[k * 128 : (k + 1) * 128]
                square = lax.dot_general(
                    tile, tile, (((1,), (1,)), ((), ())), preferred_element_type=f32
                )
                picked = square[:8]
                for i in range(1, 16):
                    picked = jnp.where(lane // 8 == i, square[8 * i : 8 * i + 8], picked)
                picked = jnp.where(lane % 8 == sub, picked, 0.0)
                sums = jnp.sum(picked, axis=0, keepdims=True)
                row = table_row(couples[k, v], here)
                total = total + jnp.where(rows == row, sums, 0.0)
            return total

        total = lax.fori_loop(0, step, body, total, unroll=True)
    own[:8, :] = total[:8]
    own[8 : 8 + here, :] = rhs[...]
    up[...] = total[8:]


def multiply(weighted, couples, table, here, mine, following):
    for r in range(here):
        for base, values in ((0, mine), (UP, following)):
            wide = jnp.broadcast_to(values[r : r + 1], (8, 128))
            high = wide.astype(bf16).astype(f32)
            table[base + r] = jnp.concatenate([high, wide - high], axis=0).astype(bf16)
    rows = lax.broadcasted_iota(jnp.int32, (16, 128), 0)

    def body(v, total):
        half = weighted[v]
        first = table_row(couples[0, v], here)
        second = table_row(couples[1, v], here)
        left = jnp.concatenate([table[first], table[second]], axis=1)
        inner = jnp.dot(left, half, preferred_element_type=f32)
        inner = inner[:8] + inner[8:]
        high = inner.astype(bf16).astype(f32)
        left = jnp.concatenate([high, inner - high], axis=0).astype(bf16)
        outer = lax.dot_general(
            left, half, (((1,), (1,)), ((), ())), preferred_element_type=f32
        )
        outer = outer[:8] + outer[8:]
        for k, row in ((0, first), (1, second)):
            part = outer[:, k * 128 : (k + 1) * 128]
            total = total + jnp.where(rows == row, jnp.concatenate([part, part], axis=0), 0.0)
        return total

    return lax.fori_loop(0, weighted.shape[0], body, jnp.zeros((16, 128), f32), unroll=16)


def starts(here, own, up, from_prev, from_next):
    live = lax.broadcasted_iota(jnp.int32, (8, 128), 0) < here
    last = lax.axis_index("sfc") == lax.axis_size("sfc") - 1
    other = live & jnp.logical_not(last)
    diag = jnp.where(live, own[:8, :] + from_prev[...], 1.0)
    diag_next = jnp.where(other, from_next[:8, :] + up[...], 1.0)
    target = jnp.where(live, own[8:, :], 0.0)
    target_next = jnp.where(other, from_next[8:, :], 0.0)
    scale, scale_next = relax / diag, relax / diag_next
    return (scale, target, scale * target), (scale_next, target_next, scale_next * target_next)


def first_sweep(here, weighted, couples, own, up, from_prev, from_next, y_own, y_up, table):
    mine, following = starts(here, own, up, from_prev, from_next)
    total = multiply(weighted, couples, table, here, mine[2], following[2])
    y_own[...] = total[:8]
    y_up[...] = total[8:]


def second_sweep(here, weighted, couples, own, up, from_prev, from_next, y_own, y_up,
                 y_prev, y_next, z_up, rest, factor, table):
    (scale, target, p), (scale_next, target_next, p_next) = starts(here, own, up, from_prev, from_next)
    p = p + scale * (target - (y_own[...] + y_prev[...]))
    last = lax.axis_index("sfc") == lax.axis_size("sfc") - 1
    p_next = p_next + scale_next * (target_next - (y_next[...] + y_up[...]))
    p_next = jnp.where(last, 0.0, p_next)
    total = multiply(weighted, couples, table, here, p, p_next)
    z_up[...] = total[8:]
    rest[...] = p + scale * (target - total[:8])
    factor[...] = scale


def shift(block, distance):
    n = lax.axis_size("sfc")
    route = [(i, i + distance) for i in range(n) if 0 <= i + distance < n]
    return lax.ppermute(block, "sfc", route)


def shards(b_tiles, pressure_tile, mobility, rhs):
    count, pairs, size = b_tiles.shape[:3]
    here = rhs.shape[0]
    tiles = pltpu.with_memory_space_constraint(
        b_tiles.reshape(count, pairs * size, size), pltpu.HBM
    )
    couples = pressure_tile.T
    small = jax.ShapeDtypeStruct((8, size), f32)
    weighted, own, up = pl.pallas_call(
        assemble,
        out_shape=(pltpu.VMEM(tiles.shape, bf16), jax.ShapeDtypeStruct((16, size), f32), small),
        in_specs=[ANY, SMEM, VMEM, VMEM],
        out_specs=(VMEM, VMEM, VMEM),
        scratch_shapes=[pltpu.SemaphoreType.DMA((CHUNKS,))],
        compiler_params=params,
        name="assemble",
    )(tiles, couples, mobility, rhs)
    table = pltpu.VMEM((16, 16, size), bf16)
    from_prev, from_next = shift(up, 1), shift(own, -1)
    weighted = pltpu.with_memory_space_constraint(weighted, pltpu.VMEM)
    known = (weighted, couples, own, up, from_prev, from_next)
    y_own, y_up = pl.pallas_call(
        lambda *refs: first_sweep(here, *refs),
        out_shape=(small, small),
        in_specs=[VMEM, SMEM] + [VMEM] * 4,
        out_specs=(VMEM, VMEM),
        scratch_shapes=[table],
        compiler_params=params,
        name="first_sweep",
    )(*known)
    y_prev, y_next = shift(y_up, 1), shift(y_own, -1)
    z_up, rest, factor = pl.pallas_call(
        lambda *refs: second_sweep(here, *refs),
        out_shape=(small, small, small),
        in_specs=[VMEM, SMEM] + [VMEM] * 8,
        out_specs=(VMEM, VMEM, VMEM),
        scratch_shapes=[table],
        compiler_params=params,
        name="second_sweep",
    )(*known, y_own, y_up, y_prev, y_next)
    z_prev = shift(z_up, 1)
    return (rest - factor * z_prev)[:here]


def solution(mesh):
    placed = (P("sfc", None, None, None), P("sfc", None), P("sfc", None), P("sfc", None))
    return jax.shard_map(
        shards, mesh=mesh, in_specs=placed, out_specs=P("sfc", None), check_vma=False
    )
```

time: 212 us -> 55.3 us (0.26)
  matrix products: 57.4 us -> 0 us
  local copies, waits for them, and re-layouts: 58.3 us -> 2.1 us
  waiting for transfers between devices: 65.7 us -> 24.8 us
  other arithmetic: 16.3 us -> 0.6 us
  Pallas kernels: 0 us -> 13.2 us
    dot_general x10 -> x0, matrix products: 57.4 us -> none  [the longest x1 15.8 us: slot_grid(): grid = jnp.einsum('vklrs,vklac->rasc', pairs, prods, precision=hp)]
    ppermute x5, waiting for transfers between devices: 65.7 us -> 24.8 us  [shift(): return lax.ppermute(block, 'sfc', route)]
    transpose x2 -> x0, local copies, waits for them, and re-layouts: 29.1 us -> none  [the longest x1 18.7 us: halves(): jnp.einsum('vkab,vkr->ravb', tiles, onehot, preferred_element_type=jnp.fl...]
    convert_element_type x2 -> x0, other arithmetic: 14.9 us -> none  [the longest x1 14.9 us: halves(): return (placed * root[None, :]).astype(jnp.bfloat16)]
    pallas_call x0 -> x3, Pallas kernels: none -> 13.2 us  [the longest x1 4.67 us: shards(): pl.pallas_call(assemble, out_shape=(pltpu.VMEM(tiles.shape, bf16), jax.Sh...]
    dot_general x1 -> x0, local copies, waits for them, and re-layouts: 12.7 us -> none  [slot_grid(): jnp.einsum('vkab,vlcb->vklac', weighted, weighted, preferred_element_type...]
    unnamed x9 -> x6, local copies, waits for them, and re-layouts: 9.29 us -> 2.1 us
    gather x1 -> x0, local copies, waits for them, and re-layouts: 6.3 us -> none  [shards(): diagonal = jnp.diagonal(centre)]
  transfers between devices with their start and end apart: 5 -> 5, of which waited for: 3 -> 3; matrix products, arithmetic and copies ran while one was open for 33% -> 0% of each run, Pallas kernels for 0% -> 0%
where the time goes in v1:
time: 55.3 us; the launch traced here: 55 us
  waiting for transfers between devices  24.8 us (45%)
  starting transfers between devices  14.3 us (26%)
  Pallas kernels  13.2 us (24%)
  local copies, waits for them, and re-layouts  2.1 us (4%)
  other arithmetic  0.6 us (1%)
    ppermute x5, waiting for transfers between devices, shift(): return lax.ppermute(block, 'sfc', route)  24.8 us
    ppermute x5, starting transfers between devices, shift(): return lax.ppermute(block, 'sfc', route)  14.3 us
    pallas_call x1, Pallas kernels, shards(): pl.pallas_call(assemble, out_shape=(pltpu.VMEM(tiles.shape, bf16), jax.Sh...  4.67 us
    pallas_call x1, Pallas kernels, shards(): pl.pallas_call(lambda *refs: second_sweep(here, *refs), out_shape=(small,...  4.27 us
    pallas_call x1, Pallas kernels, shards(): pl.pallas_call(lambda *refs: first_sweep(here, *refs), out_shape=(small,...  4.26 us
    unnamed x6, local copies, waits for them, and re-layouts  2.1 us
  transfers between devices with their start and end apart: 5, of which 3 were waited for; matrix products, arithmetic and copies ran while one was open for 0% of the time, Pallas kernels for 0%

profile of v1, /device:TPU:128, one launch (start us, length us, event | category | flops | bytes accessed | tf_op | source)
XLA Modules:
  0.0 55.0 jit_solution(17623158579492929688)
XLA Ops:
  0.0 0.0 copy-start
  0.0 0.7 %copy-done = f32[48,128]{1,0:T(8,128)S(1)} copy-done((f32[48,128]{1,0:T(8,128)S(1)}, f32[48,128]{1,0:T(8,128)}, u32[]{:S(2)}) %copy-start) | copy-done | bytes 24600
  0.7 0.0 copy-start.1
  0.7 0.7 %copy-done.1 = s32[48,2]{0,1:T(2,128)S(1)} copy-done((s32[48,2]{0,1:T(2,128)S(1)}, s32[48,2]{0,1:T(2,128)}, u32[]{:S(2)}) %copy-start.1) | copy-done | bytes 408
  1.4 0.0 copy-start.2
  1.4 0.7 %copy-done.2 = f32[6,128]{1,0:T(8,128)S(1)} copy-done((f32[6,128]{1,0:T(8,128)S(1)}, f32[6,128]{1,0:T(8,128)}, u32[]{:S(2)}) %copy-start.2) | copy-done | bytes 3096
  2.1 4.7 %assemble.1 = (bf16[48,256,128]{2,1,0:T(8,128)(2,1)S(1)}, f32[16,128]{1,0:T(8,128)S(1)}, f32[8,128]{1,0:T(8,128)S(1)}) custom-call(bf16[48,256,128]{2,1,0:T(8,128)(2,1)} %bitcast.6, s32[2,48]{1,0:T(2,128)S(1)} %bitcast.3, f32[48,128]{1,0:T(8,128)S(1)} %copy-done, f32[6,128]{1,0:T(8,128)S(1)} %copy-done.2), custom_call_target="tpu_custom_call" | custom-call | tf_op jit(solution)/shard_map/assemble/pallas_call | solution.py:138
  6.8 6.1 %collective-permute-start.1 = (f32[16,128]{1,0:T(8,128)S(1)}, f32[16,128]{1,0:T(8,128)S(1)}, u32[]{:S(2)}, u32[]{:S(2)}) collective-permute-start(f32[16,128]{1,0:T(8,128)S(1)} %get-tuple-element.14.refs_2_), channel_id=1, source_target_pairs={{1,0},{2,1},{3,2},{4,3},{5,4},{6,5},{7,6},{8,7},{9,8},{10,9},{11,1... | collective-permute-start | bytes 24584 | tf_op jit(solution)/shard_map/ppermute | solution.py:127
  12.9 1.9 %collective-permute-start = (f32[8,128]{1,0:T(8,128)S(1)}, f32[8,128]{1,0:T(8,128)S(1)}, u32[]{:S(2)}, u32[]{:S(2)}) collective-permute-start(f32[8,128]{1,0:T(8,128)S(1)} %get-tuple-element.15.refs_3_), channel_id=1, source_target_pairs={{0,1},{1,2},{2,3},{3,4},{4,5},{5,6},{6,7},{7,8},{8,9},{9,10},{10,1... | collective-permute-start | bytes 12296 | tf_op jit(solution)/shard_map/ppermute | solution.py:127
  14.8 8.4 %collective-permute-done.refs_4_ = f32[8,128]{1,0:T(8,128)S(1)} collective-permute-done((f32[8,128]{1,0:T(8,128)S(1)}, f32[8,128]{1,0:T(8,128)S(1)}, u32[]{:S(2)}, u32[]{:S(2)}) %collective-permute-start) | collective-permute-done | bytes 4128 | tf_op jit(solution)/shard_map/ppermute | solution.py:127
  23.3 0.0 collective-permute-done.1.refs_5_
  23.3 4.3 %first_sweep.1 = (f32[8,128]{1,0:T(8,128)S(1)}, f32[8,128]{1,0:T(8,128)S(1)}) custom-call(bf16[48,256,128]{2,1,0:T(8,128)(2,1)S(1)} %get-tuple-element.13.refs_0_, s32[2,48]{1,0:T(2,128)S(1)} %bitcast.4, f32[16,128]{1,0:T(8,128)S(1)} %get-tuple-element.14.refs_2_, f32[8,128]{1,0:T(8,128)S(1)} %get-tuple-element.15.refs_3_, ...), custom_call_target="tpu_custom_call" | custom-call | tf_op jit(solution)/shard_map/first_sweep/pallas_call | solution.py:151
  27.5 1.9 %collective-permute-start.3 = (f32[8,128]{1,0:T(8,128)S(1)}, f32[8,128]{1,0:T(8,128)S(1)}, u32[]{:S(2)}, u32[]{:S(2)}) collective-permute-start(f32[8,128]{1,0:T(8,128)S(1)} %get-tuple-element.16.refs_6_), channel_id=1, source_target_pairs={{1,0},{2,1},{3,2},{4,3},{5,4},{6,5},{7,6},{8,7},{9,8},{10,9},{11,1... | collective-permute-start | bytes 12296 | tf_op jit(solution)/shard_map/ppermute | solution.py:127
  29.4 2.4 %collective-permute-start.2 = (f32[8,128]{1,0:T(8,128)S(1)}, f32[8,128]{1,0:T(8,128)S(1)}, u32[]{:S(2)}, u32[]{:S(2)}) collective-permute-start(f32[8,128]{1,0:T(8,128)S(1)} %get-tuple-element.17.refs_7_), channel_id=1, source_target_pairs={{0,1},{1,2},{2,3},{3,4},{4,5},{5,6},{6,7},{7,8},{8,9},{9,10},{10,1... | collective-permute-start | bytes 12296 | tf_op jit(solution)/shard_map/ppermute | solution.py:127
  31.9 0.0 collective-permute-done.3.refs_9_
  31.9 7.9 %collective-permute-done.2.refs_8_ = f32[8,128]{1,0:T(8,128)S(1)} collective-permute-done((f32[8,128]{1,0:T(8,128)S(1)}, f32[8,128]{1,0:T(8,128)S(1)}, u32[]{:S(2)}, u32[]{:S(2)}) %collective-permute-start.2) | collective-permute-done | bytes 4128 | tf_op jit(solution)/shard_map/ppermute | solution.py:127
  39.8 4.3 %second_sweep.1 = (f32[8,128]{1,0:T(8,128)S(1)}, f32[8,128]{1,0:T(8,128)S(1)}, f32[8,128]{1,0:T(8,128)S(1)}) custom-call(bf16[48,256,128]{2,1,0:T(8,128)(2,1)S(1)} %get-tuple-element.13.refs_0_, s32[2,48]{1,0:T(2,128)S(1)} %bitcast.5, f32[16,128]{1,0:T(8,128)S(1)} %get-tuple-element.14.refs_2_, f32[8,128]{1,0:T(8,128)S(1)} %get-tuple-element.15.refs_3_, ...), custom_call_target="tpu_custom_call" | custom-call | tf_op jit(solution)/shard_map/second_sweep/pallas_call | solution.py:161
  44.1 1.9 %collective-permute-start.4 = (f32[8,128]{1,0:T(8,128)S(1)}, f32[8,128]{1,0:T(8,128)S(1)}, u32[]{:S(2)}, u32[]{:S(2)}) collective-permute-start(f32[8,128]{1,0:T(8,128)S(1)} %get-tuple-element.20), channel_id=1, source_target_pairs={{0,1},{1,2},{2,3},{3,4},{4,5},{5,6},{6,7},{7,8},{8,9},{9,10},{10,1... | collective-permute-start | bytes 12296 | tf_op jit(solution)/shard_map/ppermute | solution.py:127
  46.0 8.4 %collective-permute-done.4 = f32[8,128]{1,0:T(8,128)S(1)} collective-permute-done((f32[8,128]{1,0:T(8,128)S(1)}, f32[8,128]{1,0:T(8,128)S(1)}, u32[]{:S(2)}, u32[]{:S(2)}) %collective-permute-start.4) | collective-permute-done | bytes 4128 | tf_op jit(solution)/shard_map/ppermute | solution.py:127
  54.4 0.6 %multiply_subtract_fusion = f32[8,128]{1,0:T(8,128)} fusion(f32[8,128]{1,0:T(8,128)S(1)} %get-tuple-element.18, f32[8,128]{1,0:T(8,128)S(1)} %get-tuple-element.19, f32[8,128]{1,0:T(8,128)S(1)} %collective-permute-done.4), kind=kLoop, calls=%fused_computation | loop fusion | flops 2048 | bytes 16384 | tf_op jit(solution)/shard_map/sub | solution.py:171
Async XLA Ops:
  0.0 0.7 %copy-start = (f32[48,128]{1,0:T(8,128)S(1)}, f32[48,128]{1,0:T(8,128)}, u32[]{:S(2)}) copy-start(f32[48,128]{1,0:T(8,128)} %mobility.1) | copy-start | bytes 73732
  0.7 0.7 %copy-start.1 = (s32[48,2]{0,1:T(2,128)S(1)}, s32[48,2]{0,1:T(2,128)}, u32[]{:S(2)}) copy-start(s32[48,2]{0,1:T(2,128)} %param.5) | copy-start | bytes 1156
  1.4 0.7 %copy-start.2 = (f32[6,128]{1,0:T(8,128)S(1)}, f32[6,128]{1,0:T(8,128)}, u32[]{:S(2)}) copy-start(f32[6,128]{1,0:T(8,128)} %rhs.1) | copy-start | bytes 9220
  6.8 16.5 %collective-permute-start.1 = (f32[16,128]{1,0:T(8,128)S(1)}, f32[16,128]{1,0:T(8,128)S(1)}, u32[]{:S(2)}, u32[]{:S(2)}) collective-permute-start(f32[16,128]{1,0:T(8,128)S(1)} %get-tuple-element.14.refs_2_), channel_id=1, source_target_pairs={{1,0},{2,1},{3,2},{4,3},{5,4},{6,5},{7,6},{8,7},{9,8},{10,9},{11,1... | collective-permute-start | bytes 24584 | tf_op jit(solution)/shard_map/ppermute | solution.py:127
  12.9 10.4 %collective-permute-start = (f32[8,128]{1,0:T(8,128)S(1)}, f32[8,128]{1,0:T(8,128)S(1)}, u32[]{:S(2)}, u32[]{:S(2)}) collective-permute-start(f32[8,128]{1,0:T(8,128)S(1)} %get-tuple-element.15.refs_3_), channel_id=1, source_target_pairs={{0,1},{1,2},{2,3},{3,4},{4,5},{5,6},{6,7},{7,8},{8,9},{9,10},{10,1... | collective-permute-start | bytes 12296 | tf_op jit(solution)/shard_map/ppermute | solution.py:127
  27.5 4.3 %collective-permute-start.3 = (f32[8,128]{1,0:T(8,128)S(1)}, f32[8,128]{1,0:T(8,128)S(1)}, u32[]{:S(2)}, u32[]{:S(2)}) collective-permute-start(f32[8,128]{1,0:T(8,128)S(1)} %get-tuple-element.16.refs_6_), channel_id=1, source_target_pairs={{1,0},{2,1},{3,2},{4,3},{5,4},{6,5},{7,6},{8,7},{9,8},{10,9},{11,1... | collective-permute-start | bytes 12296 | tf_op jit(solution)/shard_map/ppermute | solution.py:127
  29.4 10.4 %collective-permute-start.2 = (f32[8,128]{1,0:T(8,128)S(1)}, f32[8,128]{1,0:T(8,128)S(1)}, u32[]{:S(2)}, u32[]{:S(2)}) collective-permute-start(f32[8,128]{1,0:T(8,128)S(1)} %get-tuple-element.17.refs_7_), channel_id=1, source_target_pairs={{0,1},{1,2},{2,3},{3,4},{4,5},{5,6},{6,7},{7,8},{8,9},{9,10},{10,1... | collective-permute-start | bytes 12296 | tf_op jit(solution)/shard_map/ppermute | solution.py:127
  44.1 10.4 %collective-permute-start.4 = (f32[8,128]{1,0:T(8,128)S(1)}, f32[8,128]{1,0:T(8,128)S(1)}, u32[]{:S(2)}, u32[]{:S(2)}) collective-permute-start(f32[8,128]{1,0:T(8,128)S(1)} %get-tuple-element.20), channel_id=1, source_target_pairs={{0,1},{1,2},{2,3},{3,4},{4,5},{5,6},{6,7},{7,8},{8,9},{9,10},{10,1... | collective-permute-start | bytes 12296 | tf_op jit(solution)/shard_map/ppermute | solution.py:127

commit v2 on v0

v2 whole, which is shorter than its diff:
```python
import functools

import jax
import jax.numpy as jnp
from jax import lax
from jax.experimental import pallas as pl
from jax.experimental.pallas import tpu as pltpu
from jax.sharding import PartitionSpec as P

relax = 0.5
f32, bf16 = jnp.float32, jnp.bfloat16
UP = 8
CHUNKS = 6
GROUP = 8
ODD, EVEN = 1, 0
cost = pl.CostEstimate(flops=10**10, bytes_accessed=10**8, transcendentals=0)
VMEM = pl.BlockSpec(memory_space=pltpu.VMEM)
ANY = pl.BlockSpec(memory_space=pl.ANY)
params = pltpu.CompilerParams(vmem_limit_bytes=32 * 1024 * 1024)


def position():
    return lax.axis_index("sfc")


def is_last():
    return position() == lax.axis_size("sfc") - 1


def parts(values):
    high = values.astype(bf16).astype(f32)
    return high, values - high


def scatter(place, per_tile):
    total = None
    for k in range(2):
        high, rest = parts(per_tile[k])
        middle, low = parts(rest)
        wide = jnp.concatenate([high, middle, low], axis=1).astype(bf16)
        sums = jnp.dot(
            place[k][:, : wide.shape[0]].astype(bf16), wide, preferred_element_type=f32
        )
        size = sums.shape[1] // 3
        sums = sums[:, :size] + sums[:, size : 2 * size] + sums[:, 2 * size :]
        total = sums if total is None else total + sums
    return total


def assemble_here(tiles, couples, mobility, rhs, weighted, place, pick, own, up, scratch, sems):
    count, here = tiles.shape[0], rhs.shape[0]
    step = count // CHUNKS
    local_couples, local_mobility, local_rhs = scratch
    small = (couples, local_couples), (mobility, local_mobility), (rhs, local_rhs)
    small = [pltpu.make_async_copy(a, b, sems.at[CHUNKS + i]) for i, (a, b) in enumerate(small)]
    for copy in small:
        copy.start()
    copies = []
    for c in range(CHUNKS):
        part = pl.ds(c * step, step)
        copies.append(pltpu.make_async_copy(tiles.at[part], weighted.at[part], sems.at[c]))
        copies[-1].start()
    for copy in small:
        copy.wait()
    slot = local_couples[...] - position() * here
    slot = jnp.where(slot >= here, slot - here + UP, slot)
    rows = lax.broadcasted_iota(jnp.int32, (16, count), 0)
    places = [
        jnp.concatenate(
            [(rows == slot[k : k + 1]).astype(f32), jnp.zeros((16, 128 - count), f32)], axis=1
        )
        for k in range(2)
    ]
    for k in range(2):
        place[k] = places[k]
    pick[...] = jnp.concatenate(places + [jnp.zeros((96, 128), f32)], axis=0).T
    sub = lax.broadcasted_iota(jnp.int32, (8, 128), 0)
    lane = lax.broadcasted_iota(jnp.int32, (8, 128), 1)
    sums = [[], []]
    for c in range(CHUNKS):
        copies[c].wait()
        for g in range(step // GROUP):
            picked_rows = [jnp.zeros((8, 128), f32)] * 2
            for j in range(GROUP):
                v = c * step + g * GROUP + j
                root = jnp.sqrt(local_mobility[v : v + 1, :])
                half = (weighted[v].astype(f32) * root).astype(bf16)
                weighted[v] = half
                for k in range(2):
                    tile = half[k * 128 : (k + 1) * 128]
                    square = lax.dot_general(
                        tile, tile, (((1,), (1,)), ((), ())), preferred_element_type=f32
                    )
                    picked = square[:8]
                    for i in range(1, 16):
                        picked = jnp.where(lane // 8 == i, square[8 * i : 8 * i + 8], picked)
                    picked = jnp.where(lane % 8 == sub, picked, 0.0)
                    picked = jnp.sum(picked, axis=0, keepdims=True)
                    picked_rows[k] = jnp.where(sub == j, picked, picked_rows[k])
            for k in range(2):
                sums[k].append(picked_rows[k])
    total = scatter(places, [jnp.concatenate(s, axis=0) for s in sums])
    own[:8, :] = total[:8]
    own[8:, :] = jnp.concatenate([local_rhs[...], jnp.zeros((8 - here, 128), f32)], axis=0)
    up[...] = total[8:]


def assemble_odd(tiles, couples, mobility, rhs, weighted, place, pick, own, up, *scratch):
    @pl.when(position() % 2 == ODD)
    def _():
        assemble_here(
            tiles, couples, mobility, rhs, weighted, place, pick, own, up, scratch[:3], scratch[3]
        )

    @pl.when(position() % 2 == EVEN)
    def _():
        up[...] = jnp.zeros_like(up)


def assemble_even(tiles, couples, mobility, rhs, odd_own, odd_up,
                  weighted, place, pick, own, up, swapped, *scratch):
    @pl.when(position() % 2 == EVEN)
    def _():
        assemble_here(
            tiles, couples, mobility, rhs, weighted, place, pick, own, up, scratch[:3], scratch[3]
        )
        swapped[:8, :] = up[...]
        swapped[8:, :] = up[...]

    @pl.when(position() % 2 == ODD)
    def _():
        own[...] = jnp.zeros_like(own)
        swapped[...] = odd_own[...]


def pass_on(block, out):
    out[...] = block[...]


def multiply(weighted, place, pick, mine, following):
    count = weighted.shape[0]
    high, low = parts(jnp.concatenate([mine, following], axis=0))
    none = jnp.zeros_like(high)
    table = jnp.concatenate(
        [
            jnp.concatenate([high, none, low, none], axis=1),
            jnp.concatenate([none, high, none, low], axis=1),
        ],
        axis=0,
    ).astype(bf16)
    values = jnp.dot(pick[:count, :32].astype(bf16), table, preferred_element_type=f32)
    sub = lax.broadcasted_iota(jnp.int32, (8, 128), 0)
    sub2 = lax.broadcasted_iota(jnp.int32, (8, 256), 0)
    inner, outer = [], []
    for g in range(count // GROUP):
        block = values[GROUP * g : GROUP * (g + 1)]
        left = jnp.concatenate([block[:, :256], block[:, 256:]], axis=0).astype(bf16)
        total = None
        for j in range(0, GROUP, 2):
            v = GROUP * g + j
            right = jnp.concatenate([weighted[v], weighted[v + 1]], axis=1)
            both = jnp.dot(left, right, preferred_element_type=f32)
            both = both[:8] + both[8:]
            total = both[:, :128] if total is None else jnp.where(sub == j, both[:, :128], total)
            total = jnp.where(sub == j + 1, both[:, 128:], total)
        inner.append(total)
    for g in range(count // GROUP):
        left = jnp.concatenate(parts(inner[g]), axis=0).astype(bf16)
        total = None
        for j in range(GROUP):
            both = lax.dot_general(
                left, weighted[GROUP * g + j], (((1,), (1,)), ((), ())), preferred_element_type=f32
            )
            both = both[:8] + both[8:]
            total = both if total is None else jnp.where(sub2 == j, both, total)
        outer.append(total)
    outer = jnp.concatenate(outer, axis=0)
    total = scatter(place, [outer[:, :128], outer[:, 128:]])
    return total[:8], total[8:]


def starts(here, own, up, from_prev, from_next):
    live = lax.broadcasted_iota(jnp.int32, (8, 128), 0) < here
    other = live & jnp.logical_not(is_last())
    diag = jnp.where(live, own[:8, :] + from_prev[:8, :], 1.0)
    diag_next = jnp.where(other, from_next[:8, :] + up[...], 1.0)
    target = jnp.where(live, own[8:, :], 0.0)
    target_next = jnp.where(other, from_next[8:, :], 0.0)
    scale, scale_next = relax / diag, relax / diag_next
    return (scale, target, scale * target), (scale_next, target_next, scale_next * target_next)


def first_sweep(here, parity, weighted, place, pick, own, up, from_prev, from_next, *outs):
    y_own, y_up = outs[-2:]

    @pl.when(position() % 2 == parity)
    def _():
        mine, following = starts(here, own, up, from_prev, from_next)
        y_own[...], y_up[...] = multiply(weighted, place, pick, mine[2], following[2])

    @pl.when(position() % 2 != parity)
    def _():
        y_own[...] = y_up[...] = jnp.zeros_like(y_up)


def second_sweep(here, parity, weighted, place, pick, own, up, from_prev, from_next,
                 y_own, y_up, y_prev, y_next, *outs):
    z_up, rest, factor = outs[-3:]

    @pl.when(position() % 2 == parity)
    def _():
        mine, following = starts(here, own, up, from_prev, from_next)
        scale, target, p = mine
        scale_next, target_next, p_next = following
        p = p + scale * (target - (y_own[...] + y_prev[...]))
        p_next = p_next + scale_next * (target_next - (y_next[...] + y_up[...]))
        p_next = jnp.where(is_last(), 0.0, p_next)
        z_own, z_up[...] = multiply(weighted, place, pick, p, p_next)
        rest[...] = p + scale * (target - z_own)
        factor[...] = scale

    @pl.when(position() % 2 != parity)
    def _():
        z_up[...] = jnp.zeros_like(z_up)


def finish_even(rest, factor, z_prev, out):
    out[...] = rest[...] - factor[...] * z_prev[...]


def finish(even, rest, factor, z_prev, out):
    odd = rest[...] - factor[...] * z_prev[...]
    out[...] = jnp.where(position() % 2 == ODD, odd, even[...])[: out.shape[0]]


def to_next():
    n = lax.axis_size("sfc")
    plane = max(n // 8, 4)
    stops = [i + 4 for i in range(0, n - 4, plane) if i + 4 < n - 2]
    route = {i: i + 1 for i in range(n)}
    route.update(zip(stops + [n - 1], [0] + [i + 1 for i in stops]))
    return list(route.items())


def forward(block):
    return lax.ppermute(block, "sfc", to_next())


def backward(block):
    return lax.ppermute(block, "sfc", [(b, a) for a, b in to_next()])


def odd_to_next(block):
    n = lax.axis_size("sfc")
    return lax.ppermute(block, "sfc", [(i, i + 1) for i in range(ODD, n - 1, 2)])


def swap(block):
    return lax.ppermute(block, "sfc", [(i, i ^ 1) for i in range(lax.axis_size("sfc"))])


def shards(b_tiles, pressure_tile, mobility, rhs):
    count, pairs, size = b_tiles.shape[:3]
    here = rhs.shape[0]
    in_hbm = lambda a: pltpu.with_memory_space_constraint(a, pltpu.HBM)
    in_vmem = lambda a: pltpu.with_memory_space_constraint(a, pltpu.VMEM)
    tiles = b_tiles.reshape(count, pairs * size, size)
    args = tuple(in_hbm(a) for a in (tiles, pressure_tile.T, mobility, rhs))
    small = jax.ShapeDtypeStruct((8, size), f32)
    assembled = (
        pltpu.VMEM(tiles.shape, bf16),
        jax.ShapeDtypeStruct((2, 16, 128), f32),
        jax.ShapeDtypeStruct((128, 128), f32),
        jax.ShapeDtypeStruct((16, size), f32),
        small,
    )
    scratch = [
        pltpu.VMEM((pairs, count), jnp.int32),
        pltpu.VMEM((count, size), f32),
        pltpu.VMEM((here, size), f32),
        pltpu.SemaphoreType.DMA((CHUNKS + 3,)),
    ]

    def call(kernel, outs, name, *operands, **more):
        return pl.pallas_call(
            kernel,
            out_shape=outs,
            in_specs=[VMEM] * len(operands),
            out_specs=jax.tree.map(lambda _: VMEM, outs),
            compiler_params=params,
            cost_estimate=cost,
            name=name,
            **more,
        )(*operands)

    def assembled_by(kernel, outs, name, *order):
        weighted, *others = pl.pallas_call(
            kernel,
            out_shape=outs,
            in_specs=[ANY] * 4 + [VMEM] * len(order),
            out_specs=(VMEM,) * len(outs),
            scratch_shapes=scratch,
            compiler_params=params,
            cost_estimate=cost,
            name=name,
        )(*args, *order)
        return in_vmem(weighted), *others

    known_o = assembled_by(assemble_odd, assembled, "assemble_odd")
    up_e = odd_to_next(known_o[4])
    *known_e, swapped = assembled_by(
        assemble_even, assembled + assembled[3:4], "assemble_even", *known_o[3:]
    )
    next_own_o = backward(known_e[3])
    swapped = swap(swapped)
    up_e = call(pass_on, small, "pass_on", up_e)
    known_e = (*known_e, up_e, swapped)
    known_o = (*known_o, swapped, next_own_o)
    y_own_e, y_up_e = call(
        functools.partial(first_sweep, here, EVEN), (small, small), "first_even", *known_e
    )
    y_next_o = backward(y_own_e)
    y_prev_o = swap(y_up_e)
    y_own_o, y_up_o = call(
        functools.partial(first_sweep, here, ODD), (small, small), "first_odd", *known_o, y_up_e
    )
    y_prev_e = forward(y_up_o)
    y_next_e = swap(y_own_o)
    z_up_o, rest_o, factor_o = call(
        functools.partial(second_sweep, here, ODD), (small,) * 3, "second_odd",
        *known_o, y_own_o, y_up_o, y_prev_o, y_next_o,
    )
    z_prev_e = forward(z_up_o)
    z_up_e, rest_e, factor_e = call(
        functools.partial(second_sweep, here, EVEN), (small,) * 3, "second_even",
        *known_e, y_own_e, y_up_e, y_prev_e, y_next_e, z_up_o,
    )
    z_prev_o = swap(z_up_e)
    even = call(finish_even, small, "finish_even", rest_e, factor_e, z_prev_e)
    outs = jax.ShapeDtypeStruct(rhs.shape, f32)
    return call(finish, outs, "finish", even, rest_o, factor_o, z_prev_o)


def solution(mesh):
    placed = (P("sfc", None, None, None), P("sfc", None), P("sfc", None), P("sfc", None))
    return jax.shard_map(
        shards, mesh=mesh, in_specs=placed, out_specs=P("sfc", None), check_vma=False
    )
```

time: 212 us -> 26 us (0.12)
  waiting for transfers between devices: 65.7 us -> 6.56 us
  local copies, waits for them, and re-layouts: 58.3 us -> 0 us
  matrix products: 57.4 us -> 0 us
  other arithmetic: 16.3 us -> 0 us
  Pallas kernels: 0 us -> 8.19 us
  starting transfers between devices: 13 us -> 10.7 us
    ppermute x5 -> x9, waiting for transfers between devices: 65.7 us -> 6.56 us  [the longest x2 5.5 us: forward(): return lax.ppermute(block, 'sfc', to_next())]
    dot_general x10 -> x0, matrix products: 57.4 us -> none  [the longest x1 15.8 us: slot_grid(): grid = jnp.einsum('vklrs,vklac->rasc', pairs, prods, precision=hp)]
    transpose x2 -> x0, local copies, waits for them, and re-layouts: 29.1 us -> none  [the longest x1 18.7 us: halves(): jnp.einsum('vkab,vkr->ravb', tiles, onehot, preferred_element_type=jnp.fl...]
    convert_element_type x2 -> x0, other arithmetic: 14.9 us -> none  [the longest x1 14.9 us: halves(): return (placed * root[None, :]).astype(jnp.bfloat16)]
    dot_general x1 -> x0, local copies, waits for them, and re-layouts: 12.7 us -> none  [slot_grid(): jnp.einsum('vkab,vlcb->vklac', weighted, weighted, preferred_element_type...]
    unnamed x9 -> x0, local copies, waits for them, and re-layouts: 9.29 us -> none
    pallas_call x0 -> x9, Pallas kernels: none -> 8.19 us  [the longest x2 4.43 us: assembled_by(): pl.pallas_call(kernel, out_shape=outs, in_specs=[ANY] * 4 + [VMEM] * len(...]
    gather x1 -> x0, local copies, waits for them, and re-layouts: 6.3 us -> none  [shards(): diagonal = jnp.diagonal(centre)]
  transfers between devices with their start and end apart: 5 -> 9, of which waited for: 3 -> 4; matrix products, arithmetic and copies ran while one was open for 33% -> 0% of each run, Pallas kernels for 0% -> 29%
where the time goes in v2:
time: 26 us; the launch traced here: 25.5 us
  starting transfers between devices  10.7 us (41%)
  Pallas kernels  8.19 us (32%)
  waiting for transfers between devices  6.56 us (25%)
    ppermute x2, waiting for transfers between devices, forward(): return lax.ppermute(block, 'sfc', to_next())  5.5 us
    ppermute x2, starting transfers between devices, backward(): return lax.ppermute(block, 'sfc', [(b, a) for a, b in to_next()])  4.9 us
    pallas_call x2, Pallas kernels, assembled_by(): pl.pallas_call(kernel, out_shape=outs, in_specs=[ANY] * 4 + [VMEM] * len(...  4.43 us
    pallas_call x7, Pallas kernels, call(): pl.pallas_call(kernel, out_shape=outs, in_specs=[VMEM] * len(operands), o...  3.76 us
    ppermute x2, starting transfers between devices, forward(): return lax.ppermute(block, 'sfc', to_next())  3.76 us
    ppermute x1, starting transfers between devices, odd_to_next(): lax.ppermute(block, 'sfc', [(i, i + 1) for i in range(ODD, n - 1, 2)])  1.29 us
    ppermute x4, starting transfers between devices, swap(): lax.ppermute(block, 'sfc', [(i, i ^ 1) for i in range(lax.axis_size('sfc'...  0.78 us
    ppermute x4, waiting for transfers between devices, swap(): lax.ppermute(block, 'sfc', [(i, i ^ 1) for i in range(lax.axis_size('sfc'...  0.67 us
  transfers between devices with their start and end apart: 9, of which 4 were waited for; matrix products, arithmetic and copies ran while one was open for 0% of the time, Pallas kernels for 29%

profile of v2, /device:TPU:128, one launch (start us, length us, event | category | flops | bytes accessed | tf_op | source)
XLA Modules:
  0.0 25.5 jit_solution(11678352250764847618)
XLA Ops:
  0.0 0.1 assemble_odd.1
  0.1 1.3 %collective-permute-start = (f32[8,128]{1,0:T(8,128)S(1)}, f32[8,128]{1,0:T(8,128)S(1)}, u32[]{:S(2)}, u32[]{:S(2)}) collective-permute-start(f32[8,128]{1,0:T(8,128)S(1)} %get-tuple-element.27.odd_up.up), channel_id=1, source_target_pairs={{1,2},{3,4},{5,6},{7,8},{9,10},{11,12},{13,14},{15,16},{17,18},{19... | collective-permute-start | bytes 12296 | tf_op jit(solution)/shard_map/ppermute | solution.py:255
  1.4 4.3 %assemble_even.1 = (bf16[48,256,128]{2,1,0:T(8,128)(2,1)S(1)}, f32[2,16,128]{2,1,0:T(8,128)S(1)}, f32[128,128]{1,0:T(8,128)S(1)}, f32[16,128]{1,0:T(8,128)S(1)},...) custom-call(bf16[48,256,128]{2,1,0:T(8,128)(2,1)} %bitcast.3, s32[2,48]{1,0:T(2,128)} %bitcast.5, f32[48,128]{1,0:T(8,128)} %mobility.3, ...), custom_call_target="tpu_custom_call" | custom-call | flops 10000000000 | bytes 100000000 | tf_op jit(solution)/shard_map/assemble_even/pallas_call | solution.py:297
  5.7 0.1 collective-permute-start.1
  5.8 4.9 %collective-permute-start.2 = (f32[16,128]{1,0:T(8,128)S(1)}, f32[16,128]{1,0:T(8,128)S(1)}, u32[]{:S(2)}, u32[]{:S(2)}) collective-permute-start(f32[16,128]{1,0:T(8,128)S(1)} %get-tuple-element.31.own), channel_id=1, source_target_pairs={{1,0},{2,1},{3,2},{4,3},{0,4},{6,5},{7,6},{8,7},{9,8},{10,9},{11,1... | collective-permute-start | bytes 24584 | tf_op jit(solution)/shard_map/ppermute | solution.py:250
  10.7 0.4 %collective-permute-done.block = f32[8,128]{1,0:T(8,128)S(1)} collective-permute-done((f32[8,128]{1,0:T(8,128)S(1)}, f32[8,128]{1,0:T(8,128)S(1)}, u32[]{:S(2)}, u32[]{:S(2)}) %collective-permute-start) | collective-permute-done | bytes 4128 | tf_op jit(solution)/shard_map/ppermute | solution.py:255
  11.1 0.0 collective-permute-done.1.from_next.from_prev
  11.1 1.6 %first_even.1 = (f32[8,128]{1,0:T(8,128)S(1)}, f32[8,128]{1,0:T(8,128)S(1)}) custom-call(bf16[48,256,128]{2,1,0:T(8,128)(2,1)S(1)} %get-tuple-element.28.weighted, f32[2,16,128]{2,1,0:T(8,128)S(1)} %get-tuple-element.29.place, f32[128,128]{1,0:T(8,128)S(1)} %get-tuple-element.30.pick, f32[16,128]{1,0:T(8,128)S(1)} %get-tuple-element.31.own, ...), custom_call_target="tpu_custom_call" | custom-call | flops 10000000000 | bytes 100000000 | tf_op jit(solution)/shard_map/first_even/pallas_call | solution.py:285
  12.7 0.0 collective-permute-start.6
  12.7 0.5 %collective-permute-start.5 = (f32[8,128]{1,0:T(8,128)S(1)}, f32[8,128]{1,0:T(8,128)S(1)}, u32[]{:S(2)}, u32[]{:S(2)}) collective-permute-start(f32[8,128]{1,0:T(8,128)S(1)} %get-tuple-element.35.outs_0_.y_up), channel_id=1, source_target_pairs={{0,1},{1,0},{2,3},{3,2},{4,5},{5,4},{6,7},{7,6},{8,9},{9,8},{10,11... | collective-permute-start | bytes 12296 | tf_op jit(solution)/shard_map/ppermute | solution.py:259
  13.2 0.0 collective-permute-done.2.from_next
  13.2 1.7 %collective-permute-start.3 = (f32[8,128]{1,0:T(8,128)S(1)}, f32[8,128]{1,0:T(8,128)S(1)}, u32[]{:S(2)}, u32[]{:S(2)}) collective-permute-start(f32[8,128]{1,0:T(8,128)S(1)} %get-tuple-element.39.y_up), channel_id=1, source_target_pairs={{0,1},{1,2},{2,3},{3,4},{4,0},{5,6},{6,7},{7,8},{8,9},{9,10},{10,1... | collective-permute-start | bytes 12296 | tf_op jit(solution)/shard_map/ppermute | solution.py:246
  14.9 0.1 collective-permute-start.4
  15.0 0.0 collective-permute-done.6.y_next
  15.0 0.0 collective-permute-done.5.y_prev
  15.0 2.1 %collective-permute-start.7 = (f32[8,128]{1,0:T(8,128)S(1)}, f32[8,128]{1,0:T(8,128)S(1)}, u32[]{:S(2)}, u32[]{:S(2)}) collective-permute-start(f32[8,128]{1,0:T(8,128)S(1)} %get-tuple-element.41.outs_0_), channel_id=1, source_target_pairs={{0,1},{1,2},{2,3},{3,4},{4,0},{5,6},{6,7},{7,8},{8,9},{9,10},{10,1... | collective-permute-start | bytes 12296 | tf_op jit(solution)/shard_map/ppermute | solution.py:246
  17.1 5.0 %collective-permute-done.3.y_prev = f32[8,128]{1,0:T(8,128)S(1)} collective-permute-done((f32[8,128]{1,0:T(8,128)S(1)}, f32[8,128]{1,0:T(8,128)S(1)}, u32[]{:S(2)}, u32[]{:S(2)}) %collective-permute-start.3) | collective-permute-done | bytes 4128 | tf_op jit(solution)/shard_map/ppermute | solution.py:246
  22.1 0.0 collective-permute-done.4.y_next
  22.1 1.6 %second_even.1 = (f32[8,128]{1,0:T(8,128)S(1)}, f32[8,128]{1,0:T(8,128)S(1)}, f32[8,128]{1,0:T(8,128)S(1)}) custom-call(bf16[48,256,128]{2,1,0:T(8,128)(2,1)S(1)} %get-tuple-element.28.weighted, f32[2,16,128]{2,1,0:T(8,128)S(1)} %get-tuple-element.29.place, f32[128,128]{1,0:T(8,128)S(1)} %get-tuple-element.30.pick, f32[16,128]{1,0:T(8,128)S(1)} %get-tuple-element.31.own, ...), custom_call_target="tpu_custom_call" | custom-call | flops 10000000000 | bytes 100000000 | tf_op jit(solution)/shard_map/second_even/pallas_call | solution.py:285
  23.7 0.1 collective-permute-start.8
  23.8 0.5 %collective-permute-done.7.z_prev = f32[8,128]{1,0:T(8,128)S(1)} collective-permute-done((f32[8,128]{1,0:T(8,128)S(1)}, f32[8,128]{1,0:T(8,128)S(1)}, u32[]{:S(2)}, u32[]{:S(2)}) %collective-permute-start.7) | collective-permute-done | bytes 4128 | tf_op jit(solution)/shard_map/ppermute | solution.py:246
  24.3 0.7 %collective-permute-done.8.z_prev = f32[8,128]{1,0:T(8,128)S(1)} collective-permute-done((f32[8,128]{1,0:T(8,128)S(1)}, f32[8,128]{1,0:T(8,128)S(1)}, u32[]{:S(2)}, u32[]{:S(2)}) %collective-permute-start.8) | collective-permute-done | bytes 4128 | tf_op jit(solution)/shard_map/ppermute | solution.py:259
  24.9 0.6 %finish.1 = f32[6,128]{1,0:T(8,128)} custom-call(f32[8,128]{1,0:T(8,128)S(1)} %finish_even.1.even, f32[8,128]{1,0:T(8,128)S(1)} %get-tuple-element.44.rest, f32[8,128]{1,0:T(8,128)S(1)} %get-tuple-element.45.factor, f32[8,128]{1,0:T(8,128)S(1)} %collective-permute-done.8.z_prev), custom_call_target="tpu_custom_call" | custom-call | flops 10000000000 | bytes 100000000 | tf_op jit(solution)/shard_map/finish/pallas_call | solution.py:285
  (4 shorter events, 0.0 us)
Async XLA Ops:
  0.1 11.0 %collective-permute-start = (f32[8,128]{1,0:T(8,128)S(1)}, f32[8,128]{1,0:T(8,128)S(1)}, u32[]{:S(2)}, u32[]{:S(2)}) collective-permute-start(f32[8,128]{1,0:T(8,128)S(1)} %get-tuple-element.27.odd_up.up), channel_id=1, source_target_pairs={{1,2},{3,4},{5,6},{7,8},{9,10},{11,12},{13,14},{15,16},{17,18},{19... | collective-permute-start | bytes 12296 | tf_op jit(solution)/shard_map/ppermute | solution.py:255
  5.7 5.4 %collective-permute-start.1 = (f32[16,128]{1,0:T(8,128)S(1)}, f32[16,128]{1,0:T(8,128)S(1)}, u32[]{:S(2)}, u32[]{:S(2)}) collective-permute-start(f32[16,128]{1,0:T(8,128)S(1)} %get-tuple-element.33), channel_id=1, source_target_pairs={{0,1},{1,0},{2,3},{3,2},{4,5},{5,4},{6,7},{7,6},{8,9},{9,8},{10,11... | collective-permute-start | bytes 24584 | tf_op jit(solution)/shard_map/ppermute | solution.py:259
  5.8 7.4 %collective-permute-start.2 = (f32[16,128]{1,0:T(8,128)S(1)}, f32[16,128]{1,0:T(8,128)S(1)}, u32[]{:S(2)}, u32[]{:S(2)}) collective-permute-start(f32[16,128]{1,0:T(8,128)S(1)} %get-tuple-element.31.own), channel_id=1, source_target_pairs={{1,0},{2,1},{3,2},{4,3},{0,4},{6,5},{7,6},{8,7},{9,8},{10,9},{11,1... | collective-permute-start | bytes 24584 | tf_op jit(solution)/shard_map/ppermute | solution.py:250
  12.7 2.4 %collective-permute-start.6 = (f32[8,128]{1,0:T(8,128)S(1)}, f32[8,128]{1,0:T(8,128)S(1)}, u32[]{:S(2)}, u32[]{:S(2)}) collective-permute-start(f32[8,128]{1,0:T(8,128)S(1)} %get-tuple-element.34.y_own), channel_id=1, source_target_pairs={{1,0},{2,1},{3,2},{4,3},{0,4},{6,5},{7,6},{8,7},{9,8},{10,9},{11,1... | collective-permute-start | bytes 12296 | tf_op jit(solution)/shard_map/ppermute | solution.py:250
  12.7 2.3 %collective-permute-start.5 = (f32[8,128]{1,0:T(8,128)S(1)}, f32[8,128]{1,0:T(8,128)S(1)}, u32[]{:S(2)}, u32[]{:S(2)}) collective-permute-start(f32[8,128]{1,0:T(8,128)S(1)} %get-tuple-element.35.outs_0_.y_up), channel_id=1, source_target_pairs={{0,1},{1,0},{2,3},{3,2},{4,5},{5,4},{6,7},{7,6},{8,9},{9,8},{10,11... | collective-permute-start | bytes 12296 | tf_op jit(solution)/shard_map/ppermute | solution.py:259
  13.2 8.9 %collective-permute-start.3 = (f32[8,128]{1,0:T(8,128)S(1)}, f32[8,128]{1,0:T(8,128)S(1)}, u32[]{:S(2)}, u32[]{:S(2)}) collective-permute-start(f32[8,128]{1,0:T(8,128)S(1)} %get-tuple-element.39.y_up), channel_id=1, source_target_pairs={{0,1},{1,2},{2,3},{3,4},{4,0},{5,6},{6,7},{7,8},{8,9},{9,10},{10,1... | collective-permute-start | bytes 12296 | tf_op jit(solution)/shard_map/ppermute | solution.py:246
  14.9 7.2 %collective-permute-start.4 = (f32[8,128]{1,0:T(8,128)S(1)}, f32[8,128]{1,0:T(8,128)S(1)}, u32[]{:S(2)}, u32[]{:S(2)}) collective-permute-start(f32[8,128]{1,0:T(8,128)S(1)} %get-tuple-element.40.y_own), channel_id=1, source_target_pairs={{0,1},{1,0},{2,3},{3,2},{4,5},{5,4},{6,7},{7,6},{8,9},{9,8},{10,11... | collective-permute-start | bytes 12296 | tf_op jit(solution)/shard_map/ppermute | solution.py:259
  15.0 9.2 %collective-permute-start.7 = (f32[8,128]{1,0:T(8,128)S(1)}, f32[8,128]{1,0:T(8,128)S(1)}, u32[]{:S(2)}, u32[]{:S(2)}) collective-permute-start(f32[8,128]{1,0:T(8,128)S(1)} %get-tuple-element.41.outs_0_), channel_id=1, source_target_pairs={{0,1},{1,2},{2,3},{3,4},{4,0},{5,6},{6,7},{7,8},{8,9},{9,10},{10,1... | collective-permute-start | bytes 12296 | tf_op jit(solution)/shard_map/ppermute | solution.py:246
  23.7 1.3 %collective-permute-start.8 = (f32[8,128]{1,0:T(8,128)S(1)}, f32[8,128]{1,0:T(8,128)S(1)}, u32[]{:S(2)}, u32[]{:S(2)}) collective-permute-start(f32[8,128]{1,0:T(8,128)S(1)} %get-tuple-element.46), channel_id=1, source_target_pairs={{0,1},{1,0},{2,3},{3,2},{4,5},{5,4},{6,7},{7,6},{8,9},{9,8},{10,11... | collective-permute-start | bytes 12296 | tf_op jit(solution)/shard_map/ppermute | solution.py:259

commit v3 on v2

--- a/solution.py
+++ b/solution.py
@@ -47,10 +47,10 @@
     return total
 
 
-def assemble_here(tiles, couples, mobility, rhs, weighted, place, pick, own, up, scratch, sems):
+def assemble_here(tiles, couples, mobility, rhs, weighted, turned, place, pick, own, up,
+                  local_couples, local_mobility, local_rhs, sems):
     count, here = tiles.shape[0], rhs.shape[0]
     step = count // CHUNKS
-    local_couples, local_mobility, local_rhs = scratch
     small = (couples, local_couples), (mobility, local_mobility), (rhs, local_rhs)
     small = [pltpu.make_async_copy(a, b, sems.at[CHUNKS + i]) for i, (a, b) in enumerate(small)]
     for copy in small:
@@ -74,42 +74,38 @@
     for k in range(2):
         place[k] = places[k]
     pick[...] = jnp.concatenate(places + [jnp.zeros((96, 128), f32)], axis=0).T
-    sub = lax.broadcasted_iota(jnp.int32, (8, 128), 0)
-    lane = lax.broadcasted_iota(jnp.int32, (8, 128), 1)
-    sums = [[], []]
+    local_mobility[...] = jnp.sqrt(local_mobility[...])
+    sub = lax.broadcasted_iota(jnp.int32, (8, 256), 0)
+    sums = []
     for c in range(CHUNKS):
         copies[c].wait()
-        for g in range(step // GROUP):
-            picked_rows = [jnp.zeros((8, 128), f32)] * 2
-            for j in range(GROUP):
-                v = c * step + g * GROUP + j
-                root = jnp.sqrt(local_mobility[v : v + 1, :])
-                half = (weighted[v].astype(f32) * root).astype(bf16)
-                weighted[v] = half
-                for k in range(2):
-                    tile = half[k * 128 : (k + 1) * 128]
-                    square = lax.dot_general(
-                        tile, tile, (((1,), (1,)), ((), ())), preferred_element_type=f32
-                    )
-                    picked = square[:8]
-                    for i in range(1, 16):
-                        picked = jnp.where(lane // 8 == i, square[8 * i : 8 * i + 8], picked)
-                    picked = jnp.where(lane % 8 == sub, picked, 0.0)
-                    picked = jnp.sum(picked, axis=0, keepdims=True)
-                    picked_rows[k] = jnp.where(sub == j, picked, picked_rows[k])
-            for k in range(2):
-                sums[k].append(picked_rows[k])
-    total = scatter(places, [jnp.concatenate(s, axis=0) for s in sums])
+        for v in range(c * step, (c + 1) * step):
+            half = (weighted[v].astype(f32) * local_mobility[v : v + 1, :]).astype(bf16)
+            weighted[v] = half
+            half = half.T
+            turned[v] = half
+            square = half.astype(f32)
+            square = square * square
+            total = square[:8]
+            for i in range(1, 16):
+                total = total + square[8 * i : 8 * i + 8]
+            total = jnp.sum(total, axis=0, keepdims=True)
+            if v % GROUP == 0:
+                sums.append(jnp.broadcast_to(total, (8, 256)))
+            else:
+                sums[-1] = jnp.where(sub == v % GROUP, total, sums[-1])
+    sums = jnp.concatenate(sums, axis=0)
+    total = scatter(places, [sums[:, :128], sums[:, 128:]])
     own[:8, :] = total[:8]
     own[8:, :] = jnp.concatenate([local_rhs[...], jnp.zeros((8 - here, 128), f32)], axis=0)
     up[...] = total[8:]
 
 
-def assemble_odd(tiles, couples, mobility, rhs, weighted, place, pick, own, up, *scratch):
+def assemble_odd(tiles, couples, mobility, rhs, weighted, turned, place, pick, own, up, *scratch):
     @pl.when(position() % 2 == ODD)
     def _():
         assemble_here(
-            tiles, couples, mobility, rhs, weighted, place, pick, own, up, scratch[:3], scratch[3]
+            tiles, couples, mobility, rhs, weighted, turned, place, pick, own, up, *scratch
         )
 
     @pl.when(position() % 2 == EVEN)
@@ -118,11 +114,11 @@
 
 
 def assemble_even(tiles, couples, mobility, rhs, odd_own, odd_up,
-                  weighted, place, pick, own, up, swapped, *scratch):
+                  weighted, turned, place, pick, own, up, swapped, *scratch):
     @pl.when(position() % 2 == EVEN)
     def _():
         assemble_here(
-            tiles, couples, mobility, rhs, weighted, place, pick, own, up, scratch[:3], scratch[3]
+            tiles, couples, mobility, rhs, weighted, turned, place, pick, own, up, *scratch
         )
         swapped[:8, :] = up[...]
         swapped[8:, :] = up[...]
@@ -137,7 +133,7 @@
     out[...] = block[...]
 
 
-def multiply(weighted, place, pick, mine, following):
+def multiply(weighted, turned, place, pick, mine, following):
     count = weighted.shape[0]
     high, low = parts(jnp.concatenate([mine, following], axis=0))
     none = jnp.zeros_like(high)
@@ -168,9 +164,7 @@
         left = jnp.concatenate(parts(inner[g]), axis=0).astype(bf16)
         total = None
         for j in range(GROUP):
-            both = lax.dot_general(
-                left, weighted[GROUP * g + j], (((1,), (1,)), ((), ())), preferred_element_type=f32
-            )
+            both = jnp.dot(left, turned[GROUP * g + j], preferred_element_type=f32)
             both = both[:8] + both[8:]
             total = both if total is None else jnp.where(sub2 == j, both, total)
         outer.append(total)
@@ -187,35 +181,34 @@
     target = jnp.where(live, own[8:, :], 0.0)
     target_next = jnp.where(other, from_next[8:, :], 0.0)
     scale, scale_next = relax / diag, relax / diag_next
-    return (scale, target, scale * target), (scale_next, target_next, scale_next * target_next)
-
-
-def first_sweep(here, parity, weighted, place, pick, own, up, from_prev, from_next, *outs):
-    y_own, y_up = outs[-2:]
+    return scale, target, scale * target, scale_next, target_next, scale_next * target_next
+
+
+def first_sweep(here, parity, weighted, turned, place, pick, own, up, from_prev, from_next, *outs):
+    y_own, y_up, state = outs[-3:]
 
     @pl.when(position() % 2 == parity)
     def _():
-        mine, following = starts(here, own, up, from_prev, from_next)
-        y_own[...], y_up[...] = multiply(weighted, place, pick, mine[2], following[2])
+        now = starts(here, own, up, from_prev, from_next)
+        y_own[...], y_up[...] = multiply(weighted, turned, place, pick, now[2], now[5])
+        for i in range(6):
+            state[i] = now[i]
 
     @pl.when(position() % 2 != parity)
     def _():
         y_own[...] = y_up[...] = jnp.zeros_like(y_up)
 
 
-def second_sweep(here, parity, weighted, place, pick, own, up, from_prev, from_next,
-                 y_own, y_up, y_prev, y_next, *outs):
+def second_sweep(parity, weighted, turned, place, pick, y_own, y_up, state, y_prev, y_next, *outs):
     z_up, rest, factor = outs[-3:]
 
     @pl.when(position() % 2 == parity)
     def _():
-        mine, following = starts(here, own, up, from_prev, from_next)
-        scale, target, p = mine
-        scale_next, target_next, p_next = following
+        scale, target, p, scale_next, target_next, p_next = [state[i] for i in range(6)]
         p = p + scale * (target - (y_own[...] + y_prev[...]))
         p_next = p_next + scale_next * (target_next - (y_next[...] + y_up[...]))
         p_next = jnp.where(is_last(), 0.0, p_next)
-        z_own, z_up[...] = multiply(weighted, place, pick, p, p_next)
+        z_own, z_up[...] = multiply(weighted, turned, place, pick, p, p_next)
         rest[...] = p + scale * (target - z_own)
         factor[...] = scale
 
@@ -269,6 +262,7 @@
     small = jax.ShapeDtypeStruct((8, size), f32)
     assembled = (
         pltpu.VMEM(tiles.shape, bf16),
+        pltpu.VMEM((count, size, pairs * size), bf16),
         jax.ShapeDtypeStruct((2, 16, 128), f32),
         jax.ShapeDtypeStruct((128, 128), f32),
         jax.ShapeDtypeStruct((16, size), f32),
@@ -294,7 +288,7 @@
         )(*operands)
 
     def assembled_by(kernel, outs, name, *order):
-        weighted, *others = pl.pallas_call(
+        weighted, turned, *others = pl.pallas_call(
             kernel,
             out_shape=outs,
             in_specs=[ANY] * 4 + [VMEM] * len(order),
@@ -304,36 +298,35 @@
             cost_estimate=cost,
             name=name,
         )(*args, *order)
-        return in_vmem(weighted), *others
-
-    known_o = assembled_by(assemble_odd, assembled, "assemble_odd")
-    up_e = odd_to_next(known_o[4])
-    *known_e, swapped = assembled_by(
-        assemble_even, assembled + assembled[3:4], "assemble_even", *known_o[3:]
-    )
-    next_own_o = backward(known_e[3])
+        return in_vmem(weighted), in_vmem(turned), *others
+
+    *matrix_o, own_o, up_o = assembled_by(assemble_odd, assembled, "assemble_odd")
+    from_prev_e = odd_to_next(up_o)
+    *matrix_e, own_e, up_e, swapped = assembled_by(
+        assemble_even, assembled + assembled[4:5], "assemble_even", own_o, up_o
+    )
+    from_next_o = backward(own_e)
     swapped = swap(swapped)
-    up_e = call(pass_on, small, "pass_on", up_e)
-    known_e = (*known_e, up_e, swapped)
-    known_o = (*known_o, swapped, next_own_o)
-    y_own_e, y_up_e = call(
-        functools.partial(first_sweep, here, EVEN), (small, small), "first_even", *known_e
-    )
-    y_next_o = backward(y_own_e)
-    y_prev_o = swap(y_up_e)
-    y_own_o, y_up_o = call(
-        functools.partial(first_sweep, here, ODD), (small, small), "first_odd", *known_o, y_up_e
-    )
-    y_prev_e = forward(y_up_o)
-    y_next_e = swap(y_own_o)
+    from_prev_e = call(pass_on, small, "pass_on", from_prev_e)
+    first = (small, small, jax.ShapeDtypeStruct((6, 8, size), f32))
+    sweep_e = call(
+        functools.partial(first_sweep, here, EVEN), first, "first_even",
+        *matrix_e, own_e, up_e, from_prev_e, swapped,
+    )
+    y_next_o, y_prev_o = backward(sweep_e[0]), swap(sweep_e[1])
+    sweep_o = call(
+        functools.partial(first_sweep, here, ODD), first, "first_odd",
+        *matrix_o, own_o, up_o, swapped, from_next_o, sweep_e[1],
+    )
+    y_prev_e, y_next_e = forward(sweep_o[1]), swap(sweep_o[0])
     z_up_o, rest_o, factor_o = call(
-        functools.partial(second_sweep, here, ODD), (small,) * 3, "second_odd",
-        *known_o, y_own_o, y_up_o, y_prev_o, y_next_o,
+        functools.partial(second_sweep, ODD), (small,) * 3, "second_odd",
+        *matrix_o, *sweep_o, y_prev_o, y_next_o,
     )
     z_prev_e = forward(z_up_o)
     z_up_e, rest_e, factor_e = call(
-        functools.partial(second_sweep, here, EVEN), (small,) * 3, "second_even",
-        *known_e, y_own_e, y_up_e, y_prev_e, y_next_e, z_up_o,
+        functools.partial(second_sweep, EVEN), (small,) * 3, "second_even",
+        *matrix_e, *sweep_e, y_prev_e, y_next_e, z_up_o,
     )
     z_prev_o = swap(z_up_e)
     even = call(finish_even, small, "finish_even", rest_e, factor_e, z_prev_e)

time: 26 us -> 24.1 us (0.927)
  Pallas kernels: 8.19 us -> 5.71 us
  waiting for transfers between devices: 6.56 us -> 7.55 us
  starting transfers between devices: 10.7 us -> 10.3 us
    pallas_call x2, Pallas kernels: 4.43 us -> 2.78 us  [assembled_by(): pl.pallas_call(kernel, out_shape=outs, in_specs=[ANY] * 4 + [VMEM] * len(...]
    pallas_call x7, Pallas kernels: 3.76 us -> 2.93 us  [call(): pl.pallas_call(kernel, out_shape=outs, in_specs=[VMEM] * len(operands), o...]
    ppermute x2, starting transfers between devices: 3.76 us -> 2.94 us  [forward(): return lax.ppermute(block, 'sfc', to_next())]
    ppermute x2, waiting for transfers between devices: 5.5 us -> 6.17 us  [forward(): return lax.ppermute(block, 'sfc', to_next())]
    ppermute x1, waiting for transfers between devices: 0.39 us -> 0.98 us  [odd_to_next(): lax.ppermute(block, 'sfc', [(i, i + 1) for i in range(ODD, n - 1, 2)])]
    ppermute x2, starting transfers between devices: 4.9 us -> 5.31 us  [backward(): return lax.ppermute(block, 'sfc', [(b, a) for a, b in to_next()])]
    ppermute x4, waiting for transfers between devices: 0.67 us -> 0.4 us  [swap(): lax.ppermute(block, 'sfc', [(i, i ^ 1) for i in range(lax.axis_size('sfc'...]
  transfers between devices with their start and end apart: 9 -> 9, of which waited for: 4 -> 4; matrix products, arithmetic and copies ran while one was open for 0% -> 0% of each run, Pallas kernels for 29% -> 21%
where the time goes in v3:
time: 24.1 us; the launch traced here: 23.6 us
  starting transfers between devices  10.3 us (43%)
  waiting for transfers between devices  7.55 us (31%)
  Pallas kernels  5.71 us (24%)
    ppermute x2, waiting for transfers between devices, forward(): return lax.ppermute(block, 'sfc', to_next())  6.17 us
    ppermute x2, starting transfers between devices, backward(): return lax.ppermute(block, 'sfc', [(b, a) for a, b in to_next()])  5.31 us
    ppermute x2, starting transfers between devices, forward(): return lax.ppermute(block, 'sfc', to_next())  2.94 us
    pallas_call x7, Pallas kernels, call(): pl.pallas_call(kernel, out_shape=outs, in_specs=[VMEM] * len(operands), o...  2.93 us
    pallas_call x2, Pallas kernels, assembled_by(): pl.pallas_call(kernel, out_shape=outs, in_specs=[ANY] * 4 + [VMEM] * len(...  2.78 us
    ppermute x1, starting transfers between devices, odd_to_next(): lax.ppermute(block, 'sfc', [(i, i + 1) for i in range(ODD, n - 1, 2)])  1.29 us
    ppermute x1, waiting for transfers between devices, odd_to_next(): lax.ppermute(block, 'sfc', [(i, i + 1) for i in range(ODD, n - 1, 2)])  0.98 us
    ppermute x4, starting transfers between devices, swap(): lax.ppermute(block, 'sfc', [(i, i ^ 1) for i in range(lax.axis_size('sfc'...  0.78 us
  transfers between devices with their start and end apart: 9, of which 4 were waited for; matrix products, arithmetic and copies ran while one was open for 0% of the time, Pallas kernels for 21%

profile of v3, /device:TPU:128, one launch (start us, length us, event | category | flops | bytes accessed | tf_op | source)
XLA Modules:
  0.0 23.6 jit_solution(8447247072364731383)
XLA Ops:
  0.0 0.1 assemble_odd.1
  0.1 1.3 %collective-permute-start = (f32[8,128]{1,0:T(8,128)S(1)}, f32[8,128]{1,0:T(8,128)S(1)}, u32[]{:S(2)}, u32[]{:S(2)}) collective-permute-start(f32[8,128]{1,0:T(8,128)S(1)} %get-tuple-element.31.odd_up.up), channel_id=1, source_target_pairs={{1,2},{3,4},{5,6},{7,8},{9,10},{11,12},{13,14},{15,16},{17,18},{19... | collective-permute-start | bytes 12296 | tf_op jit(solution)/shard_map/ppermute | solution.py:248
  1.4 2.7 %assemble_even.1 = (bf16[48,256,128]{2,1,0:T(8,128)(2,1)S(1)}, bf16[48,128,256]{2,1,0:T(8,128)(2,1)S(1)}, f32[2,16,128]{2,1,0:T(8,128)S(1)}, f32[128,128]{1,0:T(...) custom-call(bf16[48,256,128]{2,1,0:T(8,128)(2,1)} %bitcast.3, s32[2,48]{1,0:T(2,128)} %bitcast.5, ...), custom_call_target="tpu_custom_call" | custom-call | flops 10000000000 | bytes 100000000 | tf_op jit(solution)/shard_map/assemble_even/pallas_call | solution.py:291
  4.1 0.1 collective-permute-start.1
  4.2 5.3 %collective-permute-start.2 = (f32[16,128]{1,0:T(8,128)S(1)}, f32[16,128]{1,0:T(8,128)S(1)}, u32[]{:S(2)}, u32[]{:S(2)}) collective-permute-start(f32[16,128]{1,0:T(8,128)S(1)} %get-tuple-element.36.own), channel_id=1, source_target_pairs={{1,0},{2,1},{3,2},{4,3},{0,4},{6,5},{7,6},{8,7},{9,8},{10,9},{11,1... | collective-permute-start | bytes 24584 | tf_op jit(solution)/shard_map/ppermute | solution.py:243
  9.5 1.0 %collective-permute-done.block = f32[8,128]{1,0:T(8,128)S(1)} collective-permute-done((f32[8,128]{1,0:T(8,128)S(1)}, f32[8,128]{1,0:T(8,128)S(1)}, u32[]{:S(2)}, u32[]{:S(2)}) %collective-permute-start) | collective-permute-done | bytes 4128 | tf_op jit(solution)/shard_map/ppermute | solution.py:248
  10.4 0.0 collective-permute-done.1.from_next.from_prev
  10.5 1.2 %first_even.1 = (f32[8,128]{1,0:T(8,128)S(1)}, f32[8,128]{1,0:T(8,128)S(1)}, f32[6,8,128]{2,1,0:T(8,128)S(1)}) custom-call(bf16[48,256,128]{2,1,0:T(8,128)(2,1)S(1)} %get-tuple-element.32.weighted, bf16[48,128,256]{2,1,0:T(8,128)(2,1)S(1)} %get-tuple-element.33.turned, f32[2,16,128]{2,1,0:T(8,128)S(1)} %get-tuple-element.34.place, ...), custom_call_target="tpu_custom_call" | custom-call | flops 10000000000 | bytes 100000000 | tf_op jit(solution)/shard_map/first_even/pallas_call | solution.py:279
  11.6 0.0 collective-permute-start.6
  11.7 0.5 %collective-permute-start.5 = (f32[8,128]{1,0:T(8,128)S(1)}, f32[8,128]{1,0:T(8,128)S(1)}, u32[]{:S(2)}, u32[]{:S(2)}) collective-permute-start(f32[8,128]{1,0:T(8,128)S(1)} %get-tuple-element.40.outs_0_.y_up), channel_id=1, source_target_pairs={{0,1},{1,0},{2,3},{3,2},{4,5},{5,4},{6,7},{7,6},{8,9},{9,8},{10,11... | collective-permute-start | bytes 12296 | tf_op jit(solution)/shard_map/ppermute | solution.py:252
  12.2 0.0 collective-permute-done.2.from_next
  12.2 1.3 %collective-permute-start.3 = (f32[8,128]{1,0:T(8,128)S(1)}, f32[8,128]{1,0:T(8,128)S(1)}, u32[]{:S(2)}, u32[]{:S(2)}) collective-permute-start(f32[8,128]{1,0:T(8,128)S(1)} %get-tuple-element.46.y_up), channel_id=1, source_target_pairs={{0,1},{1,2},{2,3},{3,4},{4,0},{5,6},{6,7},{7,8},{8,9},{9,10},{10,1... | collective-permute-start | bytes 12296 | tf_op jit(solution)/shard_map/ppermute | solution.py:239
  13.5 0.1 collective-permute-start.4
  13.6 0.0 collective-permute-done.6.y_next
  13.6 0.0 collective-permute-done.5.y_prev
  13.6 1.6 %collective-permute-start.7 = (f32[8,128]{1,0:T(8,128)S(1)}, f32[8,128]{1,0:T(8,128)S(1)}, u32[]{:S(2)}, u32[]{:S(2)}) collective-permute-start(f32[8,128]{1,0:T(8,128)S(1)} %get-tuple-element.49.outs_0_), channel_id=1, source_target_pairs={{0,1},{1,2},{2,3},{3,4},{4,0},{5,6},{6,7},{7,8},{8,9},{9,10},{10,1... | collective-permute-start | bytes 12296 | tf_op jit(solution)/shard_map/ppermute | solution.py:239
  15.2 5.4 %collective-permute-done.3.y_prev = f32[8,128]{1,0:T(8,128)S(1)} collective-permute-done((f32[8,128]{1,0:T(8,128)S(1)}, f32[8,128]{1,0:T(8,128)S(1)}, u32[]{:S(2)}, u32[]{:S(2)}) %collective-permute-start.3) | collective-permute-done | bytes 4128 | tf_op jit(solution)/shard_map/ppermute | solution.py:239
  20.6 0.0 collective-permute-done.4.y_next
  20.6 1.2 %second_even.1 = (f32[8,128]{1,0:T(8,128)S(1)}, f32[8,128]{1,0:T(8,128)S(1)}, f32[8,128]{1,0:T(8,128)S(1)}) custom-call(bf16[48,256,128]{2,1,0:T(8,128)(2,1)S(1)} %get-tuple-element.32.weighted, bf16[48,128,256]{2,1,0:T(8,128)(2,1)S(1)} %get-tuple-element.33.turned, f32[2,16,128]{2,1,0:T(8,128)S(1)} %get-tuple-element.34.place, ...), custom_call_target="tpu_custom_call" | custom-call | flops 10000000000 | bytes 100000000 | tf_op jit(solution)/shard_map/second_even/pallas_call | solution.py:279
  21.8 0.1 collective-permute-start.8
  21.9 0.8 %collective-permute-done.7.z_prev = f32[8,128]{1,0:T(8,128)S(1)} collective-permute-done((f32[8,128]{1,0:T(8,128)S(1)}, f32[8,128]{1,0:T(8,128)S(1)}, u32[]{:S(2)}, u32[]{:S(2)}) %collective-permute-start.7) | collective-permute-done | bytes 4128 | tf_op jit(solution)/shard_map/ppermute | solution.py:239
  22.7 0.4 %collective-permute-done.8.z_prev = f32[8,128]{1,0:T(8,128)S(1)} collective-permute-done((f32[8,128]{1,0:T(8,128)S(1)}, f32[8,128]{1,0:T(8,128)S(1)}, u32[]{:S(2)}, u32[]{:S(2)}) %collective-permute-start.8) | collective-permute-done | bytes 4128 | tf_op jit(solution)/shard_map/ppermute | solution.py:252
  23.0 0.6 %finish.1 = f32[6,128]{1,0:T(8,128)} custom-call(f32[8,128]{1,0:T(8,128)S(1)} %finish_even.1.even, f32[8,128]{1,0:T(8,128)S(1)} %get-tuple-element.52.rest, f32[8,128]{1,0:T(8,128)S(1)} %get-tuple-element.53.factor, f32[8,128]{1,0:T(8,128)S(1)} %collective-permute-done.8.z_prev), custom_call_target="tpu_custom_call" | custom-call | flops 10000000000 | bytes 100000000 | tf_op jit(solution)/shard_map/finish/pallas_call | solution.py:279
  (4 shorter events, 0.0 us)
Async XLA Ops:
  0.1 10.4 %collective-permute-start = (f32[8,128]{1,0:T(8,128)S(1)}, f32[8,128]{1,0:T(8,128)S(1)}, u32[]{:S(2)}, u32[]{:S(2)}) collective-permute-start(f32[8,128]{1,0:T(8,128)S(1)} %get-tuple-element.31.odd_up.up), channel_id=1, source_target_pairs={{1,2},{3,4},{5,6},{7,8},{9,10},{11,12},{13,14},{15,16},{17,18},{19... | collective-permute-start | bytes 12296 | tf_op jit(solution)/shard_map/ppermute | solution.py:248
  4.1 6.4 %collective-permute-start.1 = (f32[16,128]{1,0:T(8,128)S(1)}, f32[16,128]{1,0:T(8,128)S(1)}, u32[]{:S(2)}, u32[]{:S(2)}) collective-permute-start(f32[16,128]{1,0:T(8,128)S(1)} %get-tuple-element.38), channel_id=1, source_target_pairs={{0,1},{1,0},{2,3},{3,2},{4,5},{5,4},{6,7},{7,6},{8,9},{9,8},{10,11... | collective-permute-start | bytes 24584 | tf_op jit(solution)/shard_map/ppermute | solution.py:252
  4.2 8.0 %collective-permute-start.2 = (f32[16,128]{1,0:T(8,128)S(1)}, f32[16,128]{1,0:T(8,128)S(1)}, u32[]{:S(2)}, u32[]{:S(2)}) collective-permute-start(f32[16,128]{1,0:T(8,128)S(1)} %get-tuple-element.36.own), channel_id=1, source_target_pairs={{1,0},{2,1},{3,2},{4,3},{0,4},{6,5},{7,6},{8,7},{9,8},{10,9},{11,1... | collective-permute-start | bytes 24584 | tf_op jit(solution)/shard_map/ppermute | solution.py:243
  11.6 1.9 %collective-permute-start.6 = (f32[8,128]{1,0:T(8,128)S(1)}, f32[8,128]{1,0:T(8,128)S(1)}, u32[]{:S(2)}, u32[]{:S(2)}) collective-permute-start(f32[8,128]{1,0:T(8,128)S(1)} %get-tuple-element.39.y_own), channel_id=1, source_target_pairs={{1,0},{2,1},{3,2},{4,3},{0,4},{6,5},{7,6},{8,7},{9,8},{10,9},{11,1... | collective-permute-start | bytes 12296 | tf_op jit(solution)/shard_map/ppermute | solution.py:243
  11.7 1.9 %collective-permute-start.5 = (f32[8,128]{1,0:T(8,128)S(1)}, f32[8,128]{1,0:T(8,128)S(1)}, u32[]{:S(2)}, u32[]{:S(2)}) collective-permute-start(f32[8,128]{1,0:T(8,128)S(1)} %get-tuple-element.40.outs_0_.y_up), channel_id=1, source_target_pairs={{0,1},{1,0},{2,3},{3,2},{4,5},{5,4},{6,7},{7,6},{8,9},{9,8},{10,11... | collective-permute-start | bytes 12296 | tf_op jit(solution)/shard_map/ppermute | solution.py:252
  12.2 8.5 %collective-permute-start.3 = (f32[8,128]{1,0:T(8,128)S(1)}, f32[8,128]{1,0:T(8,128)S(1)}, u32[]{:S(2)}, u32[]{:S(2)}) collective-permute-start(f32[8,128]{1,0:T(8,128)S(1)} %get-tuple-element.46.y_up), channel_id=1, source_target_pairs={{0,1},{1,2},{2,3},{3,4},{4,0},{5,6},{6,7},{7,8},{8,9},{9,10},{10,1... | collective-permute-start | bytes 12296 | tf_op jit(solution)/shard_map/ppermute | solution.py:239
  13.5 7.2 %collective-permute-start.4 = (f32[8,128]{1,0:T(8,128)S(1)}, f32[8,128]{1,0:T(8,128)S(1)}, u32[]{:S(2)}, u32[]{:S(2)}) collective-permute-start(f32[8,128]{1,0:T(8,128)S(1)} %get-tuple-element.47.y_own), channel_id=1, source_target_pairs={{0,1},{1,0},{2,3},{3,2},{4,5},{5,4},{6,7},{7,6},{8,9},{9,8},{10,11... | collective-permute-start | bytes 12296 | tf_op jit(solution)/shard_map/ppermute | solution.py:252
  13.6 9.1 %collective-permute-start.7 = (f32[8,128]{1,0:T(8,128)S(1)}, f32[8,128]{1,0:T(8,128)S(1)}, u32[]{:S(2)}, u32[]{:S(2)}) collective-permute-start(f32[8,128]{1,0:T(8,128)S(1)} %get-tuple-element.49.outs_0_), channel_id=1, source_target_pairs={{0,1},{1,2},{2,3},{3,4},{4,0},{5,6},{6,7},{7,8},{8,9},{9,10},{10,1... | collective-permute-start | bytes 12296 | tf_op jit(solution)/shard_map/ppermute | solution.py:239
  21.8 1.3 %collective-permute-start.8 = (f32[8,128]{1,0:T(8,128)S(1)}, f32[8,128]{1,0:T(8,128)S(1)}, u32[]{:S(2)}, u32[]{:S(2)}) collective-permute-start(f32[8,128]{1,0:T(8,128)S(1)} %get-tuple-element.54), channel_id=1, source_target_pairs={{0,1},{1,0},{2,3},{3,2},{4,5},{5,4},{6,7},{7,6},{8,9},{9,8},{10,11... | collective-permute-start | bytes 12296 | tf_op jit(solution)/shard_map/ppermute | solution.py:252

commit v4 on v3

--- a/solution.py
+++ b/solution.py
@@ -25,6 +25,19 @@
 
 def is_last():
     return position() == lax.axis_size("sfc") - 1
+
+
+def plane_size():
+    return max(lax.axis_size("sfc") // 8, 8)
+
+
+def is_tail():
+    size = plane_size()
+    return (position() % size == size - 1) & jnp.logical_not(is_last())
+
+
+def is_head():
+    return position() % plane_size() == 0
 
 
 def parts(values):
@@ -101,36 +114,42 @@
     up[...] = total[8:]
 
 
-def assemble_odd(tiles, couples, mobility, rhs, weighted, turned, place, pick, own, up, *scratch):
-    @pl.when(position() % 2 == ODD)
+def assemble_tail(tiles, couples, mobility, rhs, weighted, turned, place, pick, own, up, *scratch):
+    @pl.when(is_tail())
     def _():
         assemble_here(
             tiles, couples, mobility, rhs, weighted, turned, place, pick, own, up, *scratch
         )
 
-    @pl.when(position() % 2 == EVEN)
+    @pl.when(jnp.logical_not(is_tail()))
     def _():
         up[...] = jnp.zeros_like(up)
 
 
-def assemble_even(tiles, couples, mobility, rhs, odd_own, odd_up,
-                  weighted, turned, place, pick, own, up, swapped, *scratch):
-    @pl.when(position() % 2 == EVEN)
+def assemble_others(tiles, couples, mobility, rhs, tail_own, tail_up,
+                    weighted, turned, place, pick, own, up, swapped, *scratch):
+    @pl.when(jnp.logical_not(is_tail()))
     def _():
         assemble_here(
             tiles, couples, mobility, rhs, weighted, turned, place, pick, own, up, *scratch
         )
-        swapped[:8, :] = up[...]
-        swapped[8:, :] = up[...]
-
-    @pl.when(position() % 2 == ODD)
+        odd = position() % 2 == ODD
+        swapped[:8, :] = jnp.where(odd, own[:8, :], up[...])
+        swapped[8:, :] = own[8:, :]
+
+    @pl.when(is_tail())
     def _():
         own[...] = jnp.zeros_like(own)
-        swapped[...] = odd_own[...]
-
-
-def pass_on(block, out):
-    out[...] = block[...]
+        up[...] = jnp.zeros_like(up)
+        swapped[...] = tail_own[...]
+
+
+def keep_head(block, out):
+    out[...] = jnp.where(is_head(), block[...], 0.0)
+
+
+def keep_inner(kept, block, out):
+    out[...] = jnp.where(is_head(), kept[...], block[...])
 
 
 def multiply(weighted, turned, place, pick, mine, following):
@@ -184,37 +203,78 @@
     return scale, target, scale * target, scale_next, target_next, scale_next * target_next
 
 
-def first_sweep(here, parity, weighted, turned, place, pick, own, up, from_prev, from_next, *outs):
-    y_own, y_up, state = outs[-3:]
-
-    @pl.when(position() % 2 == parity)
-    def _():
-        now = starts(here, own, up, from_prev, from_next)
-        y_own[...], y_up[...] = multiply(weighted, turned, place, pick, now[2], now[5])
-        for i in range(6):
-            state[i] = now[i]
-
-    @pl.when(position() % 2 != parity)
-    def _():
-        y_own[...] = y_up[...] = jnp.zeros_like(y_up)
-
-
-def second_sweep(parity, weighted, turned, place, pick, y_own, y_up, state, y_prev, y_next, *outs):
-    z_up, rest, factor = outs[-3:]
-
-    @pl.when(position() % 2 == parity)
-    def _():
-        scale, target, p, scale_next, target_next, p_next = [state[i] for i in range(6)]
-        p = p + scale * (target - (y_own[...] + y_prev[...]))
-        p_next = p_next + scale_next * (target_next - (y_next[...] + y_up[...]))
-        p_next = jnp.where(is_last(), 0.0, p_next)
-        z_own, z_up[...] = multiply(weighted, turned, place, pick, p, p_next)
-        rest[...] = p + scale * (target - z_own)
-        factor[...] = scale
-
-    @pl.when(position() % 2 != parity)
-    def _():
-        z_up[...] = jnp.zeros_like(z_up)
+def first_sweep_at(here, known, from_prev, from_next, y_own, y_up, state):
+    *matrix, own, up = known
+    now = starts(here, own, up, from_prev, from_next)
+    y_own[...], y_up[...] = multiply(*matrix, now[2], now[5])
+    for i in range(6):
+        state[i] = now[i]
+
+
+def second_sweep_at(matrix, y_own, y_up, state, y_prev, y_next, z_up, rest, factor):
+    scale, target, p, scale_next, target_next, p_next = [state[i] for i in range(6)]
+    p = p + scale * (target - (y_own[...] + y_prev[...]))
+    p_next = p_next + scale_next * (target_next - (y_next[...] + y_up[...]))
+    p_next = jnp.where(is_last(), 0.0, p_next)
+    z_own, z_up[...] = multiply(*matrix, p, p_next)
+    rest[...] = p + scale * (target - z_own)
+    factor[...] = scale
+
+
+def first_even(here, *refs):
+    known, (from_prev, from_next), outs = refs[:6], refs[6:8], refs[-3:]
+
+    @pl.when(position() % 2 == EVEN)
+    def _():
+        first_sweep_at(here, known, from_prev, from_next, *outs)
+
+    @pl.when(position() % 2 == ODD)
+    def _():
+        outs[0][...] = outs[1][...] = jnp.zeros_like(outs[1])
+
+
+def first_odd(here, *refs):
+    tail, others, (from_prev, from_next), outs = refs[:6], refs[6:12], refs[12:14], refs[-3:]
+
+    @pl.when(is_tail())
+    def _():
+        first_sweep_at(here, tail, from_prev, from_next, *outs)
+
+    @pl.when((position() % 2 == ODD) & jnp.logical_not(is_tail()))
+    def _():
+        first_sweep_at(here, others, from_prev, from_next, *outs)
+
+    @pl.when(position() % 2 == EVEN)
+    def _():
+        outs[0][...] = outs[1][...] = jnp.zeros_like(outs[1])
+
+
+def second_odd(*refs):
+    tail, others, values, outs = refs[:4], refs[4:8], [refs[i] for i in (8, 9, 10, 12, 11)], refs[-3:]
+
+    @pl.when(is_tail())
+    def _():
+        second_sweep_at(tail, *values, *outs)
+
+    @pl.when((position() % 2 == ODD) & jnp.logical_not(is_tail()))
+    def _():
+        second_sweep_at(others, *values, *outs)
+
+    @pl.when(position() % 2 == EVEN)
+    def _():
+        outs[0][...] = jnp.zeros_like(outs[0])
+
+
+def second_even(*refs):
+    matrix, values, outs = refs[:4], refs[4:9], refs[-3:]
+
+    @pl.when(position() % 2 == EVEN)
+    def _():
+        second_sweep_at(matrix, *values, *outs)
+
+    @pl.when(position() % 2 == ODD)
+    def _():
+        outs[0][...] = jnp.zeros_like(outs[0])
 
 
 def finish_even(rest, factor, z_prev, out):
@@ -226,26 +286,57 @@
     out[...] = jnp.where(position() % 2 == ODD, odd, even[...])[: out.shape[0]]
 
 
+def move(block, route):
+    assert sorted(route.values()) == list(range(lax.axis_size("sfc")))
+    return lax.ppermute(block, "sfc", list(route.items()))
+
+
+def opening(block):
+    n, size = lax.axis_size("sfc"), plane_size()
+    path = [0, 1, size - 2, size - 3, size - 4, size - 1]
+    back = 2
+    if size == 32:
+        path = [0, 1, 8, 9, 16, 17, 24, 25, 26, 27, 30, 29, 28, 31]
+        back = 10
+    route = {i: i ^ 1 for i in range(n)}
+    for first in range(0, n, size):
+        for a, b in zip(path, path[1:]):
+            route[first + a] = first + b
+        route[first + size - 1] = first + size
+        route[first + back + 1] = first - size + back
+    route[n - 1], route[back + 1] = n - size + back, 0
+    return move(block, route)
+
+
+def inside(block):
+    n, size = lax.axis_size("sfc"), plane_size()
+    steps = [size - 1, size - 3, size - 4, 0]
+    if size == 32:
+        steps = [31, 29, 28, 27, 26, 25, 24, 17, 16, 9, 8, 0]
+    route = {i: i + 1 for i in range(n)}
+    for first in range(0, n, size):
+        for a, b in zip(steps[::2], steps[1::2]):
+            route[first + a] = first + b
+    return move(block, route)
+
+
 def to_next():
-    n = lax.axis_size("sfc")
-    plane = max(n // 8, 4)
-    stops = [i + 4 for i in range(0, n - 4, plane) if i + 4 < n - 2]
+    n, size = lax.axis_size("sfc"), plane_size()
+    stops = list(range(4, n, size))
     route = {i: i + 1 for i in range(n)}
     route.update(zip(stops + [n - 1], [0] + [i + 1 for i in stops]))
-    return list(route.items())
+    return route
 
 
 def forward(block):
-    return lax.ppermute(block, "sfc", to_next())
+    return move(block, to_next())
 
 
 def backward(block):
-    return lax.ppermute(block, "sfc", [(b, a) for a, b in to_next()])
-
-
-def odd_to_next(block):
-    n = lax.axis_size("sfc")
-    return lax.ppermute(block, "sfc", [(i, i + 1) for i in range(ODD, n - 1, 2)])
+    route = {b: a for a, b in to_next().items()}
+    for first in range(0, len(route), plane_size()):
+        route[first + 1], route[first + 3] = route[first + 3], route[first + 1]
+    return move(block, route)
 
 
 def swap(block):
@@ -300,33 +391,32 @@
         )(*args, *order)
         return in_vmem(weighted), in_vmem(turned), *others
 
-    *matrix_o, own_o, up_o = assembled_by(assemble_odd, assembled, "assemble_odd")
-    from_prev_e = odd_to_next(up_o)
-    *matrix_e, own_e, up_e, swapped = assembled_by(
-        assemble_even, assembled + assembled[4:5], "assemble_even", own_o, up_o
-    )
-    from_next_o = backward(own_e)
-    swapped = swap(swapped)
-    from_prev_e = call(pass_on, small, "pass_on", from_prev_e)
+    *tail, own_t, up_t = assembled_by(assemble_tail, assembled, "assemble_tail")
+    kept = opening(up_t)
+    *others, own, up, swapped = assembled_by(
+        assemble_others, assembled + assembled[4:5], "assemble_others", own_t, up_t
+    )
+    from_next_o = backward(own)
+    inner, swapped = inside(up), swap(swapped)
+    kept = call(keep_head, small, "keep_head", kept)
+    from_prev_e = call(keep_inner, small, "keep_inner", kept, inner)
     first = (small, small, jax.ShapeDtypeStruct((6, 8, size), f32))
     sweep_e = call(
-        functools.partial(first_sweep, here, EVEN), first, "first_even",
-        *matrix_e, own_e, up_e, from_prev_e, swapped,
+        functools.partial(first_even, here), first, "first_even",
+        *others, own, up, from_prev_e, swapped,
     )
     y_next_o, y_prev_o = backward(sweep_e[0]), swap(sweep_e[1])
     sweep_o = call(
-        functools.partial(first_sweep, here, ODD), first, "first_odd",
-        *matrix_o, own_o, up_o, swapped, from_next_o, sweep_e[1],
+        functools.partial(first_odd, here), first, "first_odd",
+        *tail, own_t, up_t, *others, own, up, swapped, from_next_o, sweep_e[1],
     )
     y_prev_e, y_next_e = forward(sweep_o[1]), swap(sweep_o[0])
     z_up_o, rest_o, factor_o = call(
-        functools.partial(second_sweep, ODD), (small,) * 3, "second_odd",
-        *matrix_o, *sweep_o, y_prev_o, y_next_o,
+        second_odd, (small,) * 3, "second_odd", *tail, *others, *sweep_o, y_next_o, y_prev_o
     )
     z_prev_e = forward(z_up_o)
     z_up_e, rest_e, factor_e = call(
-        functools.partial(second_sweep, EVEN), (small,) * 3, "second_even",
-        *matrix_e, *sweep_e, y_prev_e, y_next_e, z_up_o,
+        second_even, (small,) * 3, "second_even", *others, *sweep_e, y_prev_e, y_next_e, z_up_o
     )
     z_prev_o = swap(z_up_e)
     even = call(finish_even, small, "finish_even", rest_e, factor_e, z_prev_e)

time: 24.1 us -> 22.8 us (0.946)
  starting transfers between devices: 10.3 us -> 8.67 us
  waiting for transfers between devices: 7.55 us -> 7.89 us
    ppermute x5 -> x6, starting transfers between devices: 9.54 us -> 8.18 us  [move(): return lax.ppermute(block, 'sfc', list(route.items()))]
    ppermute x5 -> x6, waiting for transfers between devices: 7.16 us -> 7.5 us  [move(): return lax.ppermute(block, 'sfc', list(route.items()))]
    ppermute x4, starting transfers between devices: 0.78 us -> 0.49 us  [swap(): lax.ppermute(block, 'sfc', [(i, i ^ 1) for i in range(lax.axis_size('sfc'...]
    pallas_call x7 -> x8, Pallas kernels: 2.93 us -> 2.95 us  [call(): pl.pallas_call(kernel, out_shape=outs, in_specs=[VMEM] * len(operands), o...]
  transfers between devices with their start and end apart: 9 -> 10, of which waited for: 4 -> 5; matrix products, arithmetic and copies ran while one was open for 0% -> 0% of each run, Pallas kernels for 21% -> 23%
where the time goes in v4:
time: 22.8 us; the launch traced here: 22.4 us
  starting transfers between devices  8.67 us (38%)
  waiting for transfers between devices  7.89 us (35%)
  Pallas kernels  5.73 us (25%)
    ppermute x6, starting transfers between devices, move(): return lax.ppermute(block, 'sfc', list(route.items()))  8.18 us
    ppermute x6, waiting for transfers between devices, move(): return lax.ppermute(block, 'sfc', list(route.items()))  7.5 us
    pallas_call x8, Pallas kernels, call(): pl.pallas_call(kernel, out_shape=outs, in_specs=[VMEM] * len(operands), o...  2.95 us
    pallas_call x2, Pallas kernels, assembled_by(): pl.pallas_call(kernel, out_shape=outs, in_specs=[ANY] * 4 + [VMEM] * len(...  2.78 us
    ppermute x4, starting transfers between devices, swap(): lax.ppermute(block, 'sfc', [(i, i ^ 1) for i in range(lax.axis_size('sfc'...  0.49 us
  transfers between devices with their start and end apart: 10, of which 5 were waited for; matrix products, arithmetic and copies ran while one was open for 0% of the time, Pallas kernels for 23%

profile of v4, /device:TPU:128, one launch (start us, length us, event | category | flops | bytes accessed | tf_op | source)
XLA Modules:
  0.0 22.4 jit_solution(1052041548830824633)
XLA Ops:
  0.0 0.1 assemble_tail.1
  0.1 0.1 collective-permute-start
  0.2 2.7 %assemble_others.1 = (bf16[48,256,128]{2,1,0:T(8,128)(2,1)S(1)}, bf16[48,128,256]{2,1,0:T(8,128)(2,1)S(1)}, f32[2,16,128]{2,1,0:T(8,128)S(1)}, f32[128,128]{1,0:...) custom-call(bf16[48,256,128]{2,1,0:T(8,128)(2,1)} %bitcast.3, s32[2,48]{1,0:T(2,128)} %bitcast.5, ...), custom_call_target="tpu_custom_call" | custom-call | flops 10000000000 | bytes 100000000 | tf_op jit(solution)/shard_map/assemble_others/pallas_call | solution.py:382
  2.9 1.7 %collective-permute-start.1 = (f32[8,128]{1,0:T(8,128)S(1)}, f32[8,128]{1,0:T(8,128)S(1)}, u32[]{:S(2)}, u32[]{:S(2)}) collective-permute-start(f32[8,128]{1,0:T(8,128)S(1)} %get-tuple-element.37.refs_5_.refs_11_), channel_id=1, source_target_pairs={{0,1},{1,2},{2,3},{3,4},{4,5},{5,6},{6,7},{7,8},{8,0},{9,10},{10,1... | collective-permute-start | bytes 12296 | tf_op jit(solution)/shard_map/ppermute | solution.py:291
  4.6 0.1 collective-permute-start.2
  4.7 3.6 %collective-permute-start.3 = (f32[16,128]{1,0:T(8,128)S(1)}, f32[16,128]{1,0:T(8,128)S(1)}, u32[]{:S(2)}, u32[]{:S(2)}) collective-permute-start(f32[16,128]{1,0:T(8,128)S(1)} %get-tuple-element.36.refs_4_.refs_10_), channel_id=1, source_target_pairs={{1,2},{2,1},{3,0},{4,3},{0,4},{6,5},{7,6},{8,7},{9,8},{10,9},{11,1... | collective-permute-start | bytes 24584 | tf_op jit(solution)/shard_map/ppermute | solution.py:291
  8.3 0.3 %collective-permute-done.block = f32[8,128]{1,0:T(8,128)S(1)} collective-permute-done((f32[8,128]{1,0:T(8,128)S(1)}, f32[8,128]{1,0:T(8,128)S(1)}, u32[]{:S(2)}, u32[]{:S(2)}) %collective-permute-start) | collective-permute-done | bytes 4128 | tf_op jit(solution)/shard_map/ppermute | solution.py:291
  8.6 0.0 collective-permute-done.1.block
  8.6 0.0 collective-permute-done.2.refs_7_.refs_12_
  8.7 1.2 %first_even.1 = (f32[8,128]{1,0:T(8,128)S(1)}, f32[8,128]{1,0:T(8,128)S(1)}, f32[6,8,128]{2,1,0:T(8,128)S(1)}) custom-call(bf16[48,256,128]{2,1,0:T(8,128)(2,1)S(1)} %get-tuple-element.32.refs_0_.refs_6_.refs_4_, bf16[48,128,256]{2,1,0:T(8,128)(2,1)S(1)} %get-tuple-element.33.refs_1_.refs_7_.refs_5_, ...), custom_call_target="tpu_custom_call" | custom-call | flops 10000000000 | bytes 100000000 | tf_op jit(solution)/shard_map/first_even/pallas_call | solution.py:370
  9.8 0.3 %collective-permute-start.6 = (f32[8,128]{1,0:T(8,128)S(1)}, f32[8,128]{1,0:T(8,128)S(1)}, u32[]{:S(2)}, u32[]{:S(2)}) collective-permute-start(f32[8,128]{1,0:T(8,128)S(1)} %get-tuple-element.39.refs_4_), channel_id=1, source_target_pairs={{1,2},{2,1},{3,0},{4,3},{0,4},{6,5},{7,6},{8,7},{9,8},{10,9},{11,1... | collective-permute-start | bytes 12296 | tf_op jit(solution)/shard_map/ppermute | solution.py:291
  10.1 0.0 collective-permute-start.7
  10.1 0.0 collective-permute-done.3.refs_13_
  10.1 1.7 %collective-permute-start.4 = (f32[8,128]{1,0:T(8,128)S(1)}, f32[8,128]{1,0:T(8,128)S(1)}, u32[]{:S(2)}, u32[]{:S(2)}) collective-permute-start(f32[8,128]{1,0:T(8,128)S(1)} %get-tuple-element.46.refs_9_), channel_id=1, source_target_pairs={{0,1},{1,2},{2,3},{3,4},{4,0},{5,6},{6,7},{7,8},{8,9},{9,10},{10,1... | collective-permute-start | bytes 12296 | tf_op jit(solution)/shard_map/ppermute | solution.py:291
  11.8 0.3 %collective-permute-start.5 = (f32[8,128]{1,0:T(8,128)S(1)}, f32[8,128]{1,0:T(8,128)S(1)}, u32[]{:S(2)}, u32[]{:S(2)}) collective-permute-start(f32[8,128]{1,0:T(8,128)S(1)} %get-tuple-element.47.refs_8_), channel_id=1, source_target_pairs={{0,1},{1,0},{2,3},{3,2},{4,5},{5,4},{6,7},{7,6},{8,9},{9,8},{10,11... | collective-permute-start | bytes 12296 | tf_op jit(solution)/shard_map/ppermute | solution.py:343
  12.1 0.8 %collective-permute-done.6.refs_11_ = f32[8,128]{1,0:T(8,128)S(1)} collective-permute-done((f32[8,128]{1,0:T(8,128)S(1)}, f32[8,128]{1,0:T(8,128)S(1)}, u32[]{:S(2)}, u32[]{:S(2)}) %collective-permute-start.6) | collective-permute-done | bytes 4128 | tf_op jit(solution)/shard_map/ppermute | solution.py:291
  12.9 0.0 collective-permute-done.7.refs_12_
  12.9 0.8 %collective-permute-start.8 = (f32[8,128]{1,0:T(8,128)S(1)}, f32[8,128]{1,0:T(8,128)S(1)}, u32[]{:S(2)}, u32[]{:S(2)}) collective-permute-start(f32[8,128]{1,0:T(8,128)S(1)} %get-tuple-element.49.refs_9_), channel_id=1, source_target_pairs={{0,1},{1,2},{2,3},{3,4},{4,0},{5,6},{6,7},{7,8},{8,9},{9,10},{10,1... | collective-permute-start | bytes 12296 | tf_op jit(solution)/shard_map/ppermute | solution.py:291
  13.7 5.7 %collective-permute-done.4.refs_7_ = f32[8,128]{1,0:T(8,128)S(1)} collective-permute-done((f32[8,128]{1,0:T(8,128)S(1)}, f32[8,128]{1,0:T(8,128)S(1)}, u32[]{:S(2)}, u32[]{:S(2)}) %collective-permute-start.4) | collective-permute-done | bytes 4128 | tf_op jit(solution)/shard_map/ppermute | solution.py:291
  19.3 0.0 collective-permute-done.5.refs_8_
  19.3 1.2 %second_even.1 = (f32[8,128]{1,0:T(8,128)S(1)}, f32[8,128]{1,0:T(8,128)S(1)}, f32[8,128]{1,0:T(8,128)S(1)}) custom-call(bf16[48,256,128]{2,1,0:T(8,128)(2,1)S(1)} %get-tuple-element.32.refs_0_.refs_6_.refs_4_, bf16[48,128,256]{2,1,0:T(8,128)(2,1)S(1)} %get-tuple-element.33.refs_1_.refs_7_.refs_5_, ...), custom_call_target="tpu_custom_call" | custom-call | flops 10000000000 | bytes 100000000 | tf_op jit(solution)/shard_map/second_even/pallas_call | solution.py:370
  20.5 0.1 collective-permute-start.9
  20.6 0.8 %collective-permute-done.8.z_prev = f32[8,128]{1,0:T(8,128)S(1)} collective-permute-done((f32[8,128]{1,0:T(8,128)S(1)}, f32[8,128]{1,0:T(8,128)S(1)}, u32[]{:S(2)}, u32[]{:S(2)}) %collective-permute-start.8) | collective-permute-done | bytes 4128 | tf_op jit(solution)/shard_map/ppermute | solution.py:291
  21.4 0.4 %collective-permute-done.9.z_prev = f32[8,128]{1,0:T(8,128)S(1)} collective-permute-done((f32[8,128]{1,0:T(8,128)S(1)}, f32[8,128]{1,0:T(8,128)S(1)}, u32[]{:S(2)}, u32[]{:S(2)}) %collective-permute-start.9) | collective-permute-done | bytes 4128 | tf_op jit(solution)/shard_map/ppermute | solution.py:343
  21.8 0.6 %finish.1 = f32[6,128]{1,0:T(8,128)} custom-call(f32[8,128]{1,0:T(8,128)S(1)} %finish_even.1.even, f32[8,128]{1,0:T(8,128)S(1)} %get-tuple-element.52.rest, f32[8,128]{1,0:T(8,128)S(1)} %get-tuple-element.53.factor, f32[8,128]{1,0:T(8,128)S(1)} %collective-permute-done.9.z_prev), custom_call_target="tpu_custom_call" | custom-call | flops 10000000000 | bytes 100000000 | tf_op jit(solution)/shard_map/finish/pallas_call | solution.py:370
  (5 shorter events, 0.0 us)
Async XLA Ops:
  0.1 8.5 %collective-permute-start = (f32[8,128]{1,0:T(8,128)S(1)}, f32[8,128]{1,0:T(8,128)S(1)}, u32[]{:S(2)}, u32[]{:S(2)}) collective-permute-start(f32[8,128]{1,0:T(8,128)S(1)} %get-tuple-element.31.tail_up.refs_5_), channel_id=1, source_target_pairs={{0,1},{1,8},{2,3},{3,2},{4,5},{5,4},{6,7},{7,6},{8,9},{9,16},{10,1... | collective-permute-start | bytes 12296 | tf_op jit(solution)/shard_map/ppermute | solution.py:291
  2.9 5.7 %collective-permute-start.1 = (f32[8,128]{1,0:T(8,128)S(1)}, f32[8,128]{1,0:T(8,128)S(1)}, u32[]{:S(2)}, u32[]{:S(2)}) collective-permute-start(f32[8,128]{1,0:T(8,128)S(1)} %get-tuple-element.37.refs_5_.refs_11_), channel_id=1, source_target_pairs={{0,1},{1,2},{2,3},{3,4},{4,5},{5,6},{6,7},{7,8},{8,0},{9,10},{10,1... | collective-permute-start | bytes 12296 | tf_op jit(solution)/shard_map/ppermute | solution.py:291
  4.6 4.0 %collective-permute-start.2 = (f32[16,128]{1,0:T(8,128)S(1)}, f32[16,128]{1,0:T(8,128)S(1)}, u32[]{:S(2)}, u32[]{:S(2)}) collective-permute-start(f32[16,128]{1,0:T(8,128)S(1)} %get-tuple-element.38), channel_id=1, source_target_pairs={{0,1},{1,0},{2,3},{3,2},{4,5},{5,4},{6,7},{7,6},{8,9},{9,8},{10,11... | collective-permute-start | bytes 24584 | tf_op jit(solution)/shard_map/ppermute | solution.py:343
  4.7 5.4 %collective-permute-start.3 = (f32[16,128]{1,0:T(8,128)S(1)}, f32[16,128]{1,0:T(8,128)S(1)}, u32[]{:S(2)}, u32[]{:S(2)}) collective-permute-start(f32[16,128]{1,0:T(8,128)S(1)} %get-tuple-element.36.refs_4_.refs_10_), channel_id=1, source_target_pairs={{1,2},{2,1},{3,0},{4,3},{0,4},{6,5},{7,6},{8,7},{9,8},{10,9},{11,1... | collective-permute-start | bytes 24584 | tf_op jit(solution)/shard_map/ppermute | solution.py:291
  9.8 3.1 %collective-permute-start.6 = (f32[8,128]{1,0:T(8,128)S(1)}, f32[8,128]{1,0:T(8,128)S(1)}, u32[]{:S(2)}, u32[]{:S(2)}) collective-permute-start(f32[8,128]{1,0:T(8,128)S(1)} %get-tuple-element.39.refs_4_), channel_id=1, source_target_pairs={{1,2},{2,1},{3,0},{4,3},{0,4},{6,5},{7,6},{8,7},{9,8},{10,9},{11,1... | collective-permute-start | bytes 12296 | tf_op jit(solution)/shard_map/ppermute | solution.py:291
  10.1 2.8 %collective-permute-start.7 = (f32[8,128]{1,0:T(8,128)S(1)}, f32[8,128]{1,0:T(8,128)S(1)}, u32[]{:S(2)}, u32[]{:S(2)}) collective-permute-start(f32[8,128]{1,0:T(8,128)S(1)} %get-tuple-element.40.refs_14_.refs_5_), channel_id=1, source_target_pairs={{0,1},{1,0},{2,3},{3,2},{4,5},{5,4},{6,7},{7,6},{8,9},{9,8},{10,11... | collective-permute-start | bytes 12296 | tf_op jit(solution)/shard_map/ppermute | solution.py:343
  10.1 9.2 %collective-permute-start.4 = (f32[8,128]{1,0:T(8,128)S(1)}, f32[8,128]{1,0:T(8,128)S(1)}, u32[]{:S(2)}, u32[]{:S(2)}) collective-permute-start(f32[8,128]{1,0:T(8,128)S(1)} %get-tuple-element.46.refs_9_), channel_id=1, source_target_pairs={{0,1},{1,2},{2,3},{3,4},{4,0},{5,6},{6,7},{7,8},{8,9},{9,10},{10,1... | collective-permute-start | bytes 12296 | tf_op jit(solution)/shard_map/ppermute | solution.py:291
  11.8 7.5 %collective-permute-start.5 = (f32[8,128]{1,0:T(8,128)S(1)}, f32[8,128]{1,0:T(8,128)S(1)}, u32[]{:S(2)}, u32[]{:S(2)}) collective-permute-start(f32[8,128]{1,0:T(8,128)S(1)} %get-tuple-element.47.refs_8_), channel_id=1, source_target_pairs={{0,1},{1,0},{2,3},{3,2},{4,5},{5,4},{6,7},{7,6},{8,9},{9,8},{10,11... | collective-permute-start | bytes 12296 | tf_op jit(solution)/shard_map/ppermute | solution.py:343
  12.9 8.5 %collective-permute-start.8 = (f32[8,128]{1,0:T(8,128)S(1)}, f32[8,128]{1,0:T(8,128)S(1)}, u32[]{:S(2)}, u32[]{:S(2)}) collective-permute-start(f32[8,128]{1,0:T(8,128)S(1)} %get-tuple-element.49.refs_9_), channel_id=1, source_target_pairs={{0,1},{1,2},{2,3},{3,4},{4,0},{5,6},{6,7},{7,8},{8,9},{9,10},{10,1... | collective-permute-start | bytes 12296 | tf_op jit(solution)/shard_map/ppermute | solution.py:291
  20.5 1.3 %collective-permute-start.9 = (f32[8,128]{1,0:T(8,128)S(1)}, f32[8,128]{1,0:T(8,128)S(1)}, u32[]{:S(2)}, u32[]{:S(2)}) collective-permute-start(f32[8,128]{1,0:T(8,128)S(1)} %get-tuple-element.54), channel_id=1, source_target_pairs={{0,1},{1,0},{2,3},{3,2},{4,5},{5,4},{6,7},{7,6},{8,9},{9,8},{10,11... | collective-permute-start | bytes 12296 | tf_op jit(solution)/shard_map/ppermute | solution.py:343

commit v5 on v4

--- a/solution.py
+++ b/solution.py
@@ -14,6 +14,7 @@
 GROUP = 8
 ODD, EVEN = 1, 0
 cost = pl.CostEstimate(flops=10**10, bytes_accessed=10**8, transcendentals=0)
+quick = pl.CostEstimate(flops=0, bytes_accessed=0, transcendentals=0)
 VMEM = pl.BlockSpec(memory_space=pltpu.VMEM)
 ANY = pl.BlockSpec(memory_space=pl.ANY)
 params = pltpu.CompilerParams(vmem_limit_bytes=32 * 1024 * 1024)
@@ -114,6 +115,55 @@
     up[...] = total[8:]
 
 
+def join(here, couples, weighted, joint, total):
+    size = weighted.shape[2]
+    total[...] = jnp.zeros_like(total)
+    first = position() * here
+    for v in range(weighted.shape[0]):
+        k = jnp.where(couples[0, v] - first == v % here, 0, 1)
+        slot = couples[1 - k, v] - first - here
+        slot = jnp.where(slot >= 0, slot, here)
+        mine = weighted[v, pl.ds(pl.multiple_of(k * size, size), size), :]
+        other = weighted[v, pl.ds(pl.multiple_of((1 - k) * size, size), size), :]
+        both = lax.dot_general(
+            jnp.concatenate([mine, other], axis=0), other, (((1,), (1,)), ((), ())),
+            preferred_element_type=f32,
+        )
+        total[v % here, slot] += both[:size]
+        total[here, slot] += both[size:]
+    for row in range(here + 1):
+        for column in range(here):
+            block = total[row, column]
+            high = block.astype(bf16)
+            place = pl.ds(row * size, size), pl.ds(column * size, size)
+            joint[0, *place] = high
+            joint[1, *place] = (block - high.astype(f32)).astype(bf16)
+
+
+def across(here, joint, mine, following):
+    size = mine.shape[1]
+
+    def wide(values):
+        both = parts(values)
+        return [
+            jnp.concatenate([jnp.broadcast_to(x[r : r + 1], (8, size)) for x in both], axis=0)
+            for r in range(here)
+        ]
+
+    left = jnp.concatenate(wide(mine), axis=1).astype(bf16)
+    total = jnp.dot(left, joint[0, : here * size], preferred_element_type=f32)
+    total = total + jnp.dot(left, joint[1, : here * size], preferred_element_type=f32)
+    sub = lax.broadcasted_iota(jnp.int32, (8, size), 0)
+    result = jnp.zeros((8, size), f32)
+    for r, left in enumerate(wide(following)):
+        block = total[:, r * size : (r + 1) * size]
+        for part in range(2):
+            right = joint[part, here * size :, r * size : (r + 1) * size]
+            block = block + jnp.dot(left.astype(bf16), right, preferred_element_type=f32)
+        result = jnp.where(sub == r, block[:8] + block[8:], result)
+    return result
+
+
 def assemble_tail(tiles, couples, mobility, rhs, weighted, turned, place, pick, own, up, *scratch):
     @pl.when(is_tail())
     def _():
@@ -127,7 +177,14 @@
 
 
 def assemble_others(tiles, couples, mobility, rhs, tail_own, tail_up,
-                    weighted, turned, place, pick, own, up, swapped, *scratch):
+                    weighted, turned, place, pick, own, up, swapped, joint, *scratch):
+    *scratch, total, slots, sem = scratch
+    copy = pltpu.make_async_copy(couples, slots, sem)
+
+    @pl.when(is_head())
+    def _():
+        copy.start()
+
     @pl.when(jnp.logical_not(is_tail()))
     def _():
         assemble_here(
@@ -136,6 +193,11 @@
         odd = position() % 2 == ODD
         swapped[:8, :] = jnp.where(odd, own[:8, :], up[...])
         swapped[8:, :] = own[8:, :]
+
+    @pl.when(is_head())
+    def _():
+        copy.wait()
+        join(rhs.shape[0], slots, weighted, joint, total)
 
     @pl.when(is_tail())
     def _():
@@ -211,11 +273,15 @@
         state[i] = now[i]
 
 
-def second_sweep_at(matrix, y_own, y_up, state, y_prev, y_next, z_up, rest, factor):
+def second_values(y_own, y_up, state, y_prev, y_next):
     scale, target, p, scale_next, target_next, p_next = [state[i] for i in range(6)]
     p = p + scale * (target - (y_own[...] + y_prev[...]))
     p_next = p_next + scale_next * (target_next - (y_next[...] + y_up[...]))
-    p_next = jnp.where(is_last(), 0.0, p_next)
+    return p, jnp.where(is_last(), 0.0, p_next), scale, target
+
+
+def second_sweep_at(matrix, values, z_up, rest, factor):
+    p, p_next, scale, target = second_values(*values)
     z_own, z_up[...] = multiply(*matrix, p, p_next)
     rest[...] = p + scale * (target - z_own)
     factor[...] = scale
@@ -254,36 +320,69 @@
 
     @pl.when(is_tail())
     def _():
-        second_sweep_at(tail, *values, *outs)
+        second_sweep_at(tail, values, *outs)
 
     @pl.when((position() % 2 == ODD) & jnp.logical_not(is_tail()))
     def _():
-        second_sweep_at(others, *values, *outs)
+        second_sweep_at(others, values, *outs)
 
     @pl.when(position() % 2 == EVEN)
     def _():
         outs[0][...] = jnp.zeros_like(outs[0])
 
 
-def second_even(*refs):
-    matrix, values, outs = refs[:4], refs[4:9], refs[-3:]
-
+def second_even(here, *refs):
+    matrix, values, joint, outs = refs[:4], refs[4:9], refs[9], refs[-5:]
+    z_up, rest, factor, values_own, values_next = outs
+
+    @pl.when(is_head())
+    def _():
+        p, p_next, scale, target = second_values(*values)
+        z_up[...] = across(here, joint, p, p_next)
+        rest[...] = p + scale * target
+        factor[...] = scale
+        values_own[...] = p
+        values_next[...] = p_next
+
+    @pl.when((position() % 2 == EVEN) & jnp.logical_not(is_head()))
+    def _():
+        second_sweep_at(matrix, values, z_up, rest, factor)
+
+    @pl.when(position() % 2 == ODD)
+    def _():
+        z_up[...] = jnp.zeros_like(z_up)
+
+
+def second_late(*refs):
+    matrix, (rest, factor, values_own, values_next, out) = refs[:4], refs[4:]
+
+    @pl.when(is_head())
+    def _():
+        z_own = multiply(*matrix, values_own[...], values_next[...])[0]
+        out[...] = rest[...] - factor[...] * z_own
+
+    @pl.when(jnp.logical_not(is_head()))
+    def _():
+        out[...] = rest[...]
+
+
+def finish_even(rest, factor, z_prev, out, local, sem):
     @pl.when(position() % 2 == EVEN)
     def _():
-        second_sweep_at(matrix, *values, *outs)
-
+        finish_here(rest, factor, z_prev, out, local, sem)
+
+
+def finish_odd(even, rest, factor, z_prev, out, local, sem):
     @pl.when(position() % 2 == ODD)
     def _():
-        outs[0][...] = jnp.zeros_like(outs[0])
-
-
-def finish_even(rest, factor, z_prev, out):
-    out[...] = rest[...] - factor[...] * z_prev[...]
-
-
-def finish(even, rest, factor, z_prev, out):
-    odd = rest[...] - factor[...] * z_prev[...]
-    out[...] = jnp.where(position() % 2 == ODD, odd, even[...])[: out.shape[0]]
+        finish_here(rest, factor, z_prev, out, local, sem)
+
+
+def finish_here(rest, factor, z_prev, out, local, sem):
+    local[...] = (rest[...] - factor[...] * z_prev[...])[: local.shape[0]]
+    copy = pltpu.make_async_copy(local, out, sem)
+    copy.start()
+    copy.wait()
 
 
 def move(block, route):
@@ -366,7 +465,7 @@
         pltpu.SemaphoreType.DMA((CHUNKS + 3,)),
     ]
 
-    def call(kernel, outs, name, *operands, **more):
+    def call(kernel, outs, name, *operands, cost=cost):
         return pl.pallas_call(
             kernel,
             out_shape=outs,
@@ -375,16 +474,15 @@
             compiler_params=params,
             cost_estimate=cost,
             name=name,
-            **more,
         )(*operands)
 
-    def assembled_by(kernel, outs, name, *order):
+    def assembled_by(kernel, outs, name, *order, more=()):
         weighted, turned, *others = pl.pallas_call(
             kernel,
             out_shape=outs,
             in_specs=[ANY] * 4 + [VMEM] * len(order),
             out_specs=(VMEM,) * len(outs),
-            scratch_shapes=scratch,
+            scratch_shapes=scratch + list(more),
             compiler_params=params,
             cost_estimate=cost,
             name=name,
@@ -393,9 +491,16 @@
 
     *tail, own_t, up_t = assembled_by(assemble_tail, assembled, "assemble_tail")
     kept = opening(up_t)
-    *others, own, up, swapped = assembled_by(
-        assemble_others, assembled + assembled[4:5], "assemble_others", own_t, up_t
-    )
+    joined = pltpu.VMEM((2, (here + 1) * size, here * size), bf16)
+    more = (
+        pltpu.VMEM((here + 1, here + 1, size, size), f32),
+        pltpu.SMEM((pairs, count), jnp.int32),
+        pltpu.SemaphoreType.DMA,
+    )
+    *others, own, up, swapped, joint = assembled_by(
+        assemble_others, assembled + (assembled[4], joined), "assemble_others", own_t, up_t, more=more
+    )
+    joint = in_vmem(joint)
     from_next_o = backward(own)
     inner, swapped = inside(up), swap(swapped)
     kept = call(keep_head, small, "keep_head", kept)
@@ -415,13 +520,26 @@
         second_odd, (small,) * 3, "second_odd", *tail, *others, *sweep_o, y_next_o, y_prev_o
     )
     z_prev_e = forward(z_up_o)
-    z_up_e, rest_e, factor_e = call(
-        second_even, (small,) * 3, "second_even", *others, *sweep_e, y_prev_e, y_next_e, z_up_o
+    z_up_e, rest_e, factor_e, *values_e = call(
+        functools.partial(second_even, here), (small,) * 5, "second_even",
+        *others, *sweep_e, y_prev_e, y_next_e, joint, z_up_o, cost=quick,
     )
     z_prev_o = swap(z_up_e)
-    even = call(finish_even, small, "finish_even", rest_e, factor_e, z_prev_e)
-    outs = jax.ShapeDtypeStruct(rhs.shape, f32)
-    return call(finish, outs, "finish", even, rest_o, factor_o, z_prev_o)
+    rest_e = call(
+        second_late, small, "second_late", *others, rest_e, factor_e, *values_e, cost=quick
+    )
+    last = dict(
+        out_shape=jax.ShapeDtypeStruct(rhs.shape, f32),
+        out_specs=ANY,
+        scratch_shapes=[pltpu.VMEM(rhs.shape, f32), pltpu.SemaphoreType.DMA],
+        compiler_params=params,
+    )
+    even = pl.pallas_call(
+        finish_even, in_specs=[VMEM] * 3, cost_estimate=quick, name="finish_even", **last
+    )(rest_e, factor_e, z_prev_e)
+    return pl.pallas_call(
+        finish_odd, in_specs=[ANY] + [VMEM] * 3, input_output_aliases={0: 0}, name="finish_odd", **last
+    )(even, rest_o, factor_o, z_prev_o)
 
 
 def solution(mesh):

time: 22.8 us -> 22.5 us (0.987)
  Pallas kernels: 5.73 us -> 7.92 us
  starting transfers between devices: 8.67 us -> 7.12 us
  waiting for transfers between devices: 7.89 us -> 6.87 us
    pallas_call x2, Pallas kernels: 2.78 us -> 4.44 us  [assembled_by(): pl.pallas_call(kernel, out_shape=outs, in_specs=[ANY] * 4 + [VMEM] * len(...]
    ppermute x6, starting transfers between devices: 8.18 us -> 6.81 us  [move(): return lax.ppermute(block, 'sfc', list(route.items()))]
    ppermute x6, waiting for transfers between devices: 7.5 us -> 6.86 us  [move(): return lax.ppermute(block, 'sfc', list(route.items()))]
    pallas_call x0 -> x2, Pallas kernels: none -> 0.62 us  [the longest x1 0.59 us: shards(): pl.pallas_call(finish_even, in_specs=[VMEM] * 3, cost_estimate=quick, nam...]
    ppermute x4, waiting for transfers between devices: 0.39 us -> 0.01 us  [swap(): lax.ppermute(block, 'sfc', [(i, i ^ 1) for i in range(lax.axis_size('sfc'...]
    pallas_call x8 -> x7, Pallas kernels: 2.95 us -> 2.86 us  [call(): pl.pallas_call(kernel, out_shape=outs, in_specs=[VMEM] * len(operands), o...]
  transfers between devices with their start and end apart: 10 -> 10, of which waited for: 5 -> 3; matrix products, arithmetic and copies ran while one was open for 0% -> 0% of each run, Pallas kernels for 23% -> 35%
where the time goes in v5:
time: 22.5 us; the launch traced here: 22.2 us
  Pallas kernels  7.92 us (35%)
  starting transfers between devices  7.12 us (32%)
  waiting for transfers between devices  6.87 us (31%)
  between operations  0.26 us (1%)
    ppermute x6, waiting for transfers between devices, move(): return lax.ppermute(block, 'sfc', list(route.items()))  6.86 us
    ppermute x6, starting transfers between devices, move(): return lax.ppermute(block, 'sfc', list(route.items()))  6.81 us
    pallas_call x2, Pallas kernels, assembled_by(): pl.pallas_call(kernel, out_shape=outs, in_specs=[ANY] * 4 + [VMEM] * len(...  4.44 us
    pallas_call x7, Pallas kernels, call(): pl.pallas_call(kernel, out_shape=outs, in_specs=[VMEM] * len(operands), o...  2.86 us
    pallas_call x1, Pallas kernels, shards(): pl.pallas_call(finish_even, in_specs=[VMEM] * 3, cost_estimate=quick, nam...  0.59 us
  transfers between devices with their start and end apart: 10, of which 3 were waited for; matrix products, arithmetic and copies ran while one was open for 0% of the time, Pallas kernels for 35%

profile of v5, /device:TPU:128, one launch (start us, length us, event | category | flops | bytes accessed | tf_op | source)
XLA Modules:
  0.0 22.2 jit_solution(12963789814750112246)
XLA Ops:
  0.0 0.1 assemble_tail.1
  0.1 0.1 collective-permute-start
  0.2 4.4 %assemble_others.1 = (bf16[48,256,128]{2,1,0:T(8,128)(2,1)S(1)}, bf16[48,128,256]{2,1,0:T(8,128)(2,1)S(1)}, f32[2,16,128]{2,1,0:T(8,128)S(1)}, f32[128,128]{1,0:...) custom-call(bf16[48,256,128]{2,1,0:T(8,128)(2,1)} %bitcast.3, ...), custom_call_target="tpu_custom_call" | custom-call | flops 10000000000 | bytes 100000000 | tf_op jit(solution)/shard_map/assemble_others/pallas_call | solution.py:480
  4.5 0.1 collective-permute-start.1
  4.6 0.1 collective-permute-start.2
  4.7 3.6 %collective-permute-start.3 = (f32[16,128]{1,0:T(8,128)S(1)}, f32[16,128]{1,0:T(8,128)S(1)}, u32[]{:S(2)}, u32[]{:S(2)}) collective-permute-start(f32[16,128]{1,0:T(8,128)S(1)} %get-tuple-element.39.refs_4_.refs_10_), channel_id=1, source_target_pairs={{1,2},{2,1},{3,0},{4,3},{0,4},{6,5},{7,6},{8,7},{9,8},{10,9},{11,1... | collective-permute-start | bytes 24584 | tf_op jit(solution)/shard_map/ppermute | solution.py:390
  8.4 0.3 %collective-permute-done.block = f32[8,128]{1,0:T(8,128)S(1)} collective-permute-done((f32[8,128]{1,0:T(8,128)S(1)}, f32[8,128]{1,0:T(8,128)S(1)}, u32[]{:S(2)}, u32[]{:S(2)}) %collective-permute-start) | collective-permute-done | bytes 4128 | tf_op jit(solution)/shard_map/ppermute | solution.py:390
  8.6 0.0 collective-permute-done.1.block
  8.6 0.0 collective-permute-done.2.refs_7_.refs_12_
  8.7 1.2 %first_even.1 = (f32[8,128]{1,0:T(8,128)S(1)}, f32[8,128]{1,0:T(8,128)S(1)}, f32[6,8,128]{2,1,0:T(8,128)S(1)}) custom-call(bf16[48,256,128]{2,1,0:T(8,128)(2,1)S(1)} %get-tuple-element.35.refs_0_.refs_6_.refs_4_, bf16[48,128,256]{2,1,0:T(8,128)(2,1)S(1)} %get-tuple-element.36.refs_1_.refs_7_.refs_5_, ...), custom_call_target="tpu_custom_call" | custom-call | flops 10000000000 | bytes 100000000 | tf_op jit(solution)/shard_map/first_even/pallas_call | solution.py:469
  9.8 0.3 %collective-permute-start.6 = (f32[8,128]{1,0:T(8,128)S(1)}, f32[8,128]{1,0:T(8,128)S(1)}, u32[]{:S(2)}, u32[]{:S(2)}) collective-permute-start(f32[8,128]{1,0:T(8,128)S(1)} %get-tuple-element.42.refs_4_), channel_id=1, source_target_pairs={{1,2},{2,1},{3,0},{4,3},{0,4},{6,5},{7,6},{8,7},{9,8},{10,9},{11,1... | collective-permute-start | bytes 12296 | tf_op jit(solution)/shard_map/ppermute | solution.py:390
  10.1 0.0 collective-permute-start.7
  10.1 0.0 collective-permute-done.3.refs_13_
  10.1 1.9 %collective-permute-start.4 = (f32[8,128]{1,0:T(8,128)S(1)}, f32[8,128]{1,0:T(8,128)S(1)}, u32[]{:S(2)}, u32[]{:S(2)}) collective-permute-start(f32[8,128]{1,0:T(8,128)S(1)} %get-tuple-element.49.refs_9_), channel_id=1, source_target_pairs={{0,1},{1,2},{2,3},{3,4},{4,0},{5,6},{6,7},{7,8},{8,9},{9,10},{10,1... | collective-permute-start | bytes 12296 | tf_op jit(solution)/shard_map/ppermute | solution.py:390
  12.0 0.1 collective-permute-start.5
  12.1 0.8 %collective-permute-done.6.refs_11_ = f32[8,128]{1,0:T(8,128)S(1)} collective-permute-done((f32[8,128]{1,0:T(8,128)S(1)}, f32[8,128]{1,0:T(8,128)S(1)}, u32[]{:S(2)}, u32[]{:S(2)}) %collective-permute-start.6) | collective-permute-done | bytes 4128 | tf_op jit(solution)/shard_map/ppermute | solution.py:390
  12.9 0.0 collective-permute-done.7.refs_12_
  12.9 0.9 %collective-permute-start.8 = (f32[8,128]{1,0:T(8,128)S(1)}, f32[8,128]{1,0:T(8,128)S(1)}, u32[]{:S(2)}, u32[]{:S(2)}) collective-permute-start(f32[8,128]{1,0:T(8,128)S(1)} %get-tuple-element.53.refs_10_), channel_id=1, source_target_pairs={{0,1},{1,2},{2,3},{3,4},{4,0},{5,6},{6,7},{7,8},{8,9},{9,10},{10,1... | collective-permute-start | bytes 12296 | tf_op jit(solution)/shard_map/ppermute | solution.py:390
  13.8 5.8 %collective-permute-done.4.refs_7_ = f32[8,128]{1,0:T(8,128)S(1)} collective-permute-done((f32[8,128]{1,0:T(8,128)S(1)}, f32[8,128]{1,0:T(8,128)S(1)}, u32[]{:S(2)}, u32[]{:S(2)}) %collective-permute-start.4) | collective-permute-done | bytes 4128 | tf_op jit(solution)/shard_map/ppermute | solution.py:390
  19.5 0.0 collective-permute-done.5.refs_8_
  19.5 0.5 %second_even.1 = (f32[8,128]{1,0:T(8,128)S(1)}, f32[8,128]{1,0:T(8,128)S(1)}, f32[8,128]{1,0:T(8,128)S(1)}, f32[8,128]{1,0:T(8,128)S(1)}, f32[8,128]{1,0:T(8,128)S(1)}) custom-call(bf16[48,256,128]{2,1,0:T(8,128)(2,1)S(1)} %get-tuple-element.35.refs_0_.refs_6_.refs_4_, bf16[48,128,256]{2,1,0:T(8,128)(2,1)S(1)} %get-tuple-element.36.refs_1_.refs_7_.refs_5_, ...), custom_call_target="tpu_custom_call" | custom-call | tf_op jit(solution)/shard_map/second_even/pallas_call | solution.py:469
  20.1 0.1 collective-permute-start.9
  20.2 1.2 %second_late.1.rest = f32[8,128]{1,0:T(8,128)S(1)} custom-call(bf16[48,256,128]{2,1,0:T(8,128)(2,1)S(1)} %get-tuple-element.35.refs_0_.refs_6_.refs_4_, bf16[48,128,256]{2,1,0:T(8,128)(2,1)S(1)} %get-tuple-element.36.refs_1_.refs_7_.refs_5_, f32[2,16,128]{2,1,0:T(8,128)S(1)} %get-tuple-element.37.refs_2_.refs_8_.refs_6_, ...), custom_call_target="tpu_custom_call" | custom-call | tf_op jit(solution)/shard_map/second_late/pallas_call | solution.py:469
  21.3 0.0 collective-permute-done.8.z_prev
  21.4 0.6 %finish_even.1.even = f32[6,128]{1,0:T(8,128)} custom-call(f32[8,128]{1,0:T(8,128)S(1)} %second_late.1.rest, f32[8,128]{1,0:T(8,128)S(1)} %get-tuple-element.55.refs_5_.factor, f32[8,128]{1,0:T(8,128)S(1)} %collective-permute-done.8.z_prev), custom_call_target="tpu_custom_call" | custom-call | tf_op jit(solution)/shard_map/finish_even/pallas_call | solution.py:537
  22.0 0.0 collective-permute-done.9.z_prev
  (5 shorter events, 0.0 us)
Async XLA Ops:
  0.1 8.5 %collective-permute-start = (f32[8,128]{1,0:T(8,128)S(1)}, f32[8,128]{1,0:T(8,128)S(1)}, u32[]{:S(2)}, u32[]{:S(2)}) collective-permute-start(f32[8,128]{1,0:T(8,128)S(1)} %get-tuple-element.34.tail_up.refs_5_), channel_id=1, source_target_pairs={{0,1},{1,8},{2,3},{3,2},{4,5},{5,4},{6,7},{7,6},{8,9},{9,16},{10,1... | collective-permute-start | bytes 12296 | tf_op jit(solution)/shard_map/ppermute | solution.py:390
  4.5 4.1 %collective-permute-start.1 = (f32[8,128]{1,0:T(8,128)S(1)}, f32[8,128]{1,0:T(8,128)S(1)}, u32[]{:S(2)}, u32[]{:S(2)}) collective-permute-start(f32[8,128]{1,0:T(8,128)S(1)} %get-tuple-element.40.refs_5_.refs_11_), channel_id=1, source_target_pairs={{0,1},{1,2},{2,3},{3,4},{4,5},{5,6},{6,7},{7,8},{8,0},{9,10},{10,1... | collective-permute-start | bytes 12296 | tf_op jit(solution)/shard_map/ppermute | solution.py:390
  4.6 4.0 %collective-permute-start.2 = (f32[16,128]{1,0:T(8,128)S(1)}, f32[16,128]{1,0:T(8,128)S(1)}, u32[]{:S(2)}, u32[]{:S(2)}) collective-permute-start(f32[16,128]{1,0:T(8,128)S(1)} %get-tuple-element.41), channel_id=1, source_target_pairs={{0,1},{1,0},{2,3},{3,2},{4,5},{5,4},{6,7},{7,6},{8,9},{9,8},{10,11... | collective-permute-start | bytes 24584 | tf_op jit(solution)/shard_map/ppermute | solution.py:442
  4.7 5.4 %collective-permute-start.3 = (f32[16,128]{1,0:T(8,128)S(1)}, f32[16,128]{1,0:T(8,128)S(1)}, u32[]{:S(2)}, u32[]{:S(2)}) collective-permute-start(f32[16,128]{1,0:T(8,128)S(1)} %get-tuple-element.39.refs_4_.refs_10_), channel_id=1, source_target_pairs={{1,2},{2,1},{3,0},{4,3},{0,4},{6,5},{7,6},{8,7},{9,8},{10,9},{11,1... | collective-permute-start | bytes 24584 | tf_op jit(solution)/shard_map/ppermute | solution.py:390
  9.8 3.1 %collective-permute-start.6 = (f32[8,128]{1,0:T(8,128)S(1)}, f32[8,128]{1,0:T(8,128)S(1)}, u32[]{:S(2)}, u32[]{:S(2)}) collective-permute-start(f32[8,128]{1,0:T(8,128)S(1)} %get-tuple-element.42.refs_4_), channel_id=1, source_target_pairs={{1,2},{2,1},{3,0},{4,3},{0,4},{6,5},{7,6},{8,7},{9,8},{10,9},{11,1... | collective-permute-start | bytes 12296 | tf_op jit(solution)/shard_map/ppermute | solution.py:390
  10.1 2.8 %collective-permute-start.7 = (f32[8,128]{1,0:T(8,128)S(1)}, f32[8,128]{1,0:T(8,128)S(1)}, u32[]{:S(2)}, u32[]{:S(2)}) collective-permute-start(f32[8,128]{1,0:T(8,128)S(1)} %get-tuple-element.43.refs_14_.refs_5_), channel_id=1, source_target_pairs={{0,1},{1,0},{2,3},{3,2},{4,5},{5,4},{6,7},{7,6},{8,9},{9,8},{10,11... | collective-permute-start | bytes 12296 | tf_op jit(solution)/shard_map/ppermute | solution.py:442
  10.1 9.4 %collective-permute-start.4 = (f32[8,128]{1,0:T(8,128)S(1)}, f32[8,128]{1,0:T(8,128)S(1)}, u32[]{:S(2)}, u32[]{:S(2)}) collective-permute-start(f32[8,128]{1,0:T(8,128)S(1)} %get-tuple-element.49.refs_9_), channel_id=1, source_target_pairs={{0,1},{1,2},{2,3},{3,4},{4,0},{5,6},{6,7},{7,8},{8,9},{9,10},{10,1... | collective-permute-start | bytes 12296 | tf_op jit(solution)/shard_map/ppermute | solution.py:390
  12.0 7.5 %collective-permute-start.5 = (f32[8,128]{1,0:T(8,128)S(1)}, f32[8,128]{1,0:T(8,128)S(1)}, u32[]{:S(2)}, u32[]{:S(2)}) collective-permute-start(f32[8,128]{1,0:T(8,128)S(1)} %get-tuple-element.50.refs_8_), channel_id=1, source_target_pairs={{0,1},{1,0},{2,3},{3,2},{4,5},{5,4},{6,7},{7,6},{8,9},{9,8},{10,11... | collective-permute-start | bytes 12296 | tf_op jit(solution)/shard_map/ppermute | solution.py:442
  12.9 8.5 %collective-permute-start.8 = (f32[8,128]{1,0:T(8,128)S(1)}, f32[8,128]{1,0:T(8,128)S(1)}, u32[]{:S(2)}, u32[]{:S(2)}) collective-permute-start(f32[8,128]{1,0:T(8,128)S(1)} %get-tuple-element.53.refs_10_), channel_id=1, source_target_pairs={{0,1},{1,2},{2,3},{3,4},{4,0},{5,6},{6,7},{7,8},{8,9},{9,10},{10,1... | collective-permute-start | bytes 12296 | tf_op jit(solution)/shard_map/ppermute | solution.py:390
  20.1 1.9 %collective-permute-start.9 = (f32[8,128]{1,0:T(8,128)S(1)}, f32[8,128]{1,0:T(8,128)S(1)}, u32[]{:S(2)}, u32[]{:S(2)}) collective-permute-start(f32[8,128]{1,0:T(8,128)S(1)} %get-tuple-element.60), channel_id=1, source_target_pairs={{0,1},{1,0},{2,3},{3,2},{4,5},{5,4},{6,7},{7,6},{8,9},{9,8},{10,11... | collective-permute-start | bytes 12296 | tf_op jit(solution)/shard_map/ppermute | solution.py:442

commit v6 on v5

--- a/solution.py
+++ b/solution.py
@@ -14,7 +14,6 @@
 GROUP = 8
 ODD, EVEN = 1, 0
 cost = pl.CostEstimate(flops=10**10, bytes_accessed=10**8, transcendentals=0)
-quick = pl.CostEstimate(flops=0, bytes_accessed=0, transcendentals=0)
 VMEM = pl.BlockSpec(memory_space=pltpu.VMEM)
 ANY = pl.BlockSpec(memory_space=pl.ANY)
 params = pltpu.CompilerParams(vmem_limit_bytes=32 * 1024 * 1024)
@@ -206,6 +205,15 @@
         swapped[...] = tail_own[...]
 
 
+def join_tail(here, couples, weighted, order, joint, total, slots, sem):
+    @pl.when(is_tail())
+    def _():
+        copy = pltpu.make_async_copy(couples, slots, sem)
+        copy.start()
+        copy.wait()
+        join(here, slots, weighted, joint, total)
+
+
 def keep_head(block, out):
     out[...] = jnp.where(is_head(), block[...], 0.0)
 
@@ -300,11 +308,16 @@
 
 
 def first_odd(here, *refs):
-    tail, others, (from_prev, from_next), outs = refs[:6], refs[6:12], refs[12:14], refs[-3:]
+    tail, others, (from_prev, from_next, joint), outs = refs[:6], refs[6:12], refs[12:15], refs[-3:]
+    y_own, y_up, state = outs
 
     @pl.when(is_tail())
     def _():
-        first_sweep_at(here, tail, from_prev, from_next, *outs)
+        now = starts(here, *tail[4:], from_prev, from_next)
+        y_up[...] = across(here, joint, now[2], now[5])
+        y_own[...] = jnp.zeros_like(y_own)
+        for i in range(6):
+            state[i] = now[i]
 
     @pl.when((position() % 2 == ODD) & jnp.logical_not(is_tail()))
     def _():
@@ -312,19 +325,40 @@
 
     @pl.when(position() % 2 == EVEN)
     def _():
-        outs[0][...] = outs[1][...] = jnp.zeros_like(outs[1])
-
-
-def second_odd(*refs):
-    tail, others, values, outs = refs[:4], refs[4:8], [refs[i] for i in (8, 9, 10, 12, 11)], refs[-3:]
+        y_own[...] = y_up[...] = jnp.zeros_like(y_up)
+
+
+def first_late(*refs):
+    matrix, (y_own, state, _, out) = refs[:4], refs[4:]
 
     @pl.when(is_tail())
     def _():
-        second_sweep_at(tail, values, *outs)
+        out[...] = multiply(*matrix, state[2], state[5])[0]
+
+    @pl.when(jnp.logical_not(is_tail()))
+    def _():
+        out[...] = y_own[...]
+
+
+def second_urgent(here, values, joint, z_up, rest, factor, values_own, values_next):
+    p, p_next, scale, target = second_values(*values)
+    z_up[...] = across(here, joint, p, p_next)
+    rest[...] = p + scale * target
+    factor[...] = scale
+    values_own[...] = p
+    values_next[...] = p_next
+
+
+def second_odd(here, *refs):
+    others, values, joint, outs = refs[:4], [refs[i] for i in (4, 5, 6, 8, 7)], refs[9], refs[-5:]
+
+    @pl.when(is_tail())
+    def _():
+        second_urgent(here, values, joint, *outs)
 
     @pl.when((position() % 2 == ODD) & jnp.logical_not(is_tail()))
     def _():
-        second_sweep_at(others, values, *outs)
+        second_sweep_at(others, values, *outs[:3])
 
     @pl.when(position() % 2 == EVEN)
     def _():
@@ -333,35 +367,29 @@
 
 def second_even(here, *refs):
     matrix, values, joint, outs = refs[:4], refs[4:9], refs[9], refs[-5:]
-    z_up, rest, factor, values_own, values_next = outs
 
     @pl.when(is_head())
     def _():
-        p, p_next, scale, target = second_values(*values)
-        z_up[...] = across(here, joint, p, p_next)
-        rest[...] = p + scale * target
-        factor[...] = scale
-        values_own[...] = p
-        values_next[...] = p_next
+        second_urgent(here, values, joint, *outs)
 
     @pl.when((position() % 2 == EVEN) & jnp.logical_not(is_head()))
     def _():
-        second_sweep_at(matrix, values, z_up, rest, factor)
+        second_sweep_at(matrix, values, *outs[:3])
 
     @pl.when(position() % 2 == ODD)
     def _():
-        z_up[...] = jnp.zeros_like(z_up)
-
-
-def second_late(*refs):
+        outs[0][...] = jnp.zeros_like(outs[0])
+
+
+def second_late(role, *refs):
     matrix, (rest, factor, values_own, values_next, out) = refs[:4], refs[4:]
 
-    @pl.when(is_head())
+    @pl.when(role())
     def _():
         z_own = multiply(*matrix, values_own[...], values_next[...])[0]
         out[...] = rest[...] - factor[...] * z_own
 
-    @pl.when(jnp.logical_not(is_head()))
+    @pl.when(jnp.logical_not(role()))
     def _():
         out[...] = rest[...]
 
@@ -465,7 +493,7 @@
         pltpu.SemaphoreType.DMA((CHUNKS + 3,)),
     ]
 
-    def call(kernel, outs, name, *operands, cost=cost):
+    def call(kernel, outs, name, *operands):
         return pl.pallas_call(
             kernel,
             out_shape=outs,
@@ -511,22 +539,42 @@
         *others, own, up, from_prev_e, swapped,
     )
     y_next_o, y_prev_o = backward(sweep_e[0]), swap(sweep_e[1])
-    sweep_o = call(
+    joint_t = in_vmem(
+        pl.pallas_call(
+            functools.partial(join_tail, here),
+            out_shape=joined,
+            in_specs=[ANY, VMEM, VMEM],
+            out_specs=VMEM,
+            scratch_shapes=more,
+            compiler_params=params,
+            cost_estimate=cost,
+            name="join_tail",
+        )(args[1], tail[0], sweep_e[0])
+    )
+    y_own_o, y_up_o, state_o = call(
         functools.partial(first_odd, here), first, "first_odd",
-        *tail, own_t, up_t, *others, own, up, swapped, from_next_o, sweep_e[1],
-    )
+        *tail, own_t, up_t, *others, own, up, swapped, from_next_o, joint_t, sweep_e[1],
+    )
+    y_own_o = call(first_late, small, "first_late", *tail, y_own_o, state_o, state_o)
+    sweep_o = y_own_o, y_up_o, state_o
     y_prev_e, y_next_e = forward(sweep_o[1]), swap(sweep_o[0])
-    z_up_o, rest_o, factor_o = call(
-        second_odd, (small,) * 3, "second_odd", *tail, *others, *sweep_o, y_next_o, y_prev_o
+    z_up_o, rest_o, factor_o, *values_o = call(
+        functools.partial(second_odd, here), (small,) * 5, "second_odd",
+        *others, *sweep_o, y_next_o, y_prev_o, joint_t,
     )
     z_prev_e = forward(z_up_o)
     z_up_e, rest_e, factor_e, *values_e = call(
         functools.partial(second_even, here), (small,) * 5, "second_even",
-        *others, *sweep_e, y_prev_e, y_next_e, joint, z_up_o, cost=quick,
+        *others, *sweep_e, y_prev_e, y_next_e, joint, z_up_o,
     )
     z_prev_o = swap(z_up_e)
     rest_e = call(
-        second_late, small, "second_late", *others, rest_e, factor_e, *values_e, cost=quick
+        functools.partial(second_late, is_head), small, "late_even",
+        *others, rest_e, factor_e, *values_e,
+    )
+    rest_o = call(
+        functools.partial(second_late, is_tail), small, "late_odd",
+        *tail, rest_o, factor_o, *values_o,
     )
     last = dict(
         out_shape=jax.ShapeDtypeStruct(rhs.shape, f32),
@@ -535,7 +583,7 @@
         compiler_params=params,
     )
     even = pl.pallas_call(
-        finish_even, in_specs=[VMEM] * 3, cost_estimate=quick, name="finish_even", **last
+        finish_even, in_specs=[VMEM] * 3, name="finish_even", **last
     )(rest_e, factor_e, z_prev_e)
     return pl.pallas_call(
         finish_odd, in_specs=[ANY] + [VMEM] * 3, input_output_aliases={0: 0}, name="finish_odd", **last

time: 22.5 us -> 22.2 us (0.987); the launches traced: 22.2 us -> 22.2 us
  Pallas kernels: 7.92 us -> 8.15 us
    ppermute x6, starting transfers between devices: 6.81 us -> 6.32 us  [move(): return lax.ppermute(block, 'sfc', list(route.items()))]
    ppermute x4, starting transfers between devices: 0.31 us -> 0.57 us  [swap(): lax.ppermute(block, 'sfc', [(i, i ^ 1) for i in range(lax.axis_size('sfc'...]
    pallas_call x7 -> x9, Pallas kernels: 2.86 us -> 3.08 us  [call(): pl.pallas_call(kernel, out_shape=outs, in_specs=[VMEM] * len(operands), o...]
    pallas_call x1 -> x2, Pallas kernels: 0.59 us -> 0.6 us  [the longest x1 0.59 us: shards(): pl.pallas_call(finish_even, in_specs=[VMEM] * 3, name='finish_even', **last)]
  transfers between devices with their start and end apart: 10 -> 10, of which waited for: 3 -> 4; matrix products, arithmetic and copies ran while one was open for 0% -> 0% of each run, Pallas kernels for 35% -> 36%
where the time goes in v6:
time: 22.2 us
  Pallas kernels  8.15 us (37%)
  starting transfers between devices  6.9 us (31%)
  waiting for transfers between devices  6.82 us (31%)
  between operations  0.29 us (1%)
    ppermute x6, waiting for transfers between devices, move(): return lax.ppermute(block, 'sfc', list(route.items()))  6.81 us
    ppermute x6, starting transfers between devices, move(): return lax.ppermute(block, 'sfc', list(route.items()))  6.32 us
    pallas_call x2, Pallas kernels, assembled_by(): pl.pallas_call(kernel, out_shape=outs, in_specs=[ANY] * 4 + [VMEM] * len(...  4.44 us
    pallas_call x9, Pallas kernels, call(): pl.pallas_call(kernel, out_shape=outs, in_specs=[VMEM] * len(operands), o...  3.08 us
    pallas_call x1, Pallas kernels, shards(): pl.pallas_call(finish_even, in_specs=[VMEM] * 3, name='finish_even', **last)  0.59 us
    ppermute x4, starting transfers between devices, swap(): lax.ppermute(block, 'sfc', [(i, i ^ 1) for i in range(lax.axis_size('sfc'...  0.57 us
  transfers between devices with their start and end apart: 10, of which 4 were waited for; matrix products, arithmetic and copies ran while one was open for 0% of the time, Pallas kernels for 36%

profile of v6, /device:TPU:128, one launch (start us, length us, event | category | flops | bytes accessed | tf_op | source)
XLA Modules:
  0.0 22.2 jit_solution(14855079648280600564)
XLA Ops:
  0.0 0.1 assemble_tail.1
  0.1 0.1 collective-permute-start
  0.2 4.4 %assemble_others.1 = (bf16[48,256,128]{2,1,0:T(8,128)(2,1)S(1)}, bf16[48,128,256]{2,1,0:T(8,128)(2,1)S(1)}, f32[2,16,128]{2,1,0:T(8,128)S(1)}, f32[128,128]{1,0:...) custom-call(bf16[48,256,128]{2,1,0:T(8,128)(2,1)} %bitcast.3, ...), custom_call_target="tpu_custom_call" | custom-call | flops 10000000000 | bytes 100000000 | tf_op jit(solution)/shard_map/assemble_others/pallas_call | solution.py:508
  4.5 0.1 collective-permute-start.1
  4.6 0.1 collective-permute-start.2
  4.7 3.6 %collective-permute-start.3 = (f32[16,128]{1,0:T(8,128)S(1)}, f32[16,128]{1,0:T(8,128)S(1)}, u32[]{:S(2)}, u32[]{:S(2)}) collective-permute-start(f32[16,128]{1,0:T(8,128)S(1)} %get-tuple-element.41.refs_4_.refs_10_), channel_id=1, source_target_pairs={{1,2},{2,1},{3,0},{4,3},{0,4},{6,5},{7,6},{8,7},{9,8},{10,9},{11,1... | collective-permute-start | bytes 24584 | tf_op jit(solution)/shard_map/ppermute | solution.py:418
  8.4 0.3 %collective-permute-done.block = f32[8,128]{1,0:T(8,128)S(1)} collective-permute-done((f32[8,128]{1,0:T(8,128)S(1)}, f32[8,128]{1,0:T(8,128)S(1)}, u32[]{:S(2)}, u32[]{:S(2)}) %collective-permute-start) | collective-permute-done | bytes 4128 | tf_op jit(solution)/shard_map/ppermute | solution.py:418
  8.6 0.0 collective-permute-done.1.block
  8.6 0.0 collective-permute-done.2.refs_7_.refs_12_
  8.7 1.2 %first_even.1 = (f32[8,128]{1,0:T(8,128)S(1)}, f32[8,128]{1,0:T(8,128)S(1)}, f32[6,8,128]{2,1,0:T(8,128)S(1)}) custom-call(bf16[48,256,128]{2,1,0:T(8,128)(2,1)S(1)} %get-tuple-element.37.refs_0_.refs_6_, bf16[48,128,256]{2,1,0:T(8,128)(2,1)S(1)} %get-tuple-element.38.refs_1_.refs_7_, f32[2,16,128]{2,1,0:T(8,128)S(1)} %get-tuple-element.39.refs_2_.refs_8_, ...), custom_call_target="tpu_custom_call" | custom-call | flops 10000000000 | bytes 100000000 | tf_op jit(solution)/shard_map/first_even/pallas_call | solution.py:497
  9.8 0.3 %collective-permute-start.6 = (f32[8,128]{1,0:T(8,128)S(1)}, f32[8,128]{1,0:T(8,128)S(1)}, u32[]{:S(2)}, u32[]{:S(2)}) collective-permute-start(f32[8,128]{1,0:T(8,128)S(1)} %get-tuple-element.44.order.refs_4_), channel_id=1, source_target_pairs={{1,2},{2,1},{3,0},{4,3},{0,4},{6,5},{7,6},{8,7},{9,8},{10,9},{11,1... | collective-permute-start | bytes 12296 | tf_op jit(solution)/shard_map/ppermute | solution.py:418
  10.1 0.1 collective-permute-start.7
  10.2 0.0 collective-permute-done.3.refs_13_
  10.2 0.2 first_odd.1
  10.5 1.5 %collective-permute-start.4 = (f32[8,128]{1,0:T(8,128)S(1)}, f32[8,128]{1,0:T(8,128)S(1)}, u32[]{:S(2)}, u32[]{:S(2)}) collective-permute-start(f32[8,128]{1,0:T(8,128)S(1)} %get-tuple-element.51.refs_5_), channel_id=1, source_target_pairs={{0,1},{1,2},{2,3},{3,4},{4,0},{5,6},{6,7},{7,8},{8,9},{9,10},{10,1... | collective-permute-start | bytes 12296 | tf_op jit(solution)/shard_map/ppermute | solution.py:418
  11.9 0.3 %collective-permute-start.5 = (f32[8,128]{1,0:T(8,128)S(1)}, f32[8,128]{1,0:T(8,128)S(1)}, u32[]{:S(2)}, u32[]{:S(2)}) collective-permute-start(f32[8,128]{1,0:T(8,128)S(1)} %first_late.1.refs_4_), channel_id=1, source_target_pairs={{0,1},{1,0},{2,3},{3,2},{4,5},{5,4},{6,7},{7,6},{8,9},{9,8},{10,11... | collective-permute-start | bytes 12296 | tf_op jit(solution)/shard_map/ppermute | solution.py:470
  12.2 0.7 %collective-permute-done.6.refs_7_ = f32[8,128]{1,0:T(8,128)S(1)} collective-permute-done((f32[8,128]{1,0:T(8,128)S(1)}, f32[8,128]{1,0:T(8,128)S(1)}, u32[]{:S(2)}, u32[]{:S(2)}) %collective-permute-start.6) | collective-permute-done | bytes 4128 | tf_op jit(solution)/shard_map/ppermute | solution.py:418
  12.9 0.0 collective-permute-done.7.refs_8_
  12.9 0.8 %collective-permute-start.8 = (f32[8,128]{1,0:T(8,128)S(1)}, f32[8,128]{1,0:T(8,128)S(1)}, u32[]{:S(2)}, u32[]{:S(2)}) collective-permute-start(f32[8,128]{1,0:T(8,128)S(1)} %get-tuple-element.55.refs_10_), channel_id=1, source_target_pairs={{0,1},{1,2},{2,3},{3,4},{4,0},{5,6},{6,7},{7,8},{8,9},{9,10},{10,1... | collective-permute-start | bytes 12296 | tf_op jit(solution)/shard_map/ppermute | solution.py:418
  13.7 5.3 %collective-permute-done.4.refs_7_ = f32[8,128]{1,0:T(8,128)S(1)} collective-permute-done((f32[8,128]{1,0:T(8,128)S(1)}, f32[8,128]{1,0:T(8,128)S(1)}, u32[]{:S(2)}, u32[]{:S(2)}) %collective-permute-start.4) | collective-permute-done | bytes 4128 | tf_op jit(solution)/shard_map/ppermute | solution.py:418
  19.0 0.0 collective-permute-done.5.refs_8_
  19.0 0.5 %second_even.1 = (f32[8,128]{1,0:T(8,128)S(1)}, f32[8,128]{1,0:T(8,128)S(1)}, f32[8,128]{1,0:T(8,128)S(1)}, f32[8,128]{1,0:T(8,128)S(1)}, f32[8,128]{1,0:T(8,128)S(1)}) custom-call(bf16[48,256,128]{2,1,0:T(8,128)(2,1)S(1)} %get-tuple-element.37.refs_0_.refs_6_, bf16[48,128,256]{2,1,0:T(8,128)(2,1)S(1)} %get-tuple-element.38.refs_1_.refs_7_, ...), custom_call_target="tpu_custom_call" | custom-call | flops 10000000000 | bytes 100000000 | tf_op jit(solution)/shard_map/second_even/pallas_call | solution.py:497
  19.5 0.1 collective-permute-start.9
  19.6 1.2 %late_even.1.rest = f32[8,128]{1,0:T(8,128)S(1)} custom-call(bf16[48,256,128]{2,1,0:T(8,128)(2,1)S(1)} %get-tuple-element.37.refs_0_.refs_6_, bf16[48,128,256]{2,1,0:T(8,128)(2,1)S(1)} %get-tuple-element.38.refs_1_.refs_7_, f32[2,16,128]{2,1,0:T(8,128)S(1)} %get-tuple-element.39.refs_2_.refs_8_, f32[128,128]{1,0:T(8,128)S(1)} %get-tuple-element.40.refs_3_.refs_9_, ...), custom_call_target="tpu_custom_call" | custom-call | flops 10000000000 | bytes 100000000 | tf_op jit(solution)/shard_map/late_even/pallas_call | solution.py:497
  20.8 0.6 %collective-permute-done.8.z_prev = f32[8,128]{1,0:T(8,128)S(1)} collective-permute-done((f32[8,128]{1,0:T(8,128)S(1)}, f32[8,128]{1,0:T(8,128)S(1)}, u32[]{:S(2)}, u32[]{:S(2)}) %collective-permute-start.8) | collective-permute-done | bytes 4128 | tf_op jit(solution)/shard_map/ppermute | solution.py:418
  21.4 0.6 %finish_even.1.even = f32[6,128]{1,0:T(8,128)} custom-call(f32[8,128]{1,0:T(8,128)S(1)} %late_even.1.rest, f32[8,128]{1,0:T(8,128)S(1)} %get-tuple-element.57.refs_5_.factor, f32[8,128]{1,0:T(8,128)S(1)} %collective-permute-done.8.z_prev), custom_call_target="tpu_custom_call" | custom-call | tf_op jit(solution)/shard_map/finish_even/pallas_call | solution.py:585
  22.0 0.0 collective-permute-done.9.z_prev
  (7 shorter events, 0.0 us)
Async XLA Ops:
  0.1 8.5 %collective-permute-start = (f32[8,128]{1,0:T(8,128)S(1)}, f32[8,128]{1,0:T(8,128)S(1)}, u32[]{:S(2)}, u32[]{:S(2)}) collective-permute-start(f32[8,128]{1,0:T(8,128)S(1)} %get-tuple-element.36.tail_up.refs_5_), channel_id=1, source_target_pairs={{0,1},{1,8},{2,3},{3,2},{4,5},{5,4},{6,7},{7,6},{8,9},{9,16},{10,1... | collective-permute-start | bytes 12296 | tf_op jit(solution)/shard_map/ppermute | solution.py:418
  4.5 4.1 %collective-permute-start.1 = (f32[8,128]{1,0:T(8,128)S(1)}, f32[8,128]{1,0:T(8,128)S(1)}, u32[]{:S(2)}, u32[]{:S(2)}) collective-permute-start(f32[8,128]{1,0:T(8,128)S(1)} %get-tuple-element.42.refs_5_.refs_11_), channel_id=1, source_target_pairs={{0,1},{1,2},{2,3},{3,4},{4,5},{5,6},{6,7},{7,8},{8,0},{9,10},{10,1... | collective-permute-start | bytes 12296 | tf_op jit(solution)/shard_map/ppermute | solution.py:418
  4.6 4.0 %collective-permute-start.2 = (f32[16,128]{1,0:T(8,128)S(1)}, f32[16,128]{1,0:T(8,128)S(1)}, u32[]{:S(2)}, u32[]{:S(2)}) collective-permute-start(f32[16,128]{1,0:T(8,128)S(1)} %get-tuple-element.43), channel_id=1, source_target_pairs={{0,1},{1,0},{2,3},{3,2},{4,5},{5,4},{6,7},{7,6},{8,9},{9,8},{10,11... | collective-permute-start | bytes 24584 | tf_op jit(solution)/shard_map/ppermute | solution.py:470
  4.7 5.5 %collective-permute-start.3 = (f32[16,128]{1,0:T(8,128)S(1)}, f32[16,128]{1,0:T(8,128)S(1)}, u32[]{:S(2)}, u32[]{:S(2)}) collective-permute-start(f32[16,128]{1,0:T(8,128)S(1)} %get-tuple-element.41.refs_4_.refs_10_), channel_id=1, source_target_pairs={{1,2},{2,1},{3,0},{4,3},{0,4},{6,5},{7,6},{8,7},{9,8},{10,9},{11,1... | collective-permute-start | bytes 24584 | tf_op jit(solution)/shard_map/ppermute | solution.py:418
  9.8 3.1 %collective-permute-start.6 = (f32[8,128]{1,0:T(8,128)S(1)}, f32[8,128]{1,0:T(8,128)S(1)}, u32[]{:S(2)}, u32[]{:S(2)}) collective-permute-start(f32[8,128]{1,0:T(8,128)S(1)} %get-tuple-element.44.order.refs_4_), channel_id=1, source_target_pairs={{1,2},{2,1},{3,0},{4,3},{0,4},{6,5},{7,6},{8,7},{9,8},{10,9},{11,1... | collective-permute-start | bytes 12296 | tf_op jit(solution)/shard_map/ppermute | solution.py:418
  10.1 2.8 %collective-permute-start.7 = (f32[8,128]{1,0:T(8,128)S(1)}, f32[8,128]{1,0:T(8,128)S(1)}, u32[]{:S(2)}, u32[]{:S(2)}) collective-permute-start(f32[8,128]{1,0:T(8,128)S(1)} %get-tuple-element.45.refs_15_.refs_5_), channel_id=1, source_target_pairs={{0,1},{1,0},{2,3},{3,2},{4,5},{5,4},{6,7},{7,6},{8,9},{9,8},{10,11... | collective-permute-start | bytes 12296 | tf_op jit(solution)/shard_map/ppermute | solution.py:470
  10.5 8.5 %collective-permute-start.4 = (f32[8,128]{1,0:T(8,128)S(1)}, f32[8,128]{1,0:T(8,128)S(1)}, u32[]{:S(2)}, u32[]{:S(2)}) collective-permute-start(f32[8,128]{1,0:T(8,128)S(1)} %get-tuple-element.51.refs_5_), channel_id=1, source_target_pairs={{0,1},{1,2},{2,3},{3,4},{4,0},{5,6},{6,7},{7,8},{8,9},{9,10},{10,1... | collective-permute-start | bytes 12296 | tf_op jit(solution)/shard_map/ppermute | solution.py:418
  11.9 7.1 %collective-permute-start.5 = (f32[8,128]{1,0:T(8,128)S(1)}, f32[8,128]{1,0:T(8,128)S(1)}, u32[]{:S(2)}, u32[]{:S(2)}) collective-permute-start(f32[8,128]{1,0:T(8,128)S(1)} %first_late.1.refs_4_), channel_id=1, source_target_pairs={{0,1},{1,0},{2,3},{3,2},{4,5},{5,4},{6,7},{7,6},{8,9},{9,8},{10,11... | collective-permute-start | bytes 12296 | tf_op jit(solution)/shard_map/ppermute | solution.py:470
  12.9 8.5 %collective-permute-start.8 = (f32[8,128]{1,0:T(8,128)S(1)}, f32[8,128]{1,0:T(8,128)S(1)}, u32[]{:S(2)}, u32[]{:S(2)}) collective-permute-start(f32[8,128]{1,0:T(8,128)S(1)} %get-tuple-element.55.refs_10_), channel_id=1, source_target_pairs={{0,1},{1,2},{2,3},{3,4},{4,0},{5,6},{6,7},{7,8},{8,9},{9,10},{10,1... | collective-permute-start | bytes 12296 | tf_op jit(solution)/shard_map/ppermute | solution.py:418
  19.5 2.4 %collective-permute-start.9 = (f32[8,128]{1,0:T(8,128)S(1)}, f32[8,128]{1,0:T(8,128)S(1)}, u32[]{:S(2)}, u32[]{:S(2)}) collective-permute-start(f32[8,128]{1,0:T(8,128)S(1)} %get-tuple-element.64), channel_id=1, source_target_pairs={{0,1},{1,0},{2,3},{3,2},{4,5},{5,4},{6,7},{7,6},{8,9},{9,8},{10,11... | collective-permute-start | bytes 12296 | tf_op jit(solution)/shard_map/ppermute | solution.py:470

commit v7 on v6

--- a/solution.py
+++ b/solution.py
@@ -10,7 +10,7 @@
 relax = 0.5
 f32, bf16 = jnp.float32, jnp.bfloat16
 UP = 8
-CHUNKS = 6
+CHUNKS = 4
 GROUP = 8
 ODD, EVEN = 1, 0
 cost = pl.CostEstimate(flops=10**10, bytes_accessed=10**8, transcendentals=0)
@@ -222,6 +222,14 @@
     out[...] = jnp.where(is_head(), kept[...], block[...])
 
 
+def scatter_at_once(place, per_tile):
+    count, size = per_tile[0].shape
+    wide = jnp.concatenate(parts(jnp.concatenate(per_tile, axis=0)), axis=1).astype(bf16)
+    left = jnp.concatenate([place[k][:, :count] for k in range(2)], axis=1).astype(bf16)
+    sums = jnp.dot(left, wide, preferred_element_type=f32)
+    return sums[:, :size] + sums[:, size:]
+
+
 def multiply(weighted, turned, place, pick, mine, following):
     count = weighted.shape[0]
     high, low = parts(jnp.concatenate([mine, following], axis=0))
@@ -258,7 +266,7 @@
             total = both if total is None else jnp.where(sub2 == j, both, total)
         outer.append(total)
     outer = jnp.concatenate(outer, axis=0)
-    total = scatter(place, [outer[:, :128], outer[:, 128:]])
+    total = scatter_at_once(place, [outer[:, :128], outer[:, 128:]])
     return total[:8], total[8:]
 
 

time: 22.2 us -> 22.2 us (level)
  transfers between devices with their start and end apart: 10 -> 10, of which waited for: 4 -> 4; matrix products, arithmetic and copies ran while one was open for 0% -> 0% of each run, Pallas kernels for 36% -> 37%
where the time goes in v7:
time: 22.2 us; the launch traced here: 22.1 us
  Pallas kernels  8.17 us (37%)
  starting transfers between devices  6.86 us (31%)
  waiting for transfers between devices  6.8 us (31%)
  between operations  0.28 us (1%)
    ppermute x6, waiting for transfers between devices, move(): return lax.ppermute(block, 'sfc', list(route.items()))  6.79 us
    ppermute x6, starting transfers between devices, move(): return lax.ppermute(block, 'sfc', list(route.items()))  6.34 us
    pallas_call x2, Pallas kernels, assembled_by(): pl.pallas_call(kernel, out_shape=outs, in_specs=[ANY] * 4 + [VMEM] * len(...  4.47 us
    pallas_call x9, Pallas kernels, call(): pl.pallas_call(kernel, out_shape=outs, in_specs=[VMEM] * len(operands), o...  3.07 us
    pallas_call x1, Pallas kernels, shards(): pl.pallas_call(finish_even, in_specs=[VMEM] * 3, name='finish_even', **last)  0.59 us
    ppermute x4, starting transfers between devices, swap(): lax.ppermute(block, 'sfc', [(i, i ^ 1) for i in range(lax.axis_size('sfc'...  0.52 us
  transfers between devices with their start and end apart: 10, of which 4 were waited for; matrix products, arithmetic and copies ran while one was open for 0% of the time, Pallas kernels for 37%

profile of v7, /device:TPU:128, one launch (start us, length us, event | category | flops | bytes accessed | tf_op | source)
XLA Modules:
  0.0 22.1 jit_solution(3104830914247783259)
XLA Ops:
  0.0 0.1 assemble_tail.1
  0.1 0.1 collective-permute-start
  0.2 4.4 %assemble_others.1 = (bf16[48,256,128]{2,1,0:T(8,128)(2,1)S(1)}, bf16[48,128,256]{2,1,0:T(8,128)(2,1)S(1)}, f32[2,16,128]{2,1,0:T(8,128)S(1)}, f32[128,128]{1,0:...) custom-call(bf16[48,256,128]{2,1,0:T(8,128)(2,1)} %bitcast.3, ...), custom_call_target="tpu_custom_call" | custom-call | flops 10000000000 | bytes 100000000 | tf_op jit(solution)/shard_map/assemble_others/pallas_call | solution.py:516
  4.6 0.1 collective-permute-start.1
  4.7 0.1 collective-permute-start.2
  4.8 3.6 %collective-permute-start.3 = (f32[16,128]{1,0:T(8,128)S(1)}, f32[16,128]{1,0:T(8,128)S(1)}, u32[]{:S(2)}, u32[]{:S(2)}) collective-permute-start(f32[16,128]{1,0:T(8,128)S(1)} %get-tuple-element.41.refs_4_.refs_10_), channel_id=1, source_target_pairs={{1,2},{2,1},{3,0},{4,3},{0,4},{6,5},{7,6},{8,7},{9,8},{10,9},{11,1... | collective-permute-start | bytes 24584 | tf_op jit(solution)/shard_map/ppermute | solution.py:426
  8.4 0.2 %collective-permute-done.block = f32[8,128]{1,0:T(8,128)S(1)} collective-permute-done((f32[8,128]{1,0:T(8,128)S(1)}, f32[8,128]{1,0:T(8,128)S(1)}, u32[]{:S(2)}, u32[]{:S(2)}) %collective-permute-start) | collective-permute-done | bytes 4128 | tf_op jit(solution)/shard_map/ppermute | solution.py:426
  8.6 0.0 collective-permute-done.1.block
  8.6 0.0 collective-permute-done.2.refs_7_.refs_12_
  8.6 1.2 %first_even.1 = (f32[8,128]{1,0:T(8,128)S(1)}, f32[8,128]{1,0:T(8,128)S(1)}, f32[6,8,128]{2,1,0:T(8,128)S(1)}) custom-call(bf16[48,256,128]{2,1,0:T(8,128)(2,1)S(1)} %get-tuple-element.37.refs_0_.refs_6_, bf16[48,128,256]{2,1,0:T(8,128)(2,1)S(1)} %get-tuple-element.38.refs_1_.refs_7_, f32[2,16,128]{2,1,0:T(8,128)S(1)} %get-tuple-element.39.refs_2_.refs_8_, ...), custom_call_target="tpu_custom_call" | custom-call | flops 10000000000 | bytes 100000000 | tf_op jit(solution)/shard_map/first_even/pallas_call | solution.py:505
  9.8 0.3 %collective-permute-start.6 = (f32[8,128]{1,0:T(8,128)S(1)}, f32[8,128]{1,0:T(8,128)S(1)}, u32[]{:S(2)}, u32[]{:S(2)}) collective-permute-start(f32[8,128]{1,0:T(8,128)S(1)} %get-tuple-element.44.order.refs_4_), channel_id=1, source_target_pairs={{1,2},{2,1},{3,0},{4,3},{0,4},{6,5},{7,6},{8,7},{9,8},{10,9},{11,1... | collective-permute-start | bytes 12296 | tf_op jit(solution)/shard_map/ppermute | solution.py:426
  10.2 0.1 collective-permute-start.7
  10.3 0.0 collective-permute-done.3.refs_13_
  10.3 0.2 first_odd.1
  10.5 1.4 %collective-permute-start.4 = (f32[8,128]{1,0:T(8,128)S(1)}, f32[8,128]{1,0:T(8,128)S(1)}, u32[]{:S(2)}, u32[]{:S(2)}) collective-permute-start(f32[8,128]{1,0:T(8,128)S(1)} %get-tuple-element.51.refs_5_), channel_id=1, source_target_pairs={{0,1},{1,2},{2,3},{3,4},{4,0},{5,6},{6,7},{7,8},{8,9},{9,10},{10,1... | collective-permute-start | bytes 12296 | tf_op jit(solution)/shard_map/ppermute | solution.py:426
  12.0 0.2 %collective-permute-start.5 = (f32[8,128]{1,0:T(8,128)S(1)}, f32[8,128]{1,0:T(8,128)S(1)}, u32[]{:S(2)}, u32[]{:S(2)}) collective-permute-start(f32[8,128]{1,0:T(8,128)S(1)} %first_late.1.refs_4_), channel_id=1, source_target_pairs={{0,1},{1,0},{2,3},{3,2},{4,5},{5,4},{6,7},{7,6},{8,9},{9,8},{10,11... | collective-permute-start | bytes 12296 | tf_op jit(solution)/shard_map/ppermute | solution.py:478
  12.2 0.7 %collective-permute-done.6.refs_7_ = f32[8,128]{1,0:T(8,128)S(1)} collective-permute-done((f32[8,128]{1,0:T(8,128)S(1)}, f32[8,128]{1,0:T(8,128)S(1)}, u32[]{:S(2)}, u32[]{:S(2)}) %collective-permute-start.6) | collective-permute-done | bytes 4128 | tf_op jit(solution)/shard_map/ppermute | solution.py:426
  12.9 0.0 collective-permute-done.7.refs_8_
  12.9 0.8 %collective-permute-start.8 = (f32[8,128]{1,0:T(8,128)S(1)}, f32[8,128]{1,0:T(8,128)S(1)}, u32[]{:S(2)}, u32[]{:S(2)}) collective-permute-start(f32[8,128]{1,0:T(8,128)S(1)} %get-tuple-element.55.refs_10_), channel_id=1, source_target_pairs={{0,1},{1,2},{2,3},{3,4},{4,0},{5,6},{6,7},{7,8},{8,9},{9,10},{10,1... | collective-permute-start | bytes 12296 | tf_op jit(solution)/shard_map/ppermute | solution.py:426
  13.6 5.4 %collective-permute-done.4.refs_7_ = f32[8,128]{1,0:T(8,128)S(1)} collective-permute-done((f32[8,128]{1,0:T(8,128)S(1)}, f32[8,128]{1,0:T(8,128)S(1)}, u32[]{:S(2)}, u32[]{:S(2)}) %collective-permute-start.4) | collective-permute-done | bytes 4128 | tf_op jit(solution)/shard_map/ppermute | solution.py:426
  19.1 0.0 collective-permute-done.5.refs_8_
  19.1 0.5 %second_even.1 = (f32[8,128]{1,0:T(8,128)S(1)}, f32[8,128]{1,0:T(8,128)S(1)}, f32[8,128]{1,0:T(8,128)S(1)}, f32[8,128]{1,0:T(8,128)S(1)}, f32[8,128]{1,0:T(8,128)S(1)}) custom-call(bf16[48,256,128]{2,1,0:T(8,128)(2,1)S(1)} %get-tuple-element.37.refs_0_.refs_6_, bf16[48,128,256]{2,1,0:T(8,128)(2,1)S(1)} %get-tuple-element.38.refs_1_.refs_7_, ...), custom_call_target="tpu_custom_call" | custom-call | flops 10000000000 | bytes 100000000 | tf_op jit(solution)/shard_map/second_even/pallas_call | solution.py:505
  19.6 0.1 collective-permute-start.9
  19.7 1.2 %late_even.1.rest = f32[8,128]{1,0:T(8,128)S(1)} custom-call(bf16[48,256,128]{2,1,0:T(8,128)(2,1)S(1)} %get-tuple-element.37.refs_0_.refs_6_, bf16[48,128,256]{2,1,0:T(8,128)(2,1)S(1)} %get-tuple-element.38.refs_1_.refs_7_, f32[2,16,128]{2,1,0:T(8,128)S(1)} %get-tuple-element.39.refs_2_.refs_8_, f32[128,128]{1,0:T(8,128)S(1)} %get-tuple-element.40.refs_3_.refs_9_, ...), custom_call_target="tpu_custom_call" | custom-call | flops 10000000000 | bytes 100000000 | tf_op jit(solution)/shard_map/late_even/pallas_call | solution.py:505
  20.8 0.5 %collective-permute-done.8.z_prev = f32[8,128]{1,0:T(8,128)S(1)} collective-permute-done((f32[8,128]{1,0:T(8,128)S(1)}, f32[8,128]{1,0:T(8,128)S(1)}, u32[]{:S(2)}, u32[]{:S(2)}) %collective-permute-start.8) | collective-permute-done | bytes 4128 | tf_op jit(solution)/shard_map/ppermute | solution.py:426
  21.3 0.6 %finish_even.1.even = f32[6,128]{1,0:T(8,128)} custom-call(f32[8,128]{1,0:T(8,128)S(1)} %late_even.1.rest, f32[8,128]{1,0:T(8,128)S(1)} %get-tuple-element.57.refs_5_.factor, f32[8,128]{1,0:T(8,128)S(1)} %collective-permute-done.8.z_prev), custom_call_target="tpu_custom_call" | custom-call | tf_op jit(solution)/shard_map/finish_even/pallas_call | solution.py:593
  21.9 0.0 collective-permute-done.9.z_prev
  (7 shorter events, 0.0 us)
Async XLA Ops:
  0.1 8.5 %collective-permute-start = (f32[8,128]{1,0:T(8,128)S(1)}, f32[8,128]{1,0:T(8,128)S(1)}, u32[]{:S(2)}, u32[]{:S(2)}) collective-permute-start(f32[8,128]{1,0:T(8,128)S(1)} %get-tuple-element.36.tail_up.refs_5_), channel_id=1, source_target_pairs={{0,1},{1,8},{2,3},{3,2},{4,5},{5,4},{6,7},{7,6},{8,9},{9,16},{10,1... | collective-permute-start | bytes 12296 | tf_op jit(solution)/shard_map/ppermute | solution.py:426
  4.6 4.0 %collective-permute-start.1 = (f32[8,128]{1,0:T(8,128)S(1)}, f32[8,128]{1,0:T(8,128)S(1)}, u32[]{:S(2)}, u32[]{:S(2)}) collective-permute-start(f32[8,128]{1,0:T(8,128)S(1)} %get-tuple-element.42.refs_5_.refs_11_), channel_id=1, source_target_pairs={{0,1},{1,2},{2,3},{3,4},{4,5},{5,6},{6,7},{7,8},{8,0},{9,10},{10,1... | collective-permute-start | bytes 12296 | tf_op jit(solution)/shard_map/ppermute | solution.py:426
  4.7 4.0 %collective-permute-start.2 = (f32[16,128]{1,0:T(8,128)S(1)}, f32[16,128]{1,0:T(8,128)S(1)}, u32[]{:S(2)}, u32[]{:S(2)}) collective-permute-start(f32[16,128]{1,0:T(8,128)S(1)} %get-tuple-element.43), channel_id=1, source_target_pairs={{0,1},{1,0},{2,3},{3,2},{4,5},{5,4},{6,7},{7,6},{8,9},{9,8},{10,11... | collective-permute-start | bytes 24584 | tf_op jit(solution)/shard_map/ppermute | solution.py:478
  4.8 5.5 %collective-permute-start.3 = (f32[16,128]{1,0:T(8,128)S(1)}, f32[16,128]{1,0:T(8,128)S(1)}, u32[]{:S(2)}, u32[]{:S(2)}) collective-permute-start(f32[16,128]{1,0:T(8,128)S(1)} %get-tuple-element.41.refs_4_.refs_10_), channel_id=1, source_target_pairs={{1,2},{2,1},{3,0},{4,3},{0,4},{6,5},{7,6},{8,7},{9,8},{10,9},{11,1... | collective-permute-start | bytes 24584 | tf_op jit(solution)/shard_map/ppermute | solution.py:426
  9.8 3.0 %collective-permute-start.6 = (f32[8,128]{1,0:T(8,128)S(1)}, f32[8,128]{1,0:T(8,128)S(1)}, u32[]{:S(2)}, u32[]{:S(2)}) collective-permute-start(f32[8,128]{1,0:T(8,128)S(1)} %get-tuple-element.44.order.refs_4_), channel_id=1, source_target_pairs={{1,2},{2,1},{3,0},{4,3},{0,4},{6,5},{7,6},{8,7},{9,8},{10,9},{11,1... | collective-permute-start | bytes 12296 | tf_op jit(solution)/shard_map/ppermute | solution.py:426
  10.2 2.7 %collective-permute-start.7 = (f32[8,128]{1,0:T(8,128)S(1)}, f32[8,128]{1,0:T(8,128)S(1)}, u32[]{:S(2)}, u32[]{:S(2)}) collective-permute-start(f32[8,128]{1,0:T(8,128)S(1)} %get-tuple-element.45.refs_15_.refs_5_), channel_id=1, source_target_pairs={{0,1},{1,0},{2,3},{3,2},{4,5},{5,4},{6,7},{7,6},{8,9},{9,8},{10,11... | collective-permute-start | bytes 12296 | tf_op jit(solution)/shard_map/ppermute | solution.py:478
  10.5 8.5 %collective-permute-start.4 = (f32[8,128]{1,0:T(8,128)S(1)}, f32[8,128]{1,0:T(8,128)S(1)}, u32[]{:S(2)}, u32[]{:S(2)}) collective-permute-start(f32[8,128]{1,0:T(8,128)S(1)} %get-tuple-element.51.refs_5_), channel_id=1, source_target_pairs={{0,1},{1,2},{2,3},{3,4},{4,0},{5,6},{6,7},{7,8},{8,9},{9,10},{10,1... | collective-permute-start | bytes 12296 | tf_op jit(solution)/shard_map/ppermute | solution.py:426
  12.0 7.1 %collective-permute-start.5 = (f32[8,128]{1,0:T(8,128)S(1)}, f32[8,128]{1,0:T(8,128)S(1)}, u32[]{:S(2)}, u32[]{:S(2)}) collective-permute-start(f32[8,128]{1,0:T(8,128)S(1)} %first_late.1.refs_4_), channel_id=1, source_target_pairs={{0,1},{1,0},{2,3},{3,2},{4,5},{5,4},{6,7},{7,6},{8,9},{9,8},{10,11... | collective-permute-start | bytes 12296 | tf_op jit(solution)/shard_map/ppermute | solution.py:478
  12.9 8.5 %collective-permute-start.8 = (f32[8,128]{1,0:T(8,128)S(1)}, f32[8,128]{1,0:T(8,128)S(1)}, u32[]{:S(2)}, u32[]{:S(2)}) collective-permute-start(f32[8,128]{1,0:T(8,128)S(1)} %get-tuple-element.55.refs_10_), channel_id=1, source_target_pairs={{0,1},{1,2},{2,3},{3,4},{4,0},{5,6},{6,7},{7,8},{8,9},{9,10},{10,1... | collective-permute-start | bytes 12296 | tf_op jit(solution)/shard_map/ppermute | solution.py:426
  19.6 2.3 %collective-permute-start.9 = (f32[8,128]{1,0:T(8,128)S(1)}, f32[8,128]{1,0:T(8,128)S(1)}, u32[]{:S(2)}, u32[]{:S(2)}) collective-permute-start(f32[8,128]{1,0:T(8,128)S(1)} %get-tuple-element.64), channel_id=1, source_target_pairs={{0,1},{1,0},{2,3},{3,2},{4,5},{5,4},{6,7},{7,6},{8,9},{9,8},{10,11... | collective-permute-start | bytes 12296 | tf_op jit(solution)/shard_map/ppermute | solution.py:478
